TPU v7x, 32 devices: a whole 2x2x4 slice. The times are simulated.
32 devices in a mesh: members: 2 (over y), lat: 4 (over z), lon: 2 (over x), lev: 2 (over core).
Axes of the slice: x: 2, y: 2, z: 4, core: 2. Of those that a mesh axis runs over, the one named last changes fastest.
Arguments:
- wind_east: float32 [8, 360, 2880], P(('members', 'lev'), 'lat', 'lon'), parts along dimension 0, may hold values from -6 to 6
- wind_north: float32 [8, 360, 2880], P(('members', 'lev'), 'lat', 'lon'), parts along dimension 0, may hold values from -6 to 6
- thickness: float32 [8, 360, 2880], P(('members', 'lev'), 'lat', 'lon'), parts along dimension 0, may hold values from -6 to 6
- geopot: float32 [8, 360, 2880], P(('members', 'lev'), 'lat', 'lon'), parts along dimension 0, may hold values from -6 to 6
- surface_geopot: float32 [360, 2880], P('lat', 'lon'), may hold values from -6 to 6
- mean_depth: float32 [4], P('lev'), may hold values from 0.5 to 2
- kept_modes: int32 [180], replicated, may hold values from 1 to 360
- slot_table: int32 [180], replicated, may hold values from 0 to 179, as said below
Outputs:
- east_final: float32 [8, 360, 2880], P(('members', 'lev'), 'lat', 'lon'), parts along dimension 0
- north_final: float32 [8, 360, 2880], P(('members', 'lev'), 'lat', 'lon'), parts along dimension 0
- thick_new: float32 [8, 360, 2880], P(('members', 'lev'), 'lat', 'lon'), parts along dimension 0
- geo_new: float32 [8, 360, 2880], P(('members', 'lev'), 'lat', 'lon'), parts along dimension 0
- spectra: float32 [2, 8, 180, 720], P(None, ('members', 'lev'), 'lat', 'lon'), parts along dimension 1
There are 2 independent parts, one for each index of `members`. A program takes and returns all parts, laid end to end along the dimension named above; an argument that names none is the same for every part. Nothing has to cross between parts.
Inputs may be any that keep to these rules, and one draw needn't show every extreme that they name: `slot_table`: every slot 0 to 179 is named once; slot s belongs to latitude device s // 45. Of the 90 polar rows held by latitude device d, 45 name slots of device d and 45 name slots of the device half the lat axis away, (d + 4 / 2) mod 4.
All inputs are finite; a program needn't handle non-finite values.
Results may differ from a plain program's by a relative error of at most 0.00019.
Values sent between devices are 32-bit elements; how exact they have to be, the bound alone decides.
No kernel may reach another device: no remote copies, remote signals or barrier semaphores. Data moves between devices by JAX's collectives and lax.ppermute only.
A program may use at most 64 MiB of HBM per device.

v0:
```python
import functools
import math

import jax
import jax.numpy as jnp
import numpy as np
from jax import lax
from jax.experimental import pallas as pl
from jax.experimental.pallas import tpu as pltpu
from jax.sharding import PartitionSpec as P

KMAX = 360
HALF = 384
WIDE = 2 * HALF
SPARE = HALF - 128
BLOCK = 256

STEP_FACTOR = 0.15
CORIOLIS = 0.2
GRAVITY = 0.25

MIB = 1024 * 1024

EAST_COEF, SINE, COSINE, NORTH_COEF, LEVEL, POLAR, NUMBER, OWN = range(8)


def round_up(value, step):
    return -(-value // step) * step


class Sizes:
    def __init__(self, shape, counts):
        self.lev, self.lat, self.lon = shape
        self.n_lat, self.n_lon, self.n_lev = counts["lat"], counts["lon"], counts["lev"]
        self.nlat, self.nlon = self.lat * self.n_lat, self.lon * self.n_lon
        self.polar = self.nlat // 4
        self.help = self.lat // 2
        self.half_axis = self.n_lat // 2
        self.own = self.lat * self.lev
        self.rows = self.own + 2 * self.lev
        assert self.rows % 8 == 0
        self.mm_rows = round_up(self.rows, 16)
        self.ext = round_up(self.lon + 4, BLOCK)
        self.blocks = self.ext // BLOCK
        self.spec_width = 2 * KMAX // self.n_lon
        self.spec_rows = round_up(self.help * self.lev, 8)


def high_low(x):
    x = x.astype(np.float32)
    high = x.astype(jnp.bfloat16)
    return high, (x - high.astype(np.float32)).astype(jnp.bfloat16)


def basis_tables(z):
    k = np.arange(KMAX)
    angle = (np.arange(BLOCK)[:, None] * k[None, :] % z.nlon) * (2.0 * np.pi / z.nlon)
    full = np.zeros((BLOCK, WIDE))
    full[:, :KMAX] = np.cos(angle)
    full[:, HALF : HALF + KMAX] = np.sin(angle)
    high, low = high_low(full)
    forward = np.concatenate([high, high, low], axis=0)
    inverse = np.concatenate([high.T, high.T, low.T], axis=0)
    return forward, inverse


def phase_table(z):
    k = np.arange(KMAX)
    table = np.zeros((z.n_lon, round_up(2 * z.blocks + 2, 8), HALF), np.float32)
    for place in range(z.n_lon):
        for n, column in enumerate([*range(0, z.ext, BLOCK), -1]):
            angle = ((place * z.lon + column) * k % z.nlon) * (2.0 * np.pi / z.nlon)
            table[place, 2 * n, :KMAX] = np.cos(angle)
            table[place, 2 * n + 1, :KMAX] = np.sin(angle)
    return table


def row_table(z):
    lam_step = np.float32(2.0 * math.pi / z.nlon)
    phi_step = np.float32(math.pi / z.nlat)
    latitude = np.float32(-0.5 * math.pi) + (
        np.arange(z.nlat, dtype=np.float32) + np.float32(0.5)
    ) * phi_step
    cosine = np.cos(latitude.astype(np.float64)).astype(np.float32)
    sine = np.sin(latitude.astype(np.float64)).astype(np.float32)
    north_coef = np.float32(STEP_FACTOR) * lam_step / phi_step
    table = np.zeros((z.n_lat, z.rows, 8), np.float32)
    for place in range(z.n_lat):
        for flat in range(z.rows):
            inner, level = flat // z.lev, flat % z.lev
            inner = -1 if inner == z.lat + 1 else inner
            row = place * z.lat + inner
            one = table[place, flat]
            one[LEVEL], one[NUMBER] = level, -1
            one[OWN] = 0 <= inner < z.lat
            if 0 <= row < z.nlat:
                one[EAST_COEF] = np.float32(STEP_FACTOR) / cosine[row]
                one[SINE], one[COSINE] = sine[row], cosine[row]
                one[NORTH_COEF] = north_coef / cosine[row]
                if row < z.polar:
                    one[POLAR], one[NUMBER] = 1, row
                elif row >= z.nlat - z.polar:
                    one[POLAR], one[NUMBER] = 1, row - (z.nlat - 2 * z.polar)
    return table


def store_split(lhs_ref, first_row, x):
    rows, width = x.shape
    high = x.astype(jnp.bfloat16)
    low = (x - high.astype(jnp.float32)).astype(jnp.bfloat16)
    at = slice(first_row, first_row + rows)
    lhs_ref[at, :width] = high
    lhs_ref[at, width : 2 * width] = low
    lhs_ref[at, 2 * width :] = high


def pad_rows(x, rows):
    return jnp.concatenate([x, jnp.zeros((rows - x.shape[0], x.shape[1]), x.dtype)], axis=0)


def phase_of(phase_ref, n):
    lon_index = lax.axis_index("lon")
    return phase_ref[lon_index, 2 * n : 2 * n + 1], phase_ref[lon_index, 2 * n + 1 : 2 * n + 2]


def forward_sums(z, x, basis_ref, phase_ref, lhs_ref, payload_ref):
    for block in range(z.blocks):
        part = pad_rows(x[:, block * BLOCK : (block + 1) * BLOCK], z.mm_rows)
        store_split(lhs_ref, block * z.mm_rows, part)
    sums = jnp.dot(lhs_ref[...], basis_ref[...], preferred_element_type=jnp.float32)
    real = imag = None
    for block in range(z.blocks):
        cos, sin = phase_of(phase_ref, block)
        part = sums[block * z.mm_rows : block * z.mm_rows + z.rows]
        a, b = part[:, :HALF], part[:, HALF:]
        more_real, more_imag = a * cos - b * sin, a * sin + b * cos
        real = more_real if real is None else real + more_real
        imag = more_imag if imag is None else imag + more_imag
    payload_ref[:, :HALF] = real
    payload_ref[:, HALF:] = imag


def inverse_blocks(z, coef, basis_ref, phase_ref, lhs_ref):
    a, b = coef[:, :HALF], coef[:, HALF:]
    for block in range(z.blocks):
        cos, sin = phase_of(phase_ref, block)
        turned = jnp.concatenate([a * cos + b * sin, b * cos - a * sin], axis=1)
        store_split(lhs_ref, block * z.mm_rows, pad_rows(turned, z.mm_rows))
    rows = jnp.dot(lhs_ref[...], basis_ref[...], preferred_element_type=jnp.float32)
    cos, sin = phase_of(phase_ref, z.blocks)
    before = jnp.sum(a * cos + b * sin, axis=1, keepdims=True)
    return [rows[n * z.mm_rows : n * z.mm_rows + z.rows] for n in range(z.blocks)], before


def roll(x, shift, axis):
    return pltpu.roll(x, shift % x.shape[axis], axis)


def east_diff(x):
    return roll(x, -1, 1) - roll(x, 1, 1)


def flat_rows(z, ref):
    return ref[...].reshape(z.own, ref.shape[2])


def widen(z, x):
    return jnp.concatenate([x, jnp.zeros((x.shape[0], z.ext - x.shape[1]), x.dtype)], axis=1)


def put_lane(x, at, column):
    lane = lax.broadcasted_iota(jnp.int32, x.shape, 1)
    return jnp.where(lane == at, column, x)


def column_of(row_ref, which):
    return row_ref[lax.axis_index("lat"), :, which : which + 1]


def look_up(number, table_ref):
    table = table_ref[...].astype(jnp.float32)
    lane = lax.broadcasted_iota(jnp.int32, (number.shape[0], table.shape[1]), 1)
    return jnp.sum(jnp.where(lane == number, table, 0.0), axis=1, keepdims=True)


def add_shares(refs):
    total = refs[0][...]
    for ref in refs[1:]:
        total = total + ref[...]
    return total


def coefficients(z, sums, number, kept_ref):
    lane = lax.broadcasted_iota(jnp.int32, (1, WIDE), 1)
    k = jnp.where(lane < HALF, lane, lane - HALF)
    weight = jnp.where(k == 0, 1.0 / z.nlon, 2.0 / z.nlon).astype(jnp.float32)
    keep = (k.astype(jnp.float32) < look_up(number, kept_ref)) & (k < KMAX)
    return jnp.where(keep, sums * weight, 0.0)


def store_spectra(z, coef, number, row_ref, slot_ref, keep_ref, send_ref):
    lat_index, lon_index = lax.axis_index("lat"), lax.axis_index("lon")
    slot = look_up(number, slot_ref).astype(jnp.int32)
    level = column_of(row_ref, LEVEL).astype(jnp.int32)
    usable = (column_of(row_ref, OWN) > 0.0) & (number >= 0)
    mine = slot - lat_index * z.help
    theirs = slot - lax.rem(lat_index + z.half_axis, z.n_lat) * z.help
    place = jnp.full_like(slot, -1)
    place = jnp.where(usable & (mine >= 0) & (mine < z.help), mine * z.lev + level, place)
    place = jnp.where(
        usable & (theirs >= 0) & (theirs < z.help), z.spec_rows + theirs * z.lev + level, place
    )
    lane = lax.broadcasted_iota(jnp.int32, (z.rows, round_up(2 * z.spec_rows, 128)), 1)
    chosen = (lane == place).astype(jnp.float32)
    part = jnp.zeros((z.rows, z.spec_width), jnp.float32)
    for one in range(z.n_lon):
        first = one * z.spec_width
        first = first if first < KMAX else first - KMAX + HALF
        part = jnp.where(lon_index == one, coef[:, first : first + z.spec_width], part)
    ordered = lax.dot_general(
        chosen,
        part,
        (((0,), (0,)), ((), ())),
        precision=lax.Precision.HIGHEST,
        preferred_element_type=jnp.float32,
    )
    count = z.help * z.lev
    keep_ref[...] = ordered[:count].reshape(keep_ref.shape)
    send_ref[...] = ordered[z.spec_rows : z.spec_rows + count].reshape(send_ref.shape)


def filter_coefficients(z, share_refs, row_ref, kept_ref, slot_ref, keep_ref, send_ref):
    number = column_of(row_ref, NUMBER).astype(jnp.int32)
    coef = coefficients(z, add_shares(share_refs), number, kept_ref)
    store_spectra(z, coef, number, row_ref, slot_ref, keep_ref, send_ref)
    return coef


def depths(z, depth_ref, row_ref):
    level = column_of(row_ref, LEVEL)[: z.own]
    depth = jnp.zeros_like(level)
    for lev in range(z.lev):
        depth = jnp.where(level == lev, depth_ref[lev], depth)
    return depth


def east_forward(
    z, we_hbm, wn_hbm, g_hbm, row_ref, phase_ref, basis_ref,
    payload_ref, down_ref, up_ref, we_ref, wn_ref, g_ref, lhs_ref, sems,
):
    last = z.lon - 1
    edge = 2 * z.lev
    copies = [
        pltpu.make_async_copy(source, target, sems.at[n])
        for n, (source, target) in enumerate(((g_hbm, g_ref), (we_hbm, we_ref), (wn_hbm, wn_ref)))
    ]
    for copy in copies:
        copy.start()
    for copy in copies:
        copy.wait()
    g, we, wn = flat_rows(z, g_ref), flat_rows(z, we_ref), flat_rows(z, wn_ref)
    coef, sine = column_of(row_ref, EAST_COEF)[: z.own], column_of(row_ref, SINE)[: z.own]
    new = widen(z, we + CORIOLIS * sine * wn) - coef * east_diff(widen(z, g))
    tail = put_lane(new[:, z.ext - 128 :], 127, 0.0)
    new = jnp.concatenate([new[:, : z.ext - 128], tail], axis=1)
    forward_sums(z, pad_rows(new, z.rows), basis_ref, phase_ref, lhs_ref, payload_ref)
    cos, sin = phase_of(phase_ref, z.blocks)
    before = -coef * g[:, 0:1]
    payload_ref[: z.own, :HALF] += before * cos
    payload_ref[: z.own, HALF:] += before * sin
    spare = payload_ref[: z.own, SPARE:HALF]
    edges = ((g, last - 1), (g, last), (we, last), (wn, last), (g, 0), (g, 1), (we, 0), (wn, 0))
    for n, (x, column) in enumerate(edges):
        spare = put_lane(spare, KMAX - SPARE + n, x[:, column : column + 1])
    payload_ref[: z.own, SPARE:HALF] = spare
    down_ref[:edge] = g[z.own - edge :]
    down_ref[edge : edge + z.lev] = we[z.own - z.lev :]
    down_ref[edge + z.lev :] = wn[z.own - z.lev :]
    up_ref[:edge] = g[:edge]
    up_ref[edge : edge + z.lev] = we[: z.lev]
    up_ref[edge + z.lev :] = wn[: z.lev]


def north_forward(
    z, we_ref, wn_ref, g_ref, above_ref, below_ref, row_ref, phase_ref, basis_ref,
    payload_ref, north_ref, g_rows, lhs_ref,
):
    edge = 2 * z.lev
    coef = STEP_FACTOR * (2.0 * math.pi / z.nlon) / (math.pi / z.nlat)
    sine = column_of(row_ref, SINE)
    g = flat_rows(z, g_ref)
    g_rows[: z.own] = g
    g_rows[z.own : z.own + z.lev] = below_ref[: z.lev]
    g_rows[z.own + z.lev :] = above_ref[z.lev : edge]
    whole_g = g_rows[...]
    diff = roll(whole_g, -z.lev, 0) - roll(whole_g, z.lev, 0)
    north_ref[: z.own] = (
        flat_rows(z, wn_ref) - coef * diff[: z.own] - CORIOLIS * sine[: z.own] * flat_rows(z, we_ref)
    )
    for at, diff, ref in (
        (z.own, below_ref[z.lev : edge] - g[z.own - z.lev :], below_ref),
        (z.own + z.lev, g[: z.lev] - above_ref[: z.lev], above_ref),
    ):
        we, wn = ref[edge : edge + z.lev], ref[edge + z.lev :]
        north_ref[at : at + z.lev] = wn - coef * diff - CORIOLIS * sine[at : at + z.lev] * we
    forward_sums(z, widen(z, north_ref[...]), basis_ref, phase_ref, lhs_ref, payload_ref)


def east_inverse(
    z, depth_ref, we_ref, wn_ref, g_ref, thick_ref, row_ref, phase_ref, kept_ref, slot_ref, *rest
):
    shares, rest = rest[: z.n_lon], rest[z.n_lon :]
    basis_ref, final_ref, part_ref, keep_ref, send_ref, lhs_ref = rest
    coef = filter_coefficients(z, shares, row_ref, kept_ref, slot_ref, keep_ref, send_ref)
    blocks, before = inverse_blocks(z, coef, basis_ref, phase_ref, lhs_ref)
    filtered = jnp.concatenate(blocks, axis=1)[: z.own]
    tail = put_lane(filtered[:, z.ext - 128 :], 127, before[: z.own])
    filtered = jnp.concatenate([filtered[:, : z.ext - 128], tail], axis=1)

    first = KMAX - SPARE
    left, right = shares[1][: z.own, SPARE:HALF], shares[-1][: z.own, SPARE:HALF]
    at_right = z.lon - (z.ext - 128)

    def rimmed(ref, left_of, right_of):
        x = widen(z, flat_rows(z, ref))
        tail = x[:, z.ext - 128 :]
        for n, lane in enumerate(right_of):
            tail = put_lane(tail, at_right + n, right[:, first + lane : first + lane + 1])
        for n, lane in enumerate(left_of):
            tail = put_lane(tail, 127 - n, left[:, first + lane : first + lane + 1])
        return jnp.concatenate([x[:, : z.ext - 128], tail], axis=1)

    g = rimmed(g_ref, (1, 0), (4, 5))
    we, wn = rimmed(we_ref, (2,), (6,)), rimmed(wn_ref, (3,), (7,))
    coef, sine = column_of(row_ref, EAST_COEF)[: z.own], column_of(row_ref, SINE)[: z.own]
    new = we - coef * east_diff(g) + CORIOLIS * sine * wn
    final = jnp.where(column_of(row_ref, POLAR)[: z.own] > 0.0, filtered, new)
    final_ref[...] = final[:, : z.lon].reshape(final_ref.shape)
    change = depths(z, depth_ref, row_ref) * coef * east_diff(final)[:, : z.lon]
    part_ref[...] = flat_rows(z, thick_ref) - change


def north_inverse(
    z, depth_ref, north_ref, part_ref, surface_ref, row_ref, phase_ref, kept_ref, slot_ref, *rest
):
    shares, rest = rest[: z.n_lon], rest[z.n_lon :]
    basis_ref, final_ref, thick_ref, geo_ref, column_ref, keep_ref, send_ref, lhs_ref = rest
    coef = filter_coefficients(z, shares, row_ref, kept_ref, slot_ref, keep_ref, send_ref)
    blocks, _ = inverse_blocks(z, coef, basis_ref, phase_ref, lhs_ref)
    scale = depths(z, depth_ref, row_ref) * column_of(row_ref, NORTH_COEF)[: z.own]
    for block, filtered in enumerate(blocks):
        at = slice(block * BLOCK, min((block + 1) * BLOCK, z.lon))
        filtered = filtered[:, : at.stop - at.start]
        final = jnp.where(column_of(row_ref, POLAR) > 0.0, filtered, north_ref[:, at])
        final_ref[:, :, at] = final[: z.own].reshape(z.lat, z.lev, at.stop - at.start)
        scaled = final * column_of(row_ref, COSINE)
        diff = (roll(scaled, -z.lev, 0) - roll(scaled, z.lev, 0))[: z.own]
        thick = part_ref[:, at] - scale * diff
        thick_ref[:, :, at] = thick.reshape(z.lat, z.lev, at.stop - at.start)
    column = None
    for lev in reversed(range(z.lev)):
        one = thick_ref[:, lev, :]
        column = one if column is None else column + one
        geo_ref[:, lev, :] = surface_ref[...] + GRAVITY * column
    column_ref[...] = column


def call(kernel, n_in, out_shape, scratch, spaces=None, vmem=24):
    vmem_spec = pl.BlockSpec(memory_space=pltpu.VMEM)
    spaces = spaces or {}
    return pl.pallas_call(
        kernel,
        in_specs=[
            pl.BlockSpec(memory_space=spaces[n]) if n in spaces else vmem_spec for n in range(n_in)
        ],
        out_specs=[vmem_spec] * len(out_shape),
        out_shape=[jax.ShapeDtypeStruct(s, jnp.float32) for s in out_shape],
        scratch_shapes=scratch,
        compiler_params=pltpu.CompilerParams(vmem_limit_bytes=vmem * MIB),
        cost_estimate=pl.CostEstimate(flops=1, bytes_accessed=1, transcendentals=0),
    )


def shifted(block, axis, distance):
    count = lax.axis_size(axis)
    return lax.ppermute(block, axis, [(i, (i + distance) % count) for i in range(count)])


def level_inside(x):
    return jnp.swapaxes(x, -3, -2)


def local(
    wind_east, wind_north, thickness, geopot, surface_geopot, mean_depth, kept_modes, slot_table
):
    z = Sizes(thickness.shape, {axis: lax.axis_size(axis) for axis in ("lat", "lon", "lev")})
    lat_index = lax.axis_index("lat")
    wind_east, wind_north, thickness, geopot = (
        level_inside(x) for x in (wind_east, wind_north, thickness, geopot)
    )
    field = (z.lat, z.lev, z.lon)
    forward, inverse = (jnp.asarray(x) for x in basis_tables(z))
    phase = jnp.asarray(phase_table(z))
    per_row = jnp.asarray(row_table(z))
    kept = kept_modes[None, :]
    slots = slot_table[None, :]
    payload = (z.rows, WIDE)
    rims = (4 * z.lev, z.lon)
    spec = (z.help, z.lev, z.spec_width)
    columns_lhs = pltpu.VMEM((z.blocks * z.mm_rows, 3 * BLOCK), jnp.bfloat16)
    waves_lhs = pltpu.VMEM((z.blocks * z.mm_rows, 3 * WIDE), jnp.bfloat16)

    east_share, to_below, to_above = call(
        functools.partial(east_forward, z),
        6,
        [payload, rims, rims],
        [pltpu.VMEM(field, jnp.float32)] * 3 + [columns_lhs, pltpu.SemaphoreType.DMA((3,))],
        {n: pltpu.HBM for n in range(3)},
    )(wind_east, wind_north, geopot, per_row, phase, forward)
    east_others = [shifted(east_share, "lon", s) for s in range(1, z.n_lon)]

    odd = lat_index % 2 == 1
    met = []
    for start in range(2):
        pairs = [(i, i + 1) for i in range(start, z.n_lat - 1, 2)]
        rim = jnp.where(odd == (start == 1), to_below, to_above)
        met.append(lax.ppermute(rim, "lat", pairs + [(b, a) for a, b in pairs]))
    from_above, from_below = jnp.where(odd, met[0], met[1]), jnp.where(odd, met[1], met[0])

    north_share, north_new = call(
        functools.partial(north_forward, z),
        8,
        [payload, (z.rows, z.lon)],
        [pltpu.VMEM((z.rows, z.lon), jnp.float32), columns_lhs],
    )(wind_east, wind_north, geopot, from_above, from_below, per_row, phase, forward)
    north_others = [shifted(north_share, "lon", s) for s in range(1, z.n_lon)]

    east_final, thick_part, east_keep, east_send = call(
        functools.partial(east_inverse, z),
        10 + z.n_lon,
        [field, (z.own, z.lon), spec, spec],
        [waves_lhs],
        {0: pltpu.SMEM},
    )(
        mean_depth, wind_east, wind_north, geopot, thickness, per_row, phase, kept, slots,
        east_share, *east_others, inverse,
    )

    polar_devices = [
        i for i in range(z.n_lat) if i < z.n_lat // 4 or i >= z.n_lat - z.n_lat // 4
    ]
    to_helper = [(i, (i + z.half_axis) % z.n_lat) for i in polar_devices]
    east_arrived = lax.ppermute(east_send, "lat", to_helper)

    north_final, thick_new, geo_base, column, north_keep, north_send = call(
        functools.partial(north_inverse, z),
        9 + z.n_lon,
        [field, field, field, (z.lat, z.lon), spec, spec],
        [waves_lhs],
        {0: pltpu.SMEM},
    )(
        mean_depth, north_new, thick_part, surface_geopot, per_row, phase, kept, slots,
        north_share, *north_others, inverse,
    )
    north_arrived = lax.ppermute(north_send, "lat", to_helper)

    geo_new = geo_base
    for distance in range(1, z.n_lev):
        deeper = lax.ppermute(
            column, "lev", [(i, i - distance) for i in range(distance, z.n_lev)]
        )
        geo_new = geo_new + GRAVITY * deeper[:, None]
    is_polar = (lat_index < z.n_lat // 4) | (lat_index >= z.n_lat - z.n_lat // 4)
    spectra = jnp.stack(
        [
            jnp.where(is_polar, east_keep, east_arrived),
            jnp.where(is_polar, north_keep, north_arrived),
        ]
    )
    return tuple(level_inside(x) for x in (east_final, north_final, thick_new, geo_new, spectra))


def solution(mesh):
    field = P(("members", "lev"), "lat", "lon")
    return jax.shard_map(
        local,
        mesh=mesh,
        in_specs=(field, field, field, field, P("lat", "lon"), P("lev"), P(), P()),
        out_specs=(field, field, field, field, P(None, ("members", "lev"), "lat", "lon")),
        check_vma=False,
    )
```

profile of v0, /device:TPU:0, one launch (start us, length us, event | category | flops | bytes accessed | tf_op | source)
XLA Modules:
  0.0 58.6 jit_solution(8402400882605743626)
XLA Ops:
  0.6 0.0 copy-start
  0.7 1.2 %copy-done = f32[2,90,1440]{2,0,1:T(2,128)S(1)} copy-done((f32[2,90,1440]{2,0,1:T(2,128)S(1)}, f32[2,90,1440]{2,0,1:T(2,128)}, u32[]{:S(2)}) %copy-start) | copy-done | bytes 1036824
  1.9 0.0 copy-start.1
  1.9 1.2 %copy-done.1 = f32[2,90,1440]{2,0,1:T(2,128)S(1)} copy-done((f32[2,90,1440]{2,0,1:T(2,128)S(1)}, f32[2,90,1440]{2,0,1:T(2,128)}, u32[]{:S(2)}) %copy-start.1) | copy-done | bytes 1036824
  3.1 0.0 copy-start.2
  3.1 1.2 %copy-done.2 = f32[2,90,1440]{2,0,1:T(2,128)S(1)} copy-done((f32[2,90,1440]{2,0,1:T(2,128)S(1)}, f32[2,90,1440]{2,0,1:T(2,128)}, u32[]{:S(2)}) %copy-start.2) | copy-done | bytes 1036824
  4.4 0.0 copy-start.3
  4.4 1.0 %copy-done.3 = f32[4,184,8]{2,1,0:T(8,128)S(1)} copy-done((f32[4,184,8]{2,1,0:T(8,128)S(1)}, f32[4,184,8]{2,1,0:T(8,128)}, u32[]{:S(2)}) %copy-start.3) | copy-done | bytes 23576
  5.4 0.0 copy-start.5
  5.4 1.3 %copy-done.5 = bf16[768,768]{1,0:T(8,128)(2,1)S(1)} copy-done((bf16[768,768]{1,0:T(8,128)(2,1)S(1)}, bf16[768,768]{1,0:T(8,128)(2,1)}, u32[]{:S(2)}) %copy-start.5) | copy-done | bytes 1179672
  6.6 0.0 copy-start.10
  6.6 0.8 %copy-done.10 = f32[2,16,384]{2,1,0:T(8,128)S(1)} copy-done((f32[2,16,384]{2,1,0:T(8,128)S(1)}, f32[2,16,384]{2,1,0:T(8,128)}, u32[]{:S(2)}) %copy-start.10) | copy-done | bytes 49176
  7.4 3.2 %shard_map.155 = (f32[184,768]{1,0:T(8,128)S(1)}, f32[8,1440]{1,0:T(8,128)S(1)}, f32[8,1440]{1,0:T(8,128)S(1)}) custom-call(f32[90,2,1440]{2,1,0:T(2,128)S(1)} %bitcast.17, f32[90,2,1440]{2,1,0:T(2,128)S(1)} %bitcast.20, f32[90,2,1440]{2,1,0:T(2,128)S(1)} %bitcast.23, f32[4,184,8]{2,1,0:T(8,128)S(1)} %copy-done.3, f32[2,16,384]{2,1,0:T(8,128)S(1)} %copy-done.10, ...), custom_call_target="tpu_custom_call" | custom-call | flops 1 | bytes 1 | tf_op jit(solution)/shard_map/pallas_call | solution.py:413
  10.7 0.7 %collective-permute-start.2 = (f32[8,1440]{1,0:T(8,128)S(1)}, f32[8,1440]{1,0:T(8,128)S(1)}, u32[]{:S(2)}, u32[]{:S(2)}) collective-permute-start(f32[8,1440]{1,0:T(8,128)S(1)} %get-tuple-element.37), channel_id=1, source_target_pairs={{4,8},{8,4},{5,9},{9,5},{6,10},{10,6},{7,11},{11,7},{20,24},{24,20... | collective-permute-start | bytes 138248 | tf_op jit(solution)/shard_map/ppermute | solution.py:427
  11.4 5.9 %collective-permute-start.1 = (f32[8,1440]{1,0:T(8,128)S(1)}, f32[8,1440]{1,0:T(8,128)S(1)}, u32[]{:S(2)}, u32[]{:S(2)}) collective-permute-start(f32[8,1440]{1,0:T(8,128)S(1)} %get-tuple-element.38), channel_id=1, source_target_pairs={{0,4},{8,12},{4,0},{12,8},{1,5},{9,13},{5,1},{13,9},{2,6},{10,14},... | collective-permute-start | bytes 138248 | tf_op jit(solution)/shard_map/ppermute | solution.py:427
  17.3 1.5 %collective-permute-start = (f32[184,768]{1,0:T(8,128)S(1)}, f32[184,768]{1,0:T(8,128)S(1)}, u32[]{:S(2)}, u32[]{:S(2)}) collective-permute-start(f32[184,768]{1,0:T(8,128)S(1)} %get-tuple-element.20.rest_0_), channel_id=1, source_target_pairs={{0,2},{2,0},{1,3},{3,1},{4,6},{6,4},{5,7},{7,5},{8,10},{10,8},{9,1... | collective-permute-start | bytes 1695752 | tf_op jit(solution)/shard_map/ppermute | solution.py:386
  18.8 0.0 collective-permute-done.2
  18.8 0.6 %collective-permute-done.1 = f32[8,1440]{1,0:T(8,128)S(1)} collective-permute-done((f32[8,1440]{1,0:T(8,128)S(1)}, f32[8,1440]{1,0:T(8,128)S(1)}, u32[]{:S(2)}, u32[]{:S(2)}) %collective-permute-start.1) | collective-permute-done | bytes 46112 | tf_op jit(solution)/shard_map/ppermute | solution.py:427
  19.4 0.0 copy-start.6
  19.4 0.0 copy-start.9
  19.4 0.0 copy-start.13
  19.4 0.0 copy-start.14
  19.4 0.0 copy-start.15
  19.4 3.5 %shard_map.157 = (f32[184,768]{1,0:T(8,128)}, f32[184,1440]{1,0:T(8,128)S(1)}) custom-call(f32[90,2,1440]{2,1,0:T(2,128)S(1)} %bitcast.18, f32[90,2,1440]{2,1,0:T(2,128)S(1)} %bitcast.21, f32[90,2,1440]{2,1,0:T(2,128)S(1)} %bitcast.24, f32[8,1440]{1,0:T(8,128)S(1)} %get-tuple-element.36.above_ref, f32[8,1440]{1,0:T(8,128)S(1)} %get-tuple-element.35.below_ref, ...), custom_call_target="tpu_custom_call" | custom-call | flops 1 | bytes 1 | tf_op jit(solution)/shard_map/pallas_call | solution.py:430
  23.0 1.5 %collective-permute-start.3 = (f32[184,768]{1,0:T(8,128)}, f32[184,768]{1,0:T(8,128)}, u32[]{:S(2)}, u32[]{:S(2)}) collective-permute-start(f32[184,768]{1,0:T(8,128)} %get-tuple-element.26.rest_0_), channel_id=1, source_target_pairs={{0,2},{2,0},{1,3},{3,1},{4,6},{6,4},{5,7},{7,5},{8,10},{10,8},{9,1... | collective-permute-start | bytes 1695752 | tf_op jit(solution)/shard_map/ppermute | solution.py:386
  24.4 8.6 %collective-permute-done.rest_1_ = f32[184,768]{1,0:T(8,128)S(1)} collective-permute-done((f32[184,768]{1,0:T(8,128)S(1)}, f32[184,768]{1,0:T(8,128)S(1)}, u32[]{:S(2)}, u32[]{:S(2)}) %collective-permute-start) | collective-permute-done | bytes 565280 | tf_op jit(solution)/shard_map/ppermute | solution.py:386
  33.0 0.0 copy-done.6
  33.0 0.0 copy-done.9
  33.0 0.0 copy-done.13
  33.1 0.0 copy-done.14
  33.1 0.0 copy-done.15
  33.1 0.0 copy-start.4
  33.1 0.0 copy-start.11
  33.1 0.0 copy-start.12
  33.1 4.9 %shard_map.156 = (f32[90,2,1440]{2,1,0:T(2,128)}, f32[180,1440]{1,0:T(8,128)S(1)}, f32[45,2,360]{2,1,0:T(2,128)S(1)}, f32[45,2,360]{2,1,0:T(2,128)}) custom-call(f32[2]{0:T(128)S(1)} %copy-done.15, f32[90,2,1440]{2,1,0:T(2,128)S(1)} %bitcast.19, f32[90,2,1440]{2,1,0:T(2,128)S(1)} %bitcast.22, f32[90,2,1440]{2,1,0:T(2,128)S(1)} %bitcast.25, ...), custom_call_target="tpu_custom_call" | custom-call | flops 1 | bytes 1 | tf_op jit(solution)/shard_map/pallas_call | solution.py:438
  38.0 0.0 copy-start.7
  38.0 1.0 %copy-done.7 = f32[180,1440]{1,0:T(8,128)} copy-done((f32[180,1440]{1,0:T(8,128)}, f32[180,1440]{1,0:T(8,128)S(1)}, u32[]{:S(2)}) %copy-start.7) | copy-done | bytes 1036824
  39.0 2.5 %collective-permute-start.5 = (f32[45,2,360]{2,1,0:T(2,128)}, f32[45,2,360]{2,1,0:T(2,128)}, u32[]{:S(2)}, u32[]{:S(2)}) collective-permute-start(f32[45,2,360]{2,1,0:T(2,128)} %get-tuple-element.32), channel_id=1, source_target_pairs={{0,8},{12,4},{1,9},{13,5},{2,10},{14,6},{3,11},{15,7},{16,24},{28,... | collective-permute-start | bytes 388808 | tf_op jit(solution)/shard_map/ppermute | solution.py:453
  41.5 2.0 %collective-permute-done.3.rest_1_ = f32[184,768]{1,0:T(8,128)} collective-permute-done((f32[184,768]{1,0:T(8,128)}, f32[184,768]{1,0:T(8,128)}, u32[]{:S(2)}, u32[]{:S(2)}) %collective-permute-start.3) | collective-permute-done | bytes 565280 | tf_op jit(solution)/shard_map/ppermute | solution.py:386
  43.5 0.0 copy-done.4
  43.5 0.0 copy-done.11
  43.5 0.0 copy-done.12
  43.5 0.0 copy-start.8
  43.5 1.2 %copy-done.8 = f32[180,1440]{1,0:T(8,128)S(1)} copy-done((f32[180,1440]{1,0:T(8,128)S(1)}, f32[180,1440]{1,0:T(8,128)}, u32[]{:S(2)}) %copy-start.8) | copy-done | bytes 1036824
  44.8 6.1 %shard_map.158 = (f32[90,2,1440]{2,1,0:T(2,128)}, f32[90,2,1440]{2,1,0:T(2,128)}, f32[90,2,1440]{2,1,0:T(2,128)S(1)}, f32[90,1440]{1,0:T(8,128)S(1)}, f32[45,2,3...) custom-call(f32[2]{0:T(128)S(1)} %copy-done.15, f32[184,1440]{1,0:T(8,128)S(1)} %get-tuple-element.24.north_ref, ...), custom_call_target="tpu_custom_call" | custom-call | flops 1 | bytes 1 | tf_op jit(solution)/shard_map/pallas_call | solution.py:455
  50.9 2.2 %collective-permute-start.6 = (f32[45,2,360]{2,1,0:T(2,128)S(1)}, f32[45,2,360]{2,1,0:T(2,128)S(1)}, u32[]{:S(2)}, u32[]{:S(2)}) collective-permute-start(f32[45,2,360]{2,1,0:T(2,128)S(1)} %get-tuple-element.34), channel_id=1, source_target_pairs={{0,8},{12,4},{1,9},{13,5},{2,10},{14,6},{3,11},{15,7},{16,24},{28,... | collective-permute-start | bytes 388808 | tf_op jit(solution)/shard_map/ppermute | solution.py:465
  53.0 1.3 %collective-permute-start.4 = (f32[90,1440]{1,0:T(8,128)S(1)}, f32[90,1440]{1,0:T(8,128)S(1)}, u32[]{:S(2)}, u32[]{:S(2)}) collective-permute-start(f32[90,1440]{1,0:T(8,128)S(1)} %get-tuple-element.30), channel_id=1, source_target_pairs={{1,0},{3,2},{5,4},{7,6},{9,8},{11,10},{13,12},{15,14},{17,16},{19,... | collective-permute-start | bytes 1555208 | tf_op jit(solution)/shard_map/ppermute | solution.py:469
  54.3 0.0 collective-permute-done.5
  54.4 0.1 select_bitcast_fusion.1
  54.4 1.2 %collective-permute-done.6 = f32[45,2,360]{2,1,0:T(2,128)S(1)} collective-permute-done((f32[45,2,360]{2,1,0:T(2,128)S(1)}, f32[45,2,360]{2,1,0:T(2,128)S(1)}, u32[]{:S(2)}, u32[]{:S(2)}) %collective-permute-start.6) | collective-permute-done | bytes 129632 | tf_op jit(solution)/shard_map/ppermute | solution.py:465
  55.6 0.1 select_bitcast_fusion
  55.7 0.8 %maximum_bitcast_fusion = f32[2,2,45,360]{3,1,2,0:T(2,128)} fusion(f32[1,45,2,360]{3,2,1,0:T(2,128)S(1)} %select_bitcast_fusion, f32[1,45,2,360]{3,2,1,0:T(2,128)S(1)} %select_bitcast_fusion.1), kind=kLoop, calls=%fused_computation.2 | loop fusion | flops 64800 | bytes 518400 | tf_op jit(solution)/shard_map/transpose | solution.py:390
  56.5 0.4 collective-permute-done.4
  57.0 1.6 %add_bitcast_fusion = f32[2,90,1440]{2,0,1:T(2,128)} fusion(f32[90,2,1440]{2,1,0:T(2,128)S(1)} %get-tuple-element.29, f32[90,1440]{1,0:T(8,128)S(1)} %broadcast_multiply_fusion), kind=kLoop, calls=%fused_computation | loop fusion | flops 259200 | bytes 2592000 | tf_op jit(solution)/shard_map/transpose | solution.py:390
  (3 shorter events, 0.1 us)
Async XLA Ops:
  0.6 1.2 %copy-start = (f32[2,90,1440]{2,0,1:T(2,128)S(1)}, f32[2,90,1440]{2,0,1:T(2,128)}, u32[]{:S(2)}) copy-start(f32[2,90,1440]{2,0,1:T(2,128)} %param.12) | copy-start | bytes 3110404
  1.9 1.2 %copy-start.1 = (f32[2,90,1440]{2,0,1:T(2,128)S(1)}, f32[2,90,1440]{2,0,1:T(2,128)}, u32[]{:S(2)}) copy-start(f32[2,90,1440]{2,0,1:T(2,128)} %param.13) | copy-start | bytes 3110404
  3.1 1.2 %copy-start.2 = (f32[2,90,1440]{2,0,1:T(2,128)S(1)}, f32[2,90,1440]{2,0,1:T(2,128)}, u32[]{:S(2)}) copy-start(f32[2,90,1440]{2,0,1:T(2,128)} %param.15) | copy-start | bytes 3110404
  4.4 1.0 %copy-start.3 = (f32[4,184,8]{2,1,0:T(8,128)S(1)}, f32[4,184,8]{2,1,0:T(8,128)}, u32[]{:S(2)}) copy-start(f32[4,184,8]{2,1,0:T(8,128)} %constant.36.clone.row_ref) | copy-start | bytes 70660
  5.4 1.3 %copy-start.5 = (bf16[768,768]{1,0:T(8,128)(2,1)S(1)}, bf16[768,768]{1,0:T(8,128)(2,1)}, u32[]{:S(2)}) copy-start(bf16[768,768]{1,0:T(8,128)(2,1)} %constant.33.clone.basis_ref) | copy-start | bytes 3538948
  6.6 0.8 %copy-start.10 = (f32[2,16,384]{2,1,0:T(8,128)S(1)}, f32[2,16,384]{2,1,0:T(8,128)}, u32[]{:S(2)}) copy-start(f32[2,16,384]{2,1,0:T(8,128)} %constant.35.clone.phase_ref) | copy-start | bytes 147460
  10.7 8.1 %collective-permute-start.2 = (f32[8,1440]{1,0:T(8,128)S(1)}, f32[8,1440]{1,0:T(8,128)S(1)}, u32[]{:S(2)}, u32[]{:S(2)}) collective-permute-start(f32[8,1440]{1,0:T(8,128)S(1)} %get-tuple-element.37), channel_id=1, source_target_pairs={{4,8},{8,4},{5,9},{9,5},{6,10},{10,6},{7,11},{11,7},{20,24},{24,20... | collective-permute-start | bytes 138248 | tf_op jit(solution)/shard_map/ppermute | solution.py:427
  11.4 8.0 %collective-permute-start.1 = (f32[8,1440]{1,0:T(8,128)S(1)}, f32[8,1440]{1,0:T(8,128)S(1)}, u32[]{:S(2)}, u32[]{:S(2)}) collective-permute-start(f32[8,1440]{1,0:T(8,128)S(1)} %get-tuple-element.38), channel_id=1, source_target_pairs={{0,4},{8,12},{4,0},{12,8},{1,5},{9,13},{5,1},{13,9},{2,6},{10,14},... | collective-permute-start | bytes 138248 | tf_op jit(solution)/shard_map/ppermute | solution.py:427
  17.3 15.7 %collective-permute-start = (f32[184,768]{1,0:T(8,128)S(1)}, f32[184,768]{1,0:T(8,128)S(1)}, u32[]{:S(2)}, u32[]{:S(2)}) collective-permute-start(f32[184,768]{1,0:T(8,128)S(1)} %get-tuple-element.20.rest_0_), channel_id=1, source_target_pairs={{0,2},{2,0},{1,3},{3,1},{4,6},{6,4},{5,7},{7,5},{8,10},{10,8},{9,1... | collective-permute-start | bytes 1695752 | tf_op jit(solution)/shard_map/ppermute | solution.py:386
  19.4 13.7 %copy-start.6 = (bf16[2304,256]{1,0:T(8,128)(2,1)S(1)}, bf16[2304,256]{1,0:T(8,128)(2,1)}, u32[]{:S(2)}) copy-start(bf16[2304,256]{1,0:T(8,128)(2,1)} %constant.34.clone.rest_2_) | copy-start | bytes 3538948
  19.4 13.6 %copy-start.9 = (f32[2,90,1440]{2,0,1:T(2,128)S(1)}, f32[2,90,1440]{2,0,1:T(2,128)}, u32[]{:S(2)}) copy-start(f32[2,90,1440]{2,0,1:T(2,128)} %param.14) | copy-start | bytes 3110404
  19.4 13.6 %copy-start.13 = (s32[180]{0:T(256)S(1)}, s32[180]{0:T(256)}, u32[]{:S(2)}) copy-start(s32[180]{0:T(256)} %param.18) | copy-start | bytes 2164
  19.4 13.6 %copy-start.14 = (s32[180]{0:T(256)S(1)}, s32[180]{0:T(256)}, u32[]{:S(2)}) copy-start(s32[180]{0:T(256)} %param.19) | copy-start | bytes 2164
  19.4 13.6 %copy-start.15 = (f32[2]{0:T(128)S(1)}, f32[2]{0:T(128)}, u32[]{:S(2)}) copy-start(f32[2]{0:T(128)} %depth_ref.3) | copy-start | bytes 28
  23.0 20.5 %collective-permute-start.3 = (f32[184,768]{1,0:T(8,128)}, f32[184,768]{1,0:T(8,128)}, u32[]{:S(2)}, u32[]{:S(2)}) collective-permute-start(f32[184,768]{1,0:T(8,128)} %get-tuple-element.26.rest_0_), channel_id=1, source_target_pairs={{0,2},{2,0},{1,3},{3,1},{4,6},{6,4},{5,7},{7,5},{8,10},{10,8},{9,1... | collective-permute-start | bytes 1695752 | tf_op jit(solution)/shard_map/ppermute | solution.py:386
  33.1 10.4 %copy-start.4 = (f32[4,184,8]{2,1,0:T(8,128)S(1)}, f32[4,184,8]{2,1,0:T(8,128)}, u32[]{:S(2)}) copy-start(f32[4,184,8]{2,1,0:T(8,128)} %constant.36.clone.row_ref) | copy-start | bytes 70660
  33.1 10.4 %copy-start.11 = (f32[2,16,384]{2,1,0:T(8,128)S(1)}, f32[2,16,384]{2,1,0:T(8,128)}, u32[]{:S(2)}) copy-start(f32[2,16,384]{2,1,0:T(8,128)} %constant.35.clone.phase_ref) | copy-start | bytes 147460
  33.1 10.4 %copy-start.12 = (f32[90,1440]{1,0:T(8,128)S(1)}, f32[90,1440]{1,0:T(8,128)}, u32[]{:S(2)}) copy-start(f32[90,1440]{1,0:T(8,128)} %surface_ref.1) | copy-start | bytes 1555204
  38.0 1.0 %copy-start.7 = (f32[180,1440]{1,0:T(8,128)}, f32[180,1440]{1,0:T(8,128)S(1)}, u32[]{:S(2)}) copy-start(f32[180,1440]{1,0:T(8,128)S(1)} %get-tuple-element.25.part_ref) | copy-start | bytes 3110404
  39.0 15.3 %collective-permute-start.5 = (f32[45,2,360]{2,1,0:T(2,128)}, f32[45,2,360]{2,1,0:T(2,128)}, u32[]{:S(2)}, u32[]{:S(2)}) collective-permute-start(f32[45,2,360]{2,1,0:T(2,128)} %get-tuple-element.32), channel_id=1, source_target_pairs={{0,8},{12,4},{1,9},{13,5},{2,10},{14,6},{3,11},{15,7},{16,24},{28,... | collective-permute-start | bytes 388808 | tf_op jit(solution)/shard_map/ppermute | solution.py:453
  43.5 1.3 %copy-start.8 = (f32[180,1440]{1,0:T(8,128)S(1)}, f32[180,1440]{1,0:T(8,128)}, u32[]{:S(2)}) copy-start(f32[180,1440]{1,0:T(8,128)} %copy-done.7) | copy-start | bytes 3110404
  50.9 4.7 %collective-permute-start.6 = (f32[45,2,360]{2,1,0:T(2,128)S(1)}, f32[45,2,360]{2,1,0:T(2,128)S(1)}, u32[]{:S(2)}, u32[]{:S(2)}) collective-permute-start(f32[45,2,360]{2,1,0:T(2,128)S(1)} %get-tuple-element.34), channel_id=1, source_target_pairs={{0,8},{12,4},{1,9},{13,5},{2,10},{14,6},{3,11},{15,7},{16,24},{28,... | collective-permute-start | bytes 388808 | tf_op jit(solution)/shard_map/ppermute | solution.py:465
  53.0 3.9 %collective-permute-start.4 = (f32[90,1440]{1,0:T(8,128)S(1)}, f32[90,1440]{1,0:T(8,128)S(1)}, u32[]{:S(2)}, u32[]{:S(2)}) collective-permute-start(f32[90,1440]{1,0:T(8,128)S(1)} %get-tuple-element.30), channel_id=1, source_target_pairs={{1,0},{3,2},{5,4},{7,6},{9,8},{11,10},{13,12},{15,14},{17,16},{19,... | collective-permute-start | bytes 1555208 | tf_op jit(solution)/shard_map/ppermute | solution.py:469
where the time goes:
time: 59.1 us; the launch traced here: 58.6 us
  Pallas kernels  17.8 us (30%)
  starting transfers between devices  15.5 us (26%)
  waiting for transfers between devices  12.8 us (22%)
  local copies, waits for them, and re-layouts  9.11 us (15%)
  other arithmetic  2.66 us (5%)
  between operations  0.84 us (1%)
    ppermute x2, waiting for transfers between devices, shifted(): lax.ppermute(block, axis, [(i, (i + distance) % count) for i in range(cou...  10.6 us
    unnamed x32, local copies, waits for them, and re-layouts  9.11 us
    ppermute x2, starting transfers between devices, local(): met.append(lax.ppermute(rim, 'lat', pairs + [(b, a) for a, b in pairs]))  6.58 us
    pallas_call x1, Pallas kernels, local(): call(functools.partial(north_inverse, z), 9 + z.n_lon, [field, field, fie...  6.09 us
    pallas_call x1, Pallas kernels, local(): call(functools.partial(east_inverse, z), 10 + z.n_lon, [field, (z.own, z....  4.91 us
    pallas_call x1, Pallas kernels, local(): call(functools.partial(north_forward, z), 8, [payload, (z.rows, z.lon)],...  3.52 us
    pallas_call x1, Pallas kernels, local(): call(functools.partial(east_forward, z), 6, [payload, rims, rims], [pltpu...  3.24 us
    ppermute x2, starting transfers between devices, shifted(): lax.ppermute(block, axis, [(i, (i + distance) % count) for i in range(cou...  2.93 us
  transfers between devices with their start and end apart: 7, of which 5 were waited for; matrix products, arithmetic and copies ran while one was open for 2% of the time, Pallas kernels for 25%

commit v1 on v0

v1 whole, which is shorter than its diff:
```python
import functools
import math

import jax
import jax.numpy as jnp
import numpy as np
from jax import lax
from jax.experimental import pallas as pl
from jax.experimental.pallas import tpu as pltpu
from jax.sharding import PartitionSpec as P

KMAX = 360
HALF = 384
WIDE = 2 * HALF
SPARE = HALF - 128
BLOCK = 256
INVERSE_BLOCK = 768

STEP_FACTOR = 0.15
CORIOLIS = 0.2
GRAVITY = 0.25

MIB = 1024 * 1024

EAST_COEF, SINE, COSINE, NORTH_COEF, LEVEL, POLAR, NUMBER, OWN = range(8)


def round_up(value, step):
    return -(-value // step) * step


class Sizes:
    def __init__(self, shape, counts):
        self.lev, self.lat, self.lon = shape
        self.n_lat, self.n_lon, self.n_lev = counts["lat"], counts["lon"], counts["lev"]
        self.nlat, self.nlon = self.lat * self.n_lat, self.lon * self.n_lon
        self.polar = self.nlat // 4
        self.help = self.lat // 2
        self.half_axis = self.n_lat // 2
        self.own = self.lat * self.lev
        self.rows = self.own + 2 * self.lev
        assert self.rows % 8 == 0
        self.mm_rows = round_up(self.rows, 16)
        self.ext = round_up(self.lon + 4, BLOCK)
        self.blocks = self.ext // BLOCK
        self.inverse_block = min(INVERSE_BLOCK, self.ext)
        assert self.ext % self.inverse_block == 0
        self.spec_width = 2 * KMAX // self.n_lon


def high_low(x):
    x = x.astype(np.float32)
    high = x.astype(jnp.bfloat16)
    return high, (x - high.astype(np.float32)).astype(jnp.bfloat16)


def basis_tables(z):
    k = np.arange(KMAX)
    angle = (np.arange(z.inverse_block)[:, None] * k[None, :] % z.nlon) * (2.0 * np.pi / z.nlon)
    full = np.zeros((z.inverse_block, WIDE))
    full[:, :KMAX] = np.cos(angle)
    full[:, HALF : HALF + KMAX] = np.sin(angle)
    high, low = high_low(full)
    forward = np.concatenate([high[:BLOCK], high[:BLOCK], low[:BLOCK]], axis=0)
    inverse = np.concatenate([high.T, high.T, low.T], axis=0)
    return forward, inverse


def phase_table(z):
    k = np.arange(KMAX)
    table = np.zeros((z.n_lon, round_up(2 * z.blocks + 2, 8), HALF), np.float32)
    for place in range(z.n_lon):
        for n, column in enumerate([*range(0, z.ext, BLOCK), -1]):
            angle = ((place * z.lon + column) * k % z.nlon) * (2.0 * np.pi / z.nlon)
            table[place, 2 * n, :KMAX] = np.cos(angle)
            table[place, 2 * n + 1, :KMAX] = np.sin(angle)
    return table


def row_table(z):
    lam_step = np.float32(2.0 * math.pi / z.nlon)
    phi_step = np.float32(math.pi / z.nlat)
    latitude = np.float32(-0.5 * math.pi) + (
        np.arange(z.nlat, dtype=np.float32) + np.float32(0.5)
    ) * phi_step
    cosine = np.cos(latitude.astype(np.float64)).astype(np.float32)
    sine = np.sin(latitude.astype(np.float64)).astype(np.float32)
    north_coef = np.float32(STEP_FACTOR) * lam_step / phi_step
    table = np.zeros((z.n_lat, z.rows, 8), np.float32)
    for place in range(z.n_lat):
        for flat in range(z.rows):
            inner, level = flat // z.lev, flat % z.lev
            inner = -1 if inner == z.lat + 1 else inner
            row = place * z.lat + inner
            one = table[place, flat]
            one[LEVEL], one[NUMBER] = level, -1
            one[OWN] = 0 <= inner < z.lat
            if 0 <= row < z.nlat:
                one[EAST_COEF] = np.float32(STEP_FACTOR) / cosine[row]
                one[SINE], one[COSINE] = sine[row], cosine[row]
                one[NORTH_COEF] = north_coef / cosine[row]
                if row < z.polar:
                    one[POLAR], one[NUMBER] = 1, row
                elif row >= z.nlat - z.polar:
                    one[POLAR], one[NUMBER] = 1, row - (z.nlat - 2 * z.polar)
    return table


def store_split(lhs_ref, first_row, x):
    rows, width = x.shape
    high = x.astype(jnp.bfloat16)
    low = (x - high.astype(jnp.float32)).astype(jnp.bfloat16)
    at = slice(first_row, first_row + rows)
    lhs_ref[at, :width] = high
    lhs_ref[at, width : 2 * width] = low
    lhs_ref[at, 2 * width :] = high


def pad_rows(x, rows):
    return jnp.concatenate([x, jnp.zeros((rows - x.shape[0], x.shape[1]), x.dtype)], axis=0)


def phase_of(phase_ref, n):
    return phase_ref[2 * n : 2 * n + 1], phase_ref[2 * n + 1 : 2 * n + 2]


def store_blocks(z, x, lhs_ref):
    for block in range(z.blocks):
        part = pad_rows(x[:, block * BLOCK : (block + 1) * BLOCK], z.mm_rows)
        store_split(lhs_ref, block * z.mm_rows, part)


def turn_blocks(z, sums, phase_ref, out_ref):
    rows = sums.shape[0] // z.blocks
    real = imag = None
    for block in range(z.blocks):
        cos, sin = phase_of(phase_ref, block)
        part = sums[block * rows : block * rows + out_ref.shape[0]]
        a, b = part[:, :HALF], part[:, HALF:]
        more_real, more_imag = a * cos - b * sin, a * sin + b * cos
        real = more_real if real is None else real + more_real
        imag = more_imag if imag is None else imag + more_imag
    out_ref[:, :HALF] = real
    out_ref[:, HALF:] = imag


def inverse_blocks(z, coef, basis_ref, phase_ref, lhs_ref):
    a, b = coef[:, :HALF], coef[:, HALF:]
    width = z.inverse_block
    blocks = range(z.ext // width)
    for block in blocks:
        cos, sin = phase_of(phase_ref, block * width // BLOCK)
        turned = jnp.concatenate([a * cos + b * sin, b * cos - a * sin], axis=1)
        store_split(lhs_ref, block * z.mm_rows, pad_rows(turned, z.mm_rows))
    rows = jnp.dot(lhs_ref[...], basis_ref[...], preferred_element_type=jnp.float32)
    cos, sin = phase_of(phase_ref, z.blocks)
    before = jnp.sum(a * cos + b * sin, axis=1, keepdims=True)
    return [rows[n * z.mm_rows : n * z.mm_rows + coef.shape[0]] for n in blocks], before


def roll(x, shift, axis):
    return pltpu.roll(x, shift % x.shape[axis], axis)


def east_diff(x):
    return roll(x, -1, 1) - roll(x, 1, 1)


def flat_rows(z, ref):
    return ref[...].reshape(z.own, ref.shape[2])


def widen(z, x):
    return jnp.concatenate([x, jnp.zeros((x.shape[0], z.ext - x.shape[1]), x.dtype)], axis=1)


def put_lane(x, at, column):
    lane = lax.broadcasted_iota(jnp.int32, x.shape, 1)
    return jnp.where(lane == at, column, x)


def column_of(row_ref, which):
    return row_ref[:, which : which + 1]


def north_factor(z):
    return STEP_FACTOR * (2.0 * math.pi / z.nlon) / (math.pi / z.nlat)


def look_up(number, table_ref):
    table = table_ref[...].astype(jnp.float32)
    lane = lax.broadcasted_iota(jnp.int32, (number.shape[0], table.shape[1]), 1)
    return jnp.sum(jnp.where(lane == number, table, 0.0), axis=1, keepdims=True)


def coefficients(z, sums, number, kept_ref):
    lane = lax.broadcasted_iota(jnp.int32, (1, WIDE), 1)
    k = jnp.where(lane < HALF, lane, lane - HALF)
    weight = jnp.where(k == 0, 1.0 / z.nlon, 2.0 / z.nlon).astype(jnp.float32)
    keep = (k.astype(jnp.float32) < look_up(number, kept_ref)) & (k < KMAX)
    return jnp.where(keep, sums * weight, 0.0)


def in_slot_order(z, values, number, row_ref, slot_ref, distance):
    rows, count = values.shape[0], z.help * z.lev
    owner = lax.rem(lax.axis_index("lat") + distance, z.n_lat)
    place = look_up(number, slot_ref).astype(jnp.int32) - owner * z.help
    own = (column_of(row_ref, OWN)[:rows] > 0.0) & (number >= 0)
    place = jnp.where(own & (place >= 0) & (place < z.help), place, -count)
    place = place * z.lev + column_of(row_ref, LEVEL)[:rows].astype(jnp.int32)
    lane = lax.broadcasted_iota(jnp.int32, (rows, round_up(count, 128)), 1)
    ordered = lax.dot_general(
        (lane == place).astype(jnp.float32),
        values,
        (((0,), (0,)), ((), ())),
        precision=lax.Precision.HIGHEST,
        preferred_element_type=jnp.float32,
    )
    return ordered[:count]


def sector_part(z, coef, place):
    part = None
    for one in range(z.n_lon):
        first = one * z.spec_width
        first = first if first < KMAX else first - KMAX + HALF
        this = coef[:, first : first + z.spec_width]
        part = this if part is None else jnp.where(place == one, this, part)
    return part


def depths(z, depth_ref, row_ref):
    level = column_of(row_ref, LEVEL)[: z.own]
    depth = jnp.zeros_like(level)
    for lev in range(z.lev):
        depth = jnp.where(level == lev, depth_ref[lev], depth)
    return depth


def store_rims(z, ref, g, we, wn, last):
    edge = 2 * z.lev
    ref[:edge] = g[z.own - edge :] if last else g[:edge]
    ref[edge : edge + z.lev] = we[z.own - z.lev :] if last else we[: z.lev]
    ref[edge + z.lev :] = wn[z.own - z.lev :] if last else wn[: z.lev]


def east_forward(
    z, we_hbm, wn_hbm, g_hbm, row_hbm, phase_hbm, basis_hbm,
    share_ref, even_ref, odd_ref, we_ref, wn_ref, g_ref, row_ref, phase_ref, basis_ref, lhs_ref, sems,
):
    pairs = (
        (row_hbm.at[lax.axis_index("lat")], row_ref),
        (phase_hbm.at[lax.axis_index("lon")], phase_ref),
        (g_hbm, g_ref),
        (we_hbm, we_ref),
        (wn_hbm, wn_ref),
        (basis_hbm, basis_ref),
    )
    copies = [pltpu.make_async_copy(*pair, sems.at[n]) for n, pair in enumerate(pairs)]
    for copy in copies:
        copy.start()
    for copy in copies[:-1]:
        copy.wait()
    g, we, wn = flat_rows(z, g_ref), flat_rows(z, we_ref), flat_rows(z, wn_ref)
    coef, sine = column_of(row_ref, EAST_COEF)[: z.own], column_of(row_ref, SINE)[: z.own]
    new = widen(z, we + CORIOLIS * sine * wn) - coef * east_diff(widen(z, g))
    tail = put_lane(new[:, z.ext - 128 :], 127, 0.0)
    store_blocks(z, jnp.concatenate([new[:, : z.ext - 128], tail], axis=1), lhs_ref)

    odd = lax.rem(lax.axis_index("lat"), 2) == 1
    last, flat = z.lat - 1, (z.lev, z.lon)
    far = (g_ref[last - 1], g_ref[last], we_ref[last], wn_ref[last])
    near = (g_ref[0], g_ref[1], we_ref[0], wn_ref[0])
    for n, (bottom, top) in enumerate(zip(far, near, strict=True)):
        at = slice(n * z.lev, (n + 1) * z.lev)
        even_ref[at] = jnp.where(odd, top, bottom).reshape(flat)
        odd_ref[at] = jnp.where(odd, bottom, top).reshape(flat)

    copies[-1].wait()
    sums = jnp.dot(lhs_ref[...], basis_ref[...], preferred_element_type=jnp.float32)
    turn_blocks(z, sums, phase_ref, share_ref)
    cos, sin = phase_of(phase_ref, z.blocks)
    before = -coef * g[:, 0:1]
    share_ref[:, :HALF] += before * cos
    share_ref[:, HALF:] += before * sin
    spare = share_ref[:, SPARE:HALF]
    last = z.lon - 1
    edges = ((g, last - 1), (g, last), (we, last), (wn, last), (g, 0), (g, 1), (we, 0), (wn, 0))
    for n, (x, column) in enumerate(edges):
        spare = put_lane(spare, KMAX - SPARE + n, x[:, column : column + 1])
    share_ref[:, SPARE:HALF] = spare


def north_forward(
    z, we_ref, wn_ref, g_ref, even_ref, odd_ref, row_ref, phase_ref, basis_ref, kept_ref, slot_ref, *rest
):
    share_ref, north_ref, sends, (g_rows, lhs_ref) = rest[0], rest[1], rest[2:-2], rest[-2:]
    edge, lev = 2 * z.lev, z.lev
    odd = lax.rem(lax.axis_index("lat"), 2) == 1
    below = jnp.where(odd, odd_ref[...], even_ref[...])
    above = jnp.where(odd, even_ref[...], odd_ref[...])
    coef, sine = north_factor(z), CORIOLIS * column_of(row_ref, SINE)
    own = flat_rows(z, g_ref)
    g_rows[: z.own] = own
    g_rows[z.own : z.own + lev] = below[:lev]
    g_rows[z.own + lev :] = above[lev:edge]
    g = g_rows[...]
    diff = (roll(g, -lev, 0) - roll(g, lev, 0))[: z.own]
    north_ref[: z.own] = flat_rows(z, wn_ref) - coef * diff - sine[: z.own] * flat_rows(z, we_ref)
    for at, diff, rim in (
        (z.own, below[lev:edge] - own[z.own - lev :], below),
        (z.own + lev, own[:lev] - above[:lev], above),
    ):
        we, wn = rim[edge : edge + lev], rim[edge + lev :]
        north_ref[at : at + lev] = wn - coef * diff - sine[at : at + lev] * we
    store_blocks(z, widen(z, north_ref[...]), lhs_ref)
    sums = jnp.dot(lhs_ref[...], basis_ref[...], preferred_element_type=jnp.float32)
    turn_blocks(z, sums, phase_ref, share_ref)
    number = column_of(row_ref, NUMBER).astype(jnp.int32)
    masked = coefficients(z, share_ref[...], number, kept_ref)
    ordered = in_slot_order(z, masked, number, row_ref, slot_ref, z.half_axis)
    for distance, send_ref in enumerate(sends):
        place = lax.rem(lax.axis_index("lon") + distance, z.n_lon)
        send_ref[...] = sector_part(z, ordered, place).reshape(send_ref.shape)


def east_inverse(
    z, depth_ref, we_ref, wn_ref, g_ref, thick_ref, row_ref, phase_ref, kept_ref, slot_ref, *rest
):
    shares, rest = rest[: z.n_lon], rest[z.n_lon :]
    basis_ref, final_ref, part_ref, keep_ref, send_ref, lhs_ref = rest
    number = column_of(row_ref, NUMBER)[: z.own].astype(jnp.int32)
    coef = coefficients(z, sum(ref[...] for ref in shares), number, kept_ref)
    part = sector_part(z, coef, lax.axis_index("lon"))
    for distance, ref in ((0, keep_ref), (z.half_axis, send_ref)):
        ref[...] = in_slot_order(z, part, number, row_ref, slot_ref, distance).reshape(ref.shape)
    blocks, before = inverse_blocks(z, coef, basis_ref, phase_ref, lhs_ref)
    filtered = jnp.concatenate(blocks, axis=1)
    tail = put_lane(filtered[:, z.ext - 128 :], 127, before)
    filtered = jnp.concatenate([filtered[:, : z.ext - 128], tail], axis=1)

    first = KMAX - SPARE
    left, right = shares[1][:, SPARE:HALF], shares[-1][:, SPARE:HALF]
    at_right = z.lon - (z.ext - 128)

    def rimmed(ref, left_of, right_of):
        x = widen(z, flat_rows(z, ref))
        tail = x[:, z.ext - 128 :]
        for n, lane in enumerate(right_of):
            tail = put_lane(tail, at_right + n, right[:, first + lane : first + lane + 1])
        for n, lane in enumerate(left_of):
            tail = put_lane(tail, 127 - n, left[:, first + lane : first + lane + 1])
        return jnp.concatenate([x[:, : z.ext - 128], tail], axis=1)

    g = rimmed(g_ref, (1, 0), (4, 5))
    we, wn = rimmed(we_ref, (2,), (6,)), rimmed(wn_ref, (3,), (7,))
    coef, sine = column_of(row_ref, EAST_COEF)[: z.own], column_of(row_ref, SINE)[: z.own]
    new = we - coef * east_diff(g) + CORIOLIS * sine * wn
    final = jnp.where(column_of(row_ref, POLAR)[: z.own] > 0.0, filtered, new)
    final_ref[...] = final[:, : z.lon].reshape(final_ref.shape)
    change = depths(z, depth_ref, row_ref) * coef * east_diff(final)[:, : z.lon]
    part_ref[...] = flat_rows(z, thick_ref) - change


def on_polar_band(z):
    lat_index = lax.axis_index("lat")
    return (lat_index < z.n_lat // 4) | (lat_index >= z.n_lat - z.n_lat // 4)


def north_inverse(
    z, depth_ref, north_ref, part_ref, row_ref, phase_ref, kept_ref, slot_ref, *rest
):
    shares, arrived, rest = rest[: z.n_lon], rest[z.n_lon : 2 * z.n_lon], rest[2 * z.n_lon :]
    basis_ref, final_ref, thick_ref, column_ref, spectra_ref, lhs_ref = rest
    number = column_of(row_ref, NUMBER).astype(jnp.int32)
    coef = coefficients(z, sum(ref[...] for ref in shares), number, kept_ref)
    part = sector_part(z, coef, lax.axis_index("lon"))
    keep = in_slot_order(z, part, number, row_ref, slot_ref, 0).reshape(spectra_ref.shape)
    spectra_ref[...] = jnp.where(on_polar_band(z), keep, sum(ref[...] for ref in arrived))
    blocks, _ = inverse_blocks(z, coef, basis_ref, phase_ref, lhs_ref)
    scale = depths(z, depth_ref, row_ref) * column_of(row_ref, NORTH_COEF)[: z.own]
    for block, filtered in enumerate(blocks):
        at = slice(block * z.inverse_block, min((block + 1) * z.inverse_block, z.lon))
        filtered = filtered[:, : at.stop - at.start]
        final = jnp.where(column_of(row_ref, POLAR) > 0.0, filtered, north_ref[:, at])
        final_ref[:, :, at] = final[: z.own].reshape(z.lat, z.lev, at.stop - at.start)
        scaled = final * column_of(row_ref, COSINE)
        diff = (roll(scaled, -z.lev, 0) - roll(scaled, z.lev, 0))[: z.own]
        thick = part_ref[:, at] - scale * diff
        thick_ref[:, :, at] = thick.reshape(z.lat, z.lev, at.stop - at.start)
    column_ref[...] = sum(thick_ref[:, lev, :] for lev in range(z.lev))


def join_spectra(z, keep_ref, arrived_ref, north_ref, spectra_ref):
    spectra_ref[0] = jnp.where(on_polar_band(z), keep_ref[...], arrived_ref[...])
    spectra_ref[1] = north_ref[...]


def close(z, thick_ref, surface_ref, spectra_ref, *rest):
    del spectra_ref
    deeper, geo_ref = rest[:-1], rest[-1]
    column = sum(ref[...] for ref in deeper) if deeper else 0.0
    for lev in reversed(range(z.lev)):
        column = column + thick_ref[:, lev, :]
        geo_ref[:, lev, :] = surface_ref[...] + GRAVITY * column


def call(kernel, n_in, out_shape, scratch, micros, spaces=None, vmem=24):
    vmem_spec = pl.BlockSpec(memory_space=pltpu.VMEM)
    spaces = spaces or {}
    return pl.pallas_call(
        kernel,
        in_specs=[
            pl.BlockSpec(memory_space=spaces[n]) if n in spaces else vmem_spec for n in range(n_in)
        ],
        out_specs=[vmem_spec] * len(out_shape),
        out_shape=[
            jax.ShapeDtypeStruct(s, jnp.float32) if isinstance(s, tuple) else s for s in out_shape
        ],
        scratch_shapes=scratch,
        compiler_params=pltpu.CompilerParams(vmem_limit_bytes=vmem * MIB),
        cost_estimate=pl.CostEstimate(
            flops=int(micros * 1.15e9), bytes_accessed=0, transcendentals=0
        ),
    )


def shifted(block, axis, distance):
    count = lax.axis_size(axis)
    return lax.ppermute(block, axis, [(i, (i + distance) % count) for i in range(count)])


def level_inside(x):
    return jnp.swapaxes(x, -3, -2)


def local(
    wind_east, wind_north, thickness, geopot, surface_geopot, mean_depth, kept_modes, slot_table
):
    z = Sizes(thickness.shape, {axis: lax.axis_size(axis) for axis in ("lat", "lon", "lev")})
    wind_east, wind_north, thickness, geopot = (
        level_inside(x) for x in (wind_east, wind_north, thickness, geopot)
    )
    field = (z.lat, z.lev, z.lon)
    forward, inverse = (jnp.asarray(x) for x in basis_tables(z))
    phase = jnp.asarray(phase_table(z))
    per_row = jnp.asarray(row_table(z))
    kept = kept_modes[None, :]
    slots = slot_table[None, :]
    payload = (z.rows, WIDE)
    rims = (4 * z.lev, z.lon)
    spec = (z.help, z.lev, z.spec_width)
    waves_lhs = pltpu.VMEM((z.ext // z.inverse_block * z.mm_rows, 3 * WIDE), jnp.bfloat16)

    row_shape, phase_shape = per_row.shape[1:], phase.shape[1:]
    in_hbm = [
        pltpu.with_memory_space_constraint(x, pltpu.HBM)
        for x in (wind_east, wind_north, geopot, per_row, phase, forward)
    ]
    columns_lhs = pltpu.VMEM((z.blocks * z.mm_rows, 3 * BLOCK), jnp.bfloat16)
    waves_lhs = pltpu.VMEM((z.ext // z.inverse_block * z.mm_rows, 3 * WIDE), jnp.bfloat16)

    east_share, to_even, to_odd, wind_east, wind_north, geopot, per_row, phase, forward = call(
        functools.partial(east_forward, z),
        6,
        [(z.own, WIDE), rims, rims]
        + [field, field, field, row_shape, phase_shape]
        + [jax.ShapeDtypeStruct(forward.shape, forward.dtype)],
        [columns_lhs, pltpu.SemaphoreType.DMA((6,))],
        4,
        {n: pltpu.HBM for n in range(6)},
    )(*in_hbm)
    east_shares = [east_share] + [shifted(east_share, "lon", s) for s in range(1, z.n_lon)]
    met = []
    for start, rim in enumerate((to_even, to_odd)):
        pairs = [(i, i + 1) for i in range(start, z.n_lat - 1, 2)]
        met.append(lax.ppermute(rim, "lat", pairs + [(b, a) for a, b in pairs]))

    north_share, north_new, *north_sends = call(
        functools.partial(north_forward, z),
        10,
        [(z.rows, WIDE), (z.rows, z.lon)] + [spec] * z.n_lon,
        [pltpu.VMEM((z.rows, z.lon), jnp.float32), columns_lhs],
        0.2,
    )(wind_east, wind_north, geopot, *met, per_row, phase, forward, kept, slots)
    north_shares = [north_share] + [shifted(north_share, "lon", s) for s in range(1, z.n_lon)]

    polar_bands = [i for i in range(z.n_lat) if i < z.n_lat // 4 or i >= z.n_lat - z.n_lat // 4]
    to_helper = [(i, (i + z.half_axis) % z.n_lat) for i in polar_bands]
    north_arrived = []
    for distance, send in enumerate(north_sends):
        route = [
            (a * z.n_lon + lon, b * z.n_lon + (lon + distance) % z.n_lon)
            for a, b in to_helper
            for lon in range(z.n_lon)
        ]
        north_arrived.append(lax.ppermute(send, ("lat", "lon"), route))

    east_final, thick_part, east_keep, east_send = call(
        functools.partial(east_inverse, z),
        10 + z.n_lon,
        [field, (z.own, z.lon), spec, spec],
        [waves_lhs],
        1,
        {0: pltpu.SMEM},
    )(
        mean_depth, wind_east, wind_north, geopot, thickness, per_row, phase, kept, slots,
        *east_shares, inverse,
    )
    east_arrived = lax.ppermute(east_send, "lat", to_helper)

    north_final, thick_new, column, north_spectra = call(
        functools.partial(north_inverse, z),
        8 + 2 * z.n_lon,
        [field, field, (z.lat, z.lon), spec],
        [waves_lhs],
        2,
        {0: pltpu.SMEM},
    )(
        mean_depth, north_new, thick_part, per_row, phase, kept, slots,
        *north_shares, *north_arrived, inverse,
    )

    deeper = [
        lax.ppermute(column, "lev", [(i, i - distance) for i in range(distance, z.n_lev)])
        for distance in range(1, z.n_lev)
    ]
    (spectra,) = call(functools.partial(join_spectra, z), 3, [(2, *spec)], [], 4.2)(
        east_keep, east_arrived, north_spectra
    )
    (geo_new,) = call(functools.partial(close, z), 3 + len(deeper), [field], [], 1)(
        thick_new, surface_geopot, spectra, *deeper
    )
    return tuple(level_inside(x) for x in (east_final, north_final, thick_new, geo_new, spectra))


def solution(mesh):
    field = P(("members", "lev"), "lat", "lon")
    return jax.shard_map(
        local,
        mesh=mesh,
        in_specs=(field, field, field, field, P("lat", "lon"), P("lev"), P(), P()),
        out_specs=(field, field, field, field, P(None, ("members", "lev"), "lat", "lon")),
        check_vma=False,
    )
```

time: 59.1 us -> 47.1 us (0.80)
  the two profiles are of different devices: /device:TPU:0 before, /device:TPU:9 now
where the time goes in v1:
time: 47.1 us; the launch traced here: 46.9 us
  Pallas kernels  20.9 us (44%)
  starting transfers between devices  13.9 us (30%)
  waiting for transfers between devices  10.3 us (22%)
  local copies, waits for them, and re-layouts  0.99 us (2%)
  between operations  0.8 us (2%)
    ppermute x2, waiting for transfers between devices, shifted(): lax.ppermute(block, axis, [(i, (i + distance) % count) for i in range(cou...  7.49 us
    pallas_call x1, Pallas kernels, local(): call(functools.partial(east_inverse, z), 10 + z.n_lon, [field, (z.own, z....  5.12 us
    pallas_call x1, Pallas kernels, local(): call(functools.partial(east_forward, z), 6, [(z.own, WIDE), rims, rims] +...  5.11 us
    pallas_call x1, Pallas kernels, local(): call(functools.partial(north_inverse, z), 8 + 2 * z.n_lon, [field, field,...  4.78 us
    ppermute x2, starting transfers between devices, local(): met.append(lax.ppermute(rim, 'lat', pairs + [(b, a) for a, b in pairs]))  4.49 us
    ppermute x1, starting transfers between devices, local(): lax.ppermute(column, 'lev', [(i, i - distance) for i in range(distance, z...  3.78 us
    pallas_call x1, Pallas kernels, local(): call(functools.partial(north_forward, z), 10, [(z.rows, WIDE), (z.rows, z...  3.66 us
    ppermute x2, starting transfers between devices, local(): north_arrived.append(lax.ppermute(send, ('lat', 'lon'), route))  2.57 us
  transfers between devices with their start and end apart: 8, of which 4 were waited for; matrix products, arithmetic and copies ran while one was open for 0% of the time, Pallas kernels for 31%

profile of v1, /device:TPU:9, one launch (start us, length us, event | category | flops | bytes accessed | tf_op | source)
XLA Modules:
  0.0 46.9 jit_solution(3882347675794604785)
XLA Ops:
  0.6 0.0 copy-start.2
  0.6 0.0 copy-start.3
  0.7 5.1 %shard_map.155 = (f32[180,768]{1,0:T(8,128)S(1)}, f32[8,1440]{1,0:T(8,128)S(1)}, f32[8,1440]{1,0:T(8,128)S(1)}, f32[90,2,1440]{2,1,0:T(2,128)S(1)}, f32[90,2,144...) custom-call(f32[90,2,1440]{2,1,0:T(2,128)} %bitcast.20, ...), custom_call_target="tpu_custom_call" | custom-call | flops 4600000000 | tf_op jit(solution)/shard_map/pallas_call | solution.py:463
  5.8 1.3 %collective-permute-start = (f32[180,768]{1,0:T(8,128)S(1)}, f32[180,768]{1,0:T(8,128)S(1)}, u32[]{:S(2)}, u32[]{:S(2)}) collective-permute-start(f32[180,768]{1,0:T(8,128)S(1)} %get-tuple-element.31.rest_0_), channel_id=1, source_target_pairs={{0,2},{2,0},{1,3},{3,1},{4,6},{6,4},{5,7},{7,5},{8,10},{10,8},{9,1... | collective-permute-start | bytes 1658888 | tf_op jit(solution)/shard_map/ppermute | solution.py:430
  7.0 0.2 collective-permute-start.1
  7.2 4.3 %collective-permute-start.2 = (f32[8,1440]{1,0:T(8,128)S(1)}, f32[8,1440]{1,0:T(8,128)S(1)}, u32[]{:S(2)}, u32[]{:S(2)}) collective-permute-start(f32[8,1440]{1,0:T(8,128)S(1)} %get-tuple-element.34), channel_id=1, source_target_pairs={{4,8},{8,4},{5,9},{9,5},{6,10},{10,6},{7,11},{11,7},{20,24},{24,20... | collective-permute-start | bytes 138248 | tf_op jit(solution)/shard_map/ppermute | solution.py:477
  11.5 0.0 collective-permute-done.1.even_ref
  11.6 1.7 %collective-permute-done.2.odd_ref = f32[8,1440]{1,0:T(8,128)S(1)} collective-permute-done((f32[8,1440]{1,0:T(8,128)S(1)}, f32[8,1440]{1,0:T(8,128)S(1)}, u32[]{:S(2)}, u32[]{:S(2)}) %collective-permute-start.2) | collective-permute-done | bytes 46112 | tf_op jit(solution)/shard_map/ppermute | solution.py:477
  13.3 0.0 copy-done.2
  13.3 0.0 copy-done.3
  13.3 0.0 copy-start
  13.3 0.0 copy-start.1
  13.3 0.0 copy-start.4
  13.3 3.7 %shard_map.157 = (f32[184,768]{1,0:T(8,128)S(1)}, f32[184,1440]{1,0:T(8,128)S(1)}, f32[45,2,360]{2,1,0:T(2,128)S(1)}, f32[45,2,360]{2,1,0:T(2,128)S(1)}) custom-call(f32[90,2,1440]{2,1,0:T(2,128)S(1)} %get-tuple-element.26.we_ref, f32[90,2,1440]{2,1,0:T(2,128)S(1)} %get-tuple-element.27.wn_ref, f32[90,2,1440]{2,1,0:T(2,128)S(1)} %get-tuple-element.28.g_ref, ...), custom_call_target="tpu_custom_call" | custom-call | flops 230000000 | tf_op jit(solution)/shard_map/pallas_call | solution.py:479
  17.0 0.3 collective-permute-start.3
  17.3 1.3 %collective-permute-start.4 = (f32[45,2,360]{2,1,0:T(2,128)S(1)}, f32[45,2,360]{2,1,0:T(2,128)S(1)}, u32[]{:S(2)}, u32[]{:S(2)}) collective-permute-start(f32[45,2,360]{2,1,0:T(2,128)S(1)} %get-tuple-element.39), channel_id=1, source_target_pairs={{0,8},{2,10},{12,4},{14,6},{1,9},{3,11},{13,5},{15,7},{16,24},{18,... | collective-permute-start | bytes 388808 | tf_op jit(solution)/shard_map/ppermute | solution.py:497
  18.6 1.3 %collective-permute-start.5 = (f32[45,2,360]{2,1,0:T(2,128)S(1)}, f32[45,2,360]{2,1,0:T(2,128)S(1)}, u32[]{:S(2)}, u32[]{:S(2)}) collective-permute-start(f32[45,2,360]{2,1,0:T(2,128)S(1)} %get-tuple-element.40), channel_id=1, source_target_pairs={{0,10},{2,8},{12,6},{14,4},{1,11},{3,9},{13,7},{15,5},{16,26},{18,... | collective-permute-start | bytes 388808 | tf_op jit(solution)/shard_map/ppermute | solution.py:497
  19.9 0.0 collective-permute-done.rest_1_
  19.9 0.0 copy-done
  19.9 0.0 copy-done.1
  19.9 0.0 copy-done.4
  19.9 5.1 %shard_map.156 = (f32[90,2,1440]{2,1,0:T(2,128)}, f32[180,1440]{1,0:T(8,128)S(1)}, f32[45,2,360]{2,1,0:T(2,128)S(1)}, f32[45,2,360]{2,1,0:T(2,128)S(1)}) custom-call(f32[2]{0:T(128)S(1)} %copy-done.4, f32[90,2,1440]{2,1,0:T(2,128)S(1)} %get-tuple-element.26.we_ref, f32[90,2,1440]{2,1,0:T(2,128)S(1)} %get-tuple-element.27.wn_ref, ...), custom_call_target="tpu_custom_call" | custom-call | flops 1150000000 | tf_op jit(solution)/shard_map/pallas_call | solution.py:499
  25.1 1.5 %collective-permute-start.6 = (f32[45,2,360]{2,1,0:T(2,128)S(1)}, f32[45,2,360]{2,1,0:T(2,128)S(1)}, u32[]{:S(2)}, u32[]{:S(2)}) collective-permute-start(f32[45,2,360]{2,1,0:T(2,128)S(1)} %get-tuple-element.44), channel_id=1, source_target_pairs={{0,8},{12,4},{1,9},{13,5},{2,10},{14,6},{3,11},{15,7},{16,24},{28,... | collective-permute-start | bytes 388808 | tf_op jit(solution)/shard_map/ppermute | solution.py:510
  26.5 0.0 collective-permute-done.4.rest_2_
  26.5 0.2 collective-permute-done.5.rest_3_
  26.8 7.5 %collective-permute-done.3.rest_1_ = f32[184,768]{1,0:T(8,128)S(1)} collective-permute-done((f32[184,768]{1,0:T(8,128)S(1)}, f32[184,768]{1,0:T(8,128)S(1)}, u32[]{:S(2)}, u32[]{:S(2)}) %collective-permute-start.3) | collective-permute-done | bytes 565280 | tf_op jit(solution)/shard_map/ppermute | solution.py:430
  34.3 4.8 %shard_map.158 = (f32[90,2,1440]{2,1,0:T(2,128)}, f32[90,2,1440]{2,1,0:T(2,128)}, f32[90,1440]{1,0:T(8,128)S(1)}, f32[45,2,360]{2,1,0:T(2,128)S(1)}) custom-call(f32[2]{0:T(128)S(1)} %copy-done.4, f32[184,1440]{1,0:T(8,128)S(1)} %get-tuple-element.36.north_ref, f32[180,1440]{1,0:T(8,128)S(1)} %get-tuple-element.37.part_ref, ...), custom_call_target="tpu_custom_call" | custom-call | flops 2300000000 | tf_op jit(solution)/shard_map/pallas_call | solution.py:512
  39.1 3.8 %collective-permute-start.7 = (f32[90,1440]{1,0:T(8,128)S(1)}, f32[90,1440]{1,0:T(8,128)S(1)}, u32[]{:S(2)}, u32[]{:S(2)}) collective-permute-start(f32[90,1440]{1,0:T(8,128)S(1)} %get-tuple-element.46), channel_id=1, source_target_pairs={{1,0},{3,2},{5,4},{7,6},{9,8},{11,10},{13,12},{15,14},{17,16},{19,... | collective-permute-start | bytes 1555208 | tf_op jit(solution)/shard_map/ppermute | solution.py:525
  42.8 0.0 collective-permute-done.6.arrived_ref
  42.9 0.0 copy-start.5
  42.9 0.0 copy-start.6
  42.9 0.8 %shard_map.159.spectra_ref = f32[2,45,2,360]{3,2,1,0:T(2,128)} custom-call(f32[45,2,360]{2,1,0:T(2,128)S(1)} %get-tuple-element.43.keep_ref, f32[45,2,360]{2,1,0:T(2,128)S(1)} %collective-permute-done.6.arrived_ref, f32[45,2,360]{2,1,0:T(2,128)S(1)} %get-tuple-element.45.north_ref), custom_call_target="tpu_custom_call" | custom-call | flops 4830000128 | tf_op jit(solution)/shard_map/pallas_call | solution.py:528
  43.6 0.8 %collective-permute-done.7.rest_0_ = f32[90,1440]{1,0:T(8,128)S(1)} collective-permute-done((f32[90,1440]{1,0:T(8,128)S(1)}, f32[90,1440]{1,0:T(8,128)S(1)}, u32[]{:S(2)}, u32[]{:S(2)}) %collective-permute-start.7) | collective-permute-done | bytes 518432 | tf_op jit(solution)/shard_map/ppermute | solution.py:525
  44.4 0.0 copy-done.5
  44.4 0.0 copy-done.6
  44.4 0.0 copy-start.7
  44.4 1.0 %copy-done.7 = f32[2,45,2,360]{3,2,1,0:T(2,128)S(1)} copy-done((f32[2,45,2,360]{3,2,1,0:T(2,128)S(1)}, f32[2,45,2,360]{3,2,1,0:T(2,128)}, u32[]{:S(2)}) %copy-start.7) | copy-done | bytes 259224
  45.4 1.5 %shard_map.160 = f32[90,2,1440]{2,1,0:T(2,128)} custom-call(f32[90,2,1440]{2,1,0:T(2,128)S(1)} %copy-done.6, f32[90,1440]{1,0:T(8,128)S(1)} %copy-done.5, f32[2,45,2,360]{3,2,1,0:T(2,128)S(1)} %copy-done.7, f32[90,1440]{1,0:T(8,128)S(1)} %collective-permute-done.7.rest_0_), custom_call_target="tpu_custom_call" | custom-call | flops 1150000000 | tf_op jit(solution)/shard_map/pallas_call | solution.py:531
Async XLA Ops:
  0.6 12.7 %copy-start.2 = (s32[180]{0:T(256)S(1)}, s32[180]{0:T(256)}, u32[]{:S(2)}) copy-start(s32[180]{0:T(256)} %param.18) | copy-start | bytes 2164
  0.6 12.7 %copy-start.3 = (s32[180]{0:T(256)S(1)}, s32[180]{0:T(256)}, u32[]{:S(2)}) copy-start(s32[180]{0:T(256)} %param.19) | copy-start | bytes 2164
  5.8 14.1 %collective-permute-start = (f32[180,768]{1,0:T(8,128)S(1)}, f32[180,768]{1,0:T(8,128)S(1)}, u32[]{:S(2)}, u32[]{:S(2)}) collective-permute-start(f32[180,768]{1,0:T(8,128)S(1)} %get-tuple-element.31.rest_0_), channel_id=1, source_target_pairs={{0,2},{2,0},{1,3},{3,1},{4,6},{6,4},{5,7},{7,5},{8,10},{10,8},{9,1... | collective-permute-start | bytes 1658888 | tf_op jit(solution)/shard_map/ppermute | solution.py:430
  7.0 4.5 %collective-permute-start.1 = (f32[8,1440]{1,0:T(8,128)S(1)}, f32[8,1440]{1,0:T(8,128)S(1)}, u32[]{:S(2)}, u32[]{:S(2)}) collective-permute-start(f32[8,1440]{1,0:T(8,128)S(1)} %get-tuple-element.33), channel_id=1, source_target_pairs={{0,4},{8,12},{4,0},{12,8},{1,5},{9,13},{5,1},{13,9},{2,6},{10,14},... | collective-permute-start | bytes 138248 | tf_op jit(solution)/shard_map/ppermute | solution.py:477
  7.2 6.1 %collective-permute-start.2 = (f32[8,1440]{1,0:T(8,128)S(1)}, f32[8,1440]{1,0:T(8,128)S(1)}, u32[]{:S(2)}, u32[]{:S(2)}) collective-permute-start(f32[8,1440]{1,0:T(8,128)S(1)} %get-tuple-element.34), channel_id=1, source_target_pairs={{4,8},{8,4},{5,9},{9,5},{6,10},{10,6},{7,11},{11,7},{20,24},{24,20... | collective-permute-start | bytes 138248 | tf_op jit(solution)/shard_map/ppermute | solution.py:477
  13.3 6.6 %copy-start = (bf16[2304,768]{1,0:T(8,128)(2,1)S(1)}, bf16[2304,768]{1,0:T(8,128)(2,1)}, u32[]{:S(2)}) copy-start(bf16[2304,768]{1,0:T(8,128)(2,1)} %constant.9.clone.rest_2_.rest_4_) | copy-start | bytes 10616836
  13.3 6.6 %copy-start.1 = (f32[2,90,1440]{2,0,1:T(2,128)S(1)}, f32[2,90,1440]{2,0,1:T(2,128)}, u32[]{:S(2)}) copy-start(f32[2,90,1440]{2,0,1:T(2,128)} %param.14) | copy-start | bytes 3110404
  13.3 6.6 %copy-start.4 = (f32[2]{0:T(128)S(1)}, f32[2]{0:T(128)}, u32[]{:S(2)}) copy-start(f32[2]{0:T(128)} %depth_ref.3) | copy-start | bytes 28
  17.0 17.3 %collective-permute-start.3 = (f32[184,768]{1,0:T(8,128)S(1)}, f32[184,768]{1,0:T(8,128)S(1)}, u32[]{:S(2)}, u32[]{:S(2)}) collective-permute-start(f32[184,768]{1,0:T(8,128)S(1)} %get-tuple-element.38.rest_0_), channel_id=1, source_target_pairs={{0,2},{2,0},{1,3},{3,1},{4,6},{6,4},{5,7},{7,5},{8,10},{10,8},{9,1... | collective-permute-start | bytes 1695752 | tf_op jit(solution)/shard_map/ppermute | solution.py:430
  17.3 9.2 %collective-permute-start.4 = (f32[45,2,360]{2,1,0:T(2,128)S(1)}, f32[45,2,360]{2,1,0:T(2,128)S(1)}, u32[]{:S(2)}, u32[]{:S(2)}) collective-permute-start(f32[45,2,360]{2,1,0:T(2,128)S(1)} %get-tuple-element.39), channel_id=1, source_target_pairs={{0,8},{2,10},{12,4},{14,6},{1,9},{3,11},{13,5},{15,7},{16,24},{18,... | collective-permute-start | bytes 388808 | tf_op jit(solution)/shard_map/ppermute | solution.py:497
  18.6 8.2 %collective-permute-start.5 = (f32[45,2,360]{2,1,0:T(2,128)S(1)}, f32[45,2,360]{2,1,0:T(2,128)S(1)}, u32[]{:S(2)}, u32[]{:S(2)}) collective-permute-start(f32[45,2,360]{2,1,0:T(2,128)S(1)} %get-tuple-element.40), channel_id=1, source_target_pairs={{0,10},{2,8},{12,6},{14,4},{1,11},{3,9},{13,7},{15,5},{16,26},{18,... | collective-permute-start | bytes 388808 | tf_op jit(solution)/shard_map/ppermute | solution.py:497
  25.1 17.8 %collective-permute-start.6 = (f32[45,2,360]{2,1,0:T(2,128)S(1)}, f32[45,2,360]{2,1,0:T(2,128)S(1)}, u32[]{:S(2)}, u32[]{:S(2)}) collective-permute-start(f32[45,2,360]{2,1,0:T(2,128)S(1)} %get-tuple-element.44), channel_id=1, source_target_pairs={{0,8},{12,4},{1,9},{13,5},{2,10},{14,6},{3,11},{15,7},{16,24},{28,... | collective-permute-start | bytes 388808 | tf_op jit(solution)/shard_map/ppermute | solution.py:510
  39.1 5.4 %collective-permute-start.7 = (f32[90,1440]{1,0:T(8,128)S(1)}, f32[90,1440]{1,0:T(8,128)S(1)}, u32[]{:S(2)}, u32[]{:S(2)}) collective-permute-start(f32[90,1440]{1,0:T(8,128)S(1)} %get-tuple-element.46), channel_id=1, source_target_pairs={{1,0},{3,2},{5,4},{7,6},{9,8},{11,10},{13,12},{15,14},{17,16},{19,... | collective-permute-start | bytes 1555208 | tf_op jit(solution)/shard_map/ppermute | solution.py:525
  42.9 1.6 %copy-start.5 = (f32[90,1440]{1,0:T(8,128)S(1)}, f32[90,1440]{1,0:T(8,128)}, u32[]{:S(2)}) copy-start(f32[90,1440]{1,0:T(8,128)} %surface_ref.1) | copy-start | bytes 1555204
  42.9 1.6 %copy-start.6 = (f32[90,2,1440]{2,1,0:T(2,128)S(1)}, f32[90,2,1440]{2,1,0:T(2,128)}, u32[]{:S(2)}) copy-start(f32[90,2,1440]{2,1,0:T(2,128)} %get-tuple-element.42.thick_ref) | copy-start | bytes 3110404
  44.4 1.0 %copy-start.7 = (f32[2,45,2,360]{3,2,1,0:T(2,128)S(1)}, f32[2,45,2,360]{3,2,1,0:T(2,128)}, u32[]{:S(2)}) copy-start(f32[2,45,2,360]{3,2,1,0:T(2,128)} %shard_map.159.spectra_ref) | copy-start | bytes 777604

commit v2 on v1

--- a/solution.py
+++ b/solution.py
@@ -46,6 +46,8 @@
         self.inverse_block = min(INVERSE_BLOCK, self.ext)
         assert self.ext % self.inverse_block == 0
         self.spec_width = 2 * KMAX // self.n_lon
+        self.helped = self.help * self.lev
+        self.ahead = round_up(self.helped, 8)
 
 
 def high_low(x):
@@ -106,6 +108,11 @@
     return table
 
 
+def on_polar_band(z):
+    lat_index = lax.axis_index("lat")
+    return (lat_index < z.n_lat // 4) | (lat_index >= z.n_lat - z.n_lat // 4)
+
+
 def store_split(lhs_ref, first_row, x):
     rows, width = x.shape
     high = x.astype(jnp.bfloat16)
@@ -124,38 +131,39 @@
     return phase_ref[2 * n : 2 * n + 1], phase_ref[2 * n + 1 : 2 * n + 2]
 
 
-def store_blocks(z, x, lhs_ref):
+def forward_sums(z, x, basis_ref, phase_ref, lhs_ref, out_ref, at=slice(None)):
+    count = round_up(x.shape[0], 16)
     for block in range(z.blocks):
-        part = pad_rows(x[:, block * BLOCK : (block + 1) * BLOCK], z.mm_rows)
-        store_split(lhs_ref, block * z.mm_rows, part)
-
-
-def turn_blocks(z, sums, phase_ref, out_ref):
-    rows = sums.shape[0] // z.blocks
+        part = pad_rows(x[:, block * BLOCK : (block + 1) * BLOCK], count)
+        store_split(lhs_ref, block * count, part)
+    lhs = lhs_ref[: z.blocks * count]
+    sums = jnp.dot(lhs, basis_ref[...], preferred_element_type=jnp.float32)
     real = imag = None
     for block in range(z.blocks):
         cos, sin = phase_of(phase_ref, block)
-        part = sums[block * rows : block * rows + out_ref.shape[0]]
+        part = sums[block * count : block * count + x.shape[0]]
         a, b = part[:, :HALF], part[:, HALF:]
         more_real, more_imag = a * cos - b * sin, a * sin + b * cos
         real = more_real if real is None else real + more_real
         imag = more_imag if imag is None else imag + more_imag
-    out_ref[:, :HALF] = real
-    out_ref[:, HALF:] = imag
-
-
-def inverse_blocks(z, coef, basis_ref, phase_ref, lhs_ref):
+    out_ref[at, :HALF] = real
+    out_ref[at, HALF:] = imag
+
+
+def inverse_rows(z, coef, basis_ref, phase_ref, lhs_ref, out_ref, at=slice(None)):
     a, b = coef[:, :HALF], coef[:, HALF:]
-    width = z.inverse_block
+    count, width = round_up(coef.shape[0], 16), z.inverse_block
     blocks = range(z.ext // width)
     for block in blocks:
         cos, sin = phase_of(phase_ref, block * width // BLOCK)
         turned = jnp.concatenate([a * cos + b * sin, b * cos - a * sin], axis=1)
-        store_split(lhs_ref, block * z.mm_rows, pad_rows(turned, z.mm_rows))
-    rows = jnp.dot(lhs_ref[...], basis_ref[...], preferred_element_type=jnp.float32)
-    cos, sin = phase_of(phase_ref, z.blocks)
-    before = jnp.sum(a * cos + b * sin, axis=1, keepdims=True)
-    return [rows[n * z.mm_rows : n * z.mm_rows + coef.shape[0]] for n in blocks], before
+        store_split(lhs_ref, block * count, pad_rows(turned, count))
+    lhs = lhs_ref[: len(blocks) * count]
+    rows = jnp.dot(lhs, basis_ref[...], preferred_element_type=jnp.float32)
+    for block in blocks:
+        out_ref[at, block * width : (block + 1) * width] = rows[
+            block * count : block * count + coef.shape[0]
+        ]
 
 
 def roll(x, shift, axis):
@@ -193,30 +201,37 @@
     return jnp.sum(jnp.where(lane == number, table, 0.0), axis=1, keepdims=True)
 
 
-def coefficients(z, sums, number, kept_ref):
+def coefficients(z, sums, kept):
     lane = lax.broadcasted_iota(jnp.int32, (1, WIDE), 1)
     k = jnp.where(lane < HALF, lane, lane - HALF)
     weight = jnp.where(k == 0, 1.0 / z.nlon, 2.0 / z.nlon).astype(jnp.float32)
-    keep = (k.astype(jnp.float32) < look_up(number, kept_ref)) & (k < KMAX)
+    keep = (k.astype(jnp.float32) < kept) & (k < KMAX)
     return jnp.where(keep, sums * weight, 0.0)
 
 
-def in_slot_order(z, values, number, row_ref, slot_ref, distance):
-    rows, count = values.shape[0], z.help * z.lev
-    owner = lax.rem(lax.axis_index("lat") + distance, z.n_lat)
-    place = look_up(number, slot_ref).astype(jnp.int32) - owner * z.help
-    own = (column_of(row_ref, OWN)[:rows] > 0.0) & (number >= 0)
-    place = jnp.where(own & (place >= 0) & (place < z.help), place, -count)
-    place = place * z.lev + column_of(row_ref, LEVEL)[:rows].astype(jnp.int32)
-    lane = lax.broadcasted_iota(jnp.int32, (rows, round_up(count, 128)), 1)
-    ordered = lax.dot_general(
-        (lane == place).astype(jnp.float32),
+def slot_order(z, number, row_ref, slot_ref):
+    lat_index = lax.axis_index("lat")
+    slot = look_up(number, slot_ref).astype(jnp.int32)
+    theirs = slot - lax.rem(lat_index + z.half_axis, z.n_lat) * z.help
+    mine = slot - lat_index * z.help
+    level = column_of(row_ref, LEVEL).astype(jnp.int32)
+    flat = lax.broadcasted_iota(jnp.int32, slot.shape, 0)
+    place = jnp.where((mine >= 0) & (mine < z.help), z.helped + mine * z.lev + level, -1)
+    place = jnp.where((theirs >= 0) & (theirs < z.help), theirs * z.lev + level, place)
+    place = jnp.where(number >= 0, place, -1)
+    place = jnp.where(flat < z.own, place, flat)
+    lane = lax.broadcasted_iota(jnp.int32, (z.rows, round_up(z.rows, 128)), 1)
+    return (lane == place).astype(jnp.float32)
+
+
+def reorder(chosen, values):
+    return lax.dot_general(
+        chosen,
         values,
         (((0,), (0,)), ((), ())),
         precision=lax.Precision.HIGHEST,
         preferred_element_type=jnp.float32,
     )
-    return ordered[:count]
 
 
 def sector_part(z, coef, place):
@@ -262,11 +277,6 @@
     for copy in copies[:-1]:
         copy.wait()
     g, we, wn = flat_rows(z, g_ref), flat_rows(z, we_ref), flat_rows(z, wn_ref)
-    coef, sine = column_of(row_ref, EAST_COEF)[: z.own], column_of(row_ref, SINE)[: z.own]
-    new = widen(z, we + CORIOLIS * sine * wn) - coef * east_diff(widen(z, g))
-    tail = put_lane(new[:, z.ext - 128 :], 127, 0.0)
-    store_blocks(z, jnp.concatenate([new[:, : z.ext - 128], tail], axis=1), lhs_ref)
-
     odd = lax.rem(lax.axis_index("lat"), 2) == 1
     last, flat = z.lat - 1, (z.lev, z.lon)
     far = (g_ref[last - 1], g_ref[last], we_ref[last], wn_ref[last])
@@ -277,12 +287,23 @@
         odd_ref[at] = jnp.where(odd, bottom, top).reshape(flat)
 
     copies[-1].wait()
-    sums = jnp.dot(lhs_ref[...], basis_ref[...], preferred_element_type=jnp.float32)
-    turn_blocks(z, sums, phase_ref, share_ref)
-    cos, sin = phase_of(phase_ref, z.blocks)
-    before = -coef * g[:, 0:1]
-    share_ref[:, :HALF] += before * cos
-    share_ref[:, HALF:] += before * sin
+
+    @pl.when(on_polar_band(z))
+    def _():
+        coef, sine = column_of(row_ref, EAST_COEF)[: z.own], column_of(row_ref, SINE)[: z.own]
+        new = widen(z, we + CORIOLIS * sine * wn) - coef * east_diff(widen(z, g))
+        tail = put_lane(new[:, z.ext - 128 :], 127, 0.0)
+        new = jnp.concatenate([new[:, : z.ext - 128], tail], axis=1)
+        forward_sums(z, new, basis_ref, phase_ref, lhs_ref, share_ref)
+        cos, sin = phase_of(phase_ref, z.blocks)
+        before = -coef * g[:, 0:1]
+        share_ref[:, :HALF] += before * cos
+        share_ref[:, HALF:] += before * sin
+
+    @pl.when(jnp.logical_not(on_polar_band(z)))
+    def _():
+        share_ref[...] = jnp.zeros_like(share_ref)
+
     spare = share_ref[:, SPARE:HALF]
     last = z.lon - 1
     edges = ((g, last - 1), (g, last), (we, last), (wn, last), (g, 0), (g, 1), (we, 0), (wn, 0))
@@ -294,7 +315,7 @@
 def north_forward(
     z, we_ref, wn_ref, g_ref, even_ref, odd_ref, row_ref, phase_ref, basis_ref, kept_ref, slot_ref, *rest
 ):
-    share_ref, north_ref, sends, (g_rows, lhs_ref) = rest[0], rest[1], rest[2:-2], rest[-2:]
+    ahead_ref, rest_ref, north_ref, chosen_ref, g_rows, lhs_ref, share_ref = rest
     edge, lev = 2 * z.lev, z.lev
     odd = lax.rem(lax.axis_index("lat"), 2) == 1
     below = jnp.where(odd, odd_ref[...], even_ref[...])
@@ -313,87 +334,137 @@
     ):
         we, wn = rim[edge : edge + lev], rim[edge + lev :]
         north_ref[at : at + lev] = wn - coef * diff - sine[at : at + lev] * we
-    store_blocks(z, widen(z, north_ref[...]), lhs_ref)
-    sums = jnp.dot(lhs_ref[...], basis_ref[...], preferred_element_type=jnp.float32)
-    turn_blocks(z, sums, phase_ref, share_ref)
     number = column_of(row_ref, NUMBER).astype(jnp.int32)
-    masked = coefficients(z, share_ref[...], number, kept_ref)
-    ordered = in_slot_order(z, masked, number, row_ref, slot_ref, z.half_axis)
-    for distance, send_ref in enumerate(sends):
-        place = lax.rem(lax.axis_index("lon") + distance, z.n_lon)
-        send_ref[...] = sector_part(z, ordered, place).reshape(send_ref.shape)
+    kept = look_up(number, kept_ref)
+
+    @pl.when(on_polar_band(z))
+    def _():
+        forward_sums(z, widen(z, north_ref[...]), basis_ref, phase_ref, lhs_ref, share_ref)
+        share_ref[:, SPARE:HALF] = put_lane(share_ref[:, SPARE:HALF], KMAX - SPARE, kept)
+        chosen = slot_order(z, number, row_ref, slot_ref)
+        ordered = reorder(chosen, share_ref[...])
+        ahead_ref[...] = ordered[: z.ahead]
+        rest_ref[...] = ordered[z.ahead : z.rows]
+        chosen_ref[...] = chosen
+
+    @pl.when(jnp.logical_not(on_polar_band(z)))
+    def _():
+        beyond = slice(z.own - z.ahead, z.rows - z.ahead)
+        ahead_ref[...] = jnp.zeros_like(ahead_ref)
+        rest_ref[...] = jnp.zeros_like(rest_ref)
+        chosen_ref[...] = jnp.zeros_like(chosen_ref)
+        rows = widen(z, north_ref[z.own :])
+        forward_sums(z, rows, basis_ref, phase_ref, lhs_ref, rest_ref, beyond)
+        rest_ref[beyond, SPARE:HALF] = put_lane(
+            rest_ref[beyond, SPARE:HALF], KMAX - SPARE, kept[z.own :]
+        )
 
 
 def east_inverse(
-    z, depth_ref, we_ref, wn_ref, g_ref, thick_ref, row_ref, phase_ref, kept_ref, slot_ref, *rest
+    z, depth_ref, we_ref, wn_ref, g_ref, thick_ref, row_ref, phase_ref, kept_ref, chosen_ref, *rest
 ):
     shares, rest = rest[: z.n_lon], rest[z.n_lon :]
-    basis_ref, final_ref, part_ref, keep_ref, send_ref, lhs_ref = rest
-    number = column_of(row_ref, NUMBER)[: z.own].astype(jnp.int32)
-    coef = coefficients(z, sum(ref[...] for ref in shares), number, kept_ref)
-    part = sector_part(z, coef, lax.axis_index("lon"))
-    for distance, ref in ((0, keep_ref), (z.half_axis, send_ref)):
-        ref[...] = in_slot_order(z, part, number, row_ref, slot_ref, distance).reshape(ref.shape)
-    blocks, before = inverse_blocks(z, coef, basis_ref, phase_ref, lhs_ref)
-    filtered = jnp.concatenate(blocks, axis=1)
-    tail = put_lane(filtered[:, z.ext - 128 :], 127, before)
-    filtered = jnp.concatenate([filtered[:, : z.ext - 128], tail], axis=1)
-
-    first = KMAX - SPARE
-    left, right = shares[1][:, SPARE:HALF], shares[-1][:, SPARE:HALF]
-    at_right = z.lon - (z.ext - 128)
-
-    def rimmed(ref, left_of, right_of):
-        x = widen(z, flat_rows(z, ref))
-        tail = x[:, z.ext - 128 :]
-        for n, lane in enumerate(right_of):
-            tail = put_lane(tail, at_right + n, right[:, first + lane : first + lane + 1])
-        for n, lane in enumerate(left_of):
-            tail = put_lane(tail, 127 - n, left[:, first + lane : first + lane + 1])
-        return jnp.concatenate([x[:, : z.ext - 128], tail], axis=1)
-
-    g = rimmed(g_ref, (1, 0), (4, 5))
-    we, wn = rimmed(we_ref, (2,), (6,)), rimmed(wn_ref, (3,), (7,))
+    basis_ref, final_ref, part_ref, keep_ref, send_ref, lhs_ref, rows_ref = rest
     coef, sine = column_of(row_ref, EAST_COEF)[: z.own], column_of(row_ref, SINE)[: z.own]
-    new = we - coef * east_diff(g) + CORIOLIS * sine * wn
-    final = jnp.where(column_of(row_ref, POLAR)[: z.own] > 0.0, filtered, new)
+
+    @pl.when(on_polar_band(z))
+    def _():
+        number = column_of(row_ref, NUMBER)[: z.own].astype(jnp.int32)
+        waves = coefficients(z, sum(ref[...] for ref in shares), look_up(number, kept_ref))
+        part = sector_part(z, waves, lax.axis_index("lon"))
+        ordered = reorder(chosen_ref[: z.own], part)
+        send_ref[...] = ordered[: z.helped].reshape(send_ref.shape)
+        keep_ref[...] = ordered[z.helped : 2 * z.helped].reshape(keep_ref.shape)
+        inverse_rows(z, waves, basis_ref, phase_ref, lhs_ref, rows_ref)
+        cos, sin = phase_of(phase_ref, z.blocks)
+        before = jnp.sum(waves[:, :HALF] * cos + waves[:, HALF:] * sin, axis=1, keepdims=True)
+        rows_ref[:, z.ext - 128 :] = put_lane(rows_ref[:, z.ext - 128 :], 127, before)
+
+    @pl.when(jnp.logical_not(on_polar_band(z)))
+    def _():
+        send_ref[...] = jnp.zeros_like(send_ref)
+        keep_ref[...] = jnp.zeros_like(keep_ref)
+        first = KMAX - SPARE
+        left, right = shares[1][:, SPARE:HALF], shares[-1][:, SPARE:HALF]
+        at_right = z.lon - (z.ext - 128)
+
+        def rimmed(ref, left_of, right_of):
+            x = widen(z, flat_rows(z, ref))
+            tail = x[:, z.ext - 128 :]
+            for n, lane in enumerate(right_of):
+                tail = put_lane(tail, at_right + n, right[:, first + lane : first + lane + 1])
+            for n, lane in enumerate(left_of):
+                tail = put_lane(tail, 127 - n, left[:, first + lane : first + lane + 1])
+            return jnp.concatenate([x[:, : z.ext - 128], tail], axis=1)
+
+        g = rimmed(g_ref, (1, 0), (4, 5))
+        we, wn = rimmed(we_ref, (2,), (6,)), rimmed(wn_ref, (3,), (7,))
+        rows_ref[...] = we - coef * east_diff(g) + CORIOLIS * sine * wn
+
+    final = rows_ref[...]
     final_ref[...] = final[:, : z.lon].reshape(final_ref.shape)
     change = depths(z, depth_ref, row_ref) * coef * east_diff(final)[:, : z.lon]
     part_ref[...] = flat_rows(z, thick_ref) - change
 
 
-def on_polar_band(z):
-    lat_index = lax.axis_index("lat")
-    return (lat_index < z.n_lat // 4) | (lat_index >= z.n_lat - z.n_lat // 4)
-
-
-def north_inverse(
-    z, depth_ref, north_ref, part_ref, row_ref, phase_ref, kept_ref, slot_ref, *rest
-):
-    shares, arrived, rest = rest[: z.n_lon], rest[z.n_lon : 2 * z.n_lon], rest[2 * z.n_lon :]
-    basis_ref, final_ref, thick_ref, column_ref, spectra_ref, lhs_ref = rest
-    number = column_of(row_ref, NUMBER).astype(jnp.int32)
-    coef = coefficients(z, sum(ref[...] for ref in shares), number, kept_ref)
+def send_spectra(z, east_ref, *rest):
+    shares, send_ref = rest[:-1], rest[-1]
+    kept = shares[0][:, KMAX : KMAX + 1]
+    coef = coefficients(z, sum(ref[...] for ref in shares), kept)
     part = sector_part(z, coef, lax.axis_index("lon"))
-    keep = in_slot_order(z, part, number, row_ref, slot_ref, 0).reshape(spectra_ref.shape)
-    spectra_ref[...] = jnp.where(on_polar_band(z), keep, sum(ref[...] for ref in arrived))
-    blocks, _ = inverse_blocks(z, coef, basis_ref, phase_ref, lhs_ref)
+    send_ref[0] = east_ref[...]
+    send_ref[1] = part[: z.helped].reshape(east_ref.shape)
+
+
+def north_inverse(z, depth_ref, north_ref, part_ref, row_ref, phase_ref, chosen_ref, *rest):
+    ahead, shares, rest = rest[: z.n_lon], rest[z.n_lon : 2 * z.n_lon], rest[2 * z.n_lon :]
+    basis_ref, final_ref, thick_ref, column_ref, keep_ref, lhs_ref, sums_ref, rows_ref = rest
+
+    @pl.when(on_polar_band(z))
+    def _():
+        sums_ref[: z.ahead] = sum(ref[...] for ref in ahead)
+        sums_ref[z.ahead : z.rows] = sum(ref[...] for ref in shares)
+        sums_ref[z.rows :] = jnp.zeros((sums_ref.shape[0] - z.rows, WIDE), jnp.float32)
+        sums = sums_ref[...]
+        kept = [ahead[0][:, KMAX : KMAX + 1], shares[0][:, KMAX : KMAX + 1]]
+        waves = coefficients(z, sums, pad_rows(jnp.concatenate(kept, axis=0), sums.shape[0]))
+        part = sector_part(z, waves, lax.axis_index("lon"))
+        keep_ref[...] = part[z.helped : 2 * z.helped].reshape(keep_ref.shape)
+        high = waves.astype(jnp.bfloat16)
+        low = (waves - high.astype(jnp.float32)).astype(jnp.bfloat16)
+        chosen = chosen_ref[...].astype(jnp.bfloat16)
+        waves = jnp.dot(chosen, high, preferred_element_type=jnp.float32) + jnp.dot(
+            chosen, low, preferred_element_type=jnp.float32
+        )
+        inverse_rows(z, waves, basis_ref, phase_ref, lhs_ref, rows_ref)
+        beyond = slice(z.own, z.rows)
+        polar = column_of(row_ref, POLAR)[beyond] > 0.0
+        rows_ref[beyond, : z.lon] = jnp.where(polar, rows_ref[beyond, : z.lon], north_ref[beyond])
+
+    @pl.when(jnp.logical_not(on_polar_band(z)))
+    def _():
+        keep_ref[...] = jnp.zeros_like(keep_ref)
+        beyond = slice(z.own, z.rows)
+        at = slice(z.own - z.ahead, z.rows - z.ahead)
+        waves = coefficients(z, sum(ref[at] for ref in shares), shares[0][at, KMAX : KMAX + 1])
+        inverse_rows(z, waves, basis_ref, phase_ref, lhs_ref, rows_ref, beyond)
+        polar = column_of(row_ref, POLAR)[beyond] > 0.0
+        rows_ref[beyond, : z.lon] = jnp.where(polar, rows_ref[beyond, : z.lon], north_ref[beyond])
+        rows_ref[: z.own, : z.lon] = north_ref[: z.own]
+
+    final = rows_ref[:, : z.lon]
+    final_ref[...] = final[: z.own].reshape(final_ref.shape)
+    scaled = final * column_of(row_ref, COSINE)
+    diff = (roll(scaled, -z.lev, 0) - roll(scaled, z.lev, 0))[: z.own]
     scale = depths(z, depth_ref, row_ref) * column_of(row_ref, NORTH_COEF)[: z.own]
-    for block, filtered in enumerate(blocks):
-        at = slice(block * z.inverse_block, min((block + 1) * z.inverse_block, z.lon))
-        filtered = filtered[:, : at.stop - at.start]
-        final = jnp.where(column_of(row_ref, POLAR) > 0.0, filtered, north_ref[:, at])
-        final_ref[:, :, at] = final[: z.own].reshape(z.lat, z.lev, at.stop - at.start)
-        scaled = final * column_of(row_ref, COSINE)
-        diff = (roll(scaled, -z.lev, 0) - roll(scaled, z.lev, 0))[: z.own]
-        thick = part_ref[:, at] - scale * diff
-        thick_ref[:, :, at] = thick.reshape(z.lat, z.lev, at.stop - at.start)
+    thick_ref[...] = (part_ref[...] - scale * diff).reshape(thick_ref.shape)
     column_ref[...] = sum(thick_ref[:, lev, :] for lev in range(z.lev))
 
 
-def join_spectra(z, keep_ref, arrived_ref, north_ref, spectra_ref):
-    spectra_ref[0] = jnp.where(on_polar_band(z), keep_ref[...], arrived_ref[...])
-    spectra_ref[1] = north_ref[...]
+def join_spectra(z, east_ref, north_ref, arrived_ref, spectra_ref):
+    polar = on_polar_band(z)
+    spectra_ref[0] = jnp.where(polar, east_ref[...], arrived_ref[0])
+    spectra_ref[1] = jnp.where(polar, north_ref[...], arrived_ref[1])
 
 
 def close(z, thick_ref, surface_ref, spectra_ref, *rest):
@@ -476,49 +547,56 @@
         pairs = [(i, i + 1) for i in range(start, z.n_lat - 1, 2)]
         met.append(lax.ppermute(rim, "lat", pairs + [(b, a) for a, b in pairs]))
 
-    north_share, north_new, *north_sends = call(
+    places = round_up(z.rows, 128)
+    north_ahead, north_rest, north_new, chosen = call(
         functools.partial(north_forward, z),
         10,
-        [(z.rows, WIDE), (z.rows, z.lon)] + [spec] * z.n_lon,
-        [pltpu.VMEM((z.rows, z.lon), jnp.float32), columns_lhs],
+        [(z.ahead, WIDE), (z.rows - z.ahead, WIDE), (z.rows, z.lon), (z.rows, places)],
+        [
+            pltpu.VMEM((z.rows, z.lon), jnp.float32),
+            columns_lhs,
+            pltpu.VMEM((z.rows, WIDE), jnp.float32),
+        ],
         0.2,
     )(wind_east, wind_north, geopot, *met, per_row, phase, forward, kept, slots)
-    north_shares = [north_share] + [shifted(north_share, "lon", s) for s in range(1, z.n_lon)]
-
-    polar_bands = [i for i in range(z.n_lat) if i < z.n_lat // 4 or i >= z.n_lat - z.n_lat // 4]
-    to_helper = [(i, (i + z.half_axis) % z.n_lat) for i in polar_bands]
-    north_arrived = []
-    for distance, send in enumerate(north_sends):
-        route = [
-            (a * z.n_lon + lon, b * z.n_lon + (lon + distance) % z.n_lon)
-            for a, b in to_helper
-            for lon in range(z.n_lon)
-        ]
-        north_arrived.append(lax.ppermute(send, ("lat", "lon"), route))
+    north_aheads, north_rests = (
+        [x] + [shifted(x, "lon", s) for s in range(1, z.n_lon)] for x in (north_ahead, north_rest)
+    )
 
     east_final, thick_part, east_keep, east_send = call(
         functools.partial(east_inverse, z),
         10 + z.n_lon,
         [field, (z.own, z.lon), spec, spec],
-        [waves_lhs],
+        [waves_lhs, pltpu.VMEM((z.own, z.ext), jnp.float32)],
         1,
         {0: pltpu.SMEM},
     )(
-        mean_depth, wind_east, wind_north, geopot, thickness, per_row, phase, kept, slots,
+        mean_depth, wind_east, wind_north, geopot, thickness, per_row, phase, kept, chosen,
         *east_shares, inverse,
     )
-    east_arrived = lax.ppermute(east_send, "lat", to_helper)
-
-    north_final, thick_new, column, north_spectra = call(
+
+    polar_bands = [i for i in range(z.n_lat) if i < z.n_lat // 4 or i >= z.n_lat - z.n_lat // 4]
+    (to_helper,) = call(
+        functools.partial(send_spectra, z), 1 + z.n_lon, [(2, *spec)], [], 0.1
+    )(east_send, *north_aheads)
+    arrived = lax.ppermute(
+        to_helper, "lat", [(i, (i + z.half_axis) % z.n_lat) for i in polar_bands]
+    )
+
+    north_final, thick_new, column, north_keep = call(
         functools.partial(north_inverse, z),
-        8 + 2 * z.n_lon,
+        7 + 2 * z.n_lon,
         [field, field, (z.lat, z.lon), spec],
-        [waves_lhs],
+        [
+            waves_lhs,
+            pltpu.VMEM((places, WIDE), jnp.float32),
+            pltpu.VMEM((z.rows, z.ext), jnp.float32),
+        ],
         2,
         {0: pltpu.SMEM},
     )(
-        mean_depth, north_new, thick_part, per_row, phase, kept, slots,
-        *north_shares, *north_arrived, inverse,
+        mean_depth, north_new, thick_part, per_row, phase, chosen,
+        *north_aheads, *north_rests, inverse,
     )
 
     deeper = [
@@ -526,7 +604,7 @@
         for distance in range(1, z.n_lev)
     ]
     (spectra,) = call(functools.partial(join_spectra, z), 3, [(2, *spec)], [], 4.2)(
-        east_keep, east_arrived, north_spectra
+        east_keep, north_keep, arrived
     )
     (geo_new,) = call(functools.partial(close, z), 3 + len(deeper), [field], [], 1)(
         thick_new, surface_geopot, spectra, *deeper

time: 47.1 us -> 45.3 us (0.962)
  the two profiles are of different devices: /device:TPU:9 before, /device:TPU:0 now
where the time goes in v2:
time: 45.3 us; the launch traced here: 45.1 us
  Pallas kernels  21.4 us (47%)
  waiting for transfers between devices  11.2 us (25%)
  starting transfers between devices  10.8 us (24%)
  local copies, waits for them, and re-layouts  1 us (2%)
  between operations  0.76 us (2%)
    ppermute x3, waiting for transfers between devices, shifted(): lax.ppermute(block, axis, [(i, (i + distance) % count) for i in range(cou...  5.97 us
    pallas_call x1, Pallas kernels, local(): call(functools.partial(east_forward, z), 6, [(z.own, WIDE), rims, rims] +...  5.63 us
    ppermute x3, starting transfers between devices, shifted(): lax.ppermute(block, axis, [(i, (i + distance) % count) for i in range(cou...  5.1 us
    pallas_call x1, Pallas kernels, local(): call(functools.partial(north_forward, z), 10, [(z.ahead, WIDE), (z.rows -...  4.7 us
    pallas_call x1, Pallas kernels, local(): call(functools.partial(north_inverse, z), 7 + 2 * z.n_lon, [field, field,...  4.55 us
    pallas_call x1, Pallas kernels, local(): call(functools.partial(east_inverse, z), 10 + z.n_lon, [field, (z.own, z....  4.11 us
    ppermute x1, starting transfers between devices, local(): lax.ppermute(to_helper, 'lat', [(i, (i + z.half_axis) % z.n_lat) for i in...  3.77 us
    ppermute x2, waiting for transfers between devices, local(): met.append(lax.ppermute(rim, 'lat', pairs + [(b, a) for a, b in pairs]))  3.43 us
  transfers between devices with their start and end apart: 7, of which 5 were waited for; matrix products, arithmetic and copies ran while one was open for 0% of the time, Pallas kernels for 32%

profile of v2, /device:TPU:0, one launch (start us, length us, event | category | flops | bytes accessed | tf_op | source)
XLA Modules:
  0.0 45.1 jit_solution(13611116850936423114)
XLA Ops:
  0.6 0.0 copy-start.2
  0.6 0.0 copy-start.3
  0.7 5.6 %shard_map.155 = (f32[180,768]{1,0:T(8,128)S(1)}, f32[8,1440]{1,0:T(8,128)S(1)}, f32[8,1440]{1,0:T(8,128)S(1)}, f32[90,2,1440]{2,1,0:T(2,128)S(1)}, f32[90,2,144...) custom-call(f32[90,2,1440]{2,1,0:T(2,128)} %bitcast.17, ...), custom_call_target="tpu_custom_call" | custom-call | flops 4600000000 | tf_op jit(solution)/shard_map/pallas_call | solution.py:534
  6.3 3.0 %collective-permute-start.2 = (f32[180,768]{1,0:T(8,128)S(1)}, f32[180,768]{1,0:T(8,128)S(1)}, u32[]{:S(2)}, u32[]{:S(2)}) collective-permute-start(f32[180,768]{1,0:T(8,128)S(1)} %get-tuple-element.35.rest_0_), channel_id=1, source_target_pairs={{0,2},{2,0},{1,3},{3,1},{4,6},{6,4},{5,7},{7,5},{8,10},{10,8},{9,1... | collective-permute-start | bytes 1658888 | tf_op jit(solution)/shard_map/ppermute | solution.py:501
  9.3 0.0 collective-permute-start
  9.3 0.7 %collective-permute-start.1 = (f32[8,1440]{1,0:T(8,128)S(1)}, f32[8,1440]{1,0:T(8,128)S(1)}, u32[]{:S(2)}, u32[]{:S(2)}) collective-permute-start(f32[8,1440]{1,0:T(8,128)S(1)} %get-tuple-element.32), channel_id=1, source_target_pairs={{4,8},{8,4},{5,9},{9,5},{6,10},{10,6},{7,11},{11,7},{20,24},{24,20... | collective-permute-start | bytes 138248 | tf_op jit(solution)/shard_map/ppermute | solution.py:548
  10.0 3.4 %collective-permute-done.even_ref = f32[8,1440]{1,0:T(8,128)S(1)} collective-permute-done((f32[8,1440]{1,0:T(8,128)S(1)}, f32[8,1440]{1,0:T(8,128)S(1)}, u32[]{:S(2)}, u32[]{:S(2)}) %collective-permute-start) | collective-permute-done | bytes 46112 | tf_op jit(solution)/shard_map/ppermute | solution.py:548
  13.4 0.0 collective-permute-done.1.odd_ref
  13.4 0.0 copy-done.2
  13.4 0.0 copy-done.3
  13.4 0.0 copy-start
  13.4 0.0 copy-start.1
  13.4 0.0 copy-start.4
  13.4 4.7 %shard_map.156 = (f32[96,768]{1,0:T(8,128)S(1)}, f32[88,768]{1,0:T(8,128)S(1)}, f32[184,1440]{1,0:T(8,128)S(1)}, f32[184,256]{1,0:T(8,128)S(1)}) custom-call(f32[90,2,1440]{2,1,0:T(2,128)S(1)} %get-tuple-element.26.we_ref, f32[90,2,1440]{2,1,0:T(2,128)S(1)} %get-tuple-element.27.wn_ref, f32[90,2,1440]{2,1,0:T(2,128)S(1)} %get-tuple-element.28.g_ref, ...), custom_call_target="tpu_custom_call" | custom-call | flops 230000000 | tf_op jit(solution)/shard_map/pallas_call | solution.py:551
  18.1 0.2 collective-permute-start.3
  18.3 1.9 %collective-permute-start.4 = (f32[88,768]{1,0:T(8,128)S(1)}, f32[88,768]{1,0:T(8,128)S(1)}, u32[]{:S(2)}, u32[]{:S(2)}) collective-permute-start(f32[88,768]{1,0:T(8,128)S(1)} %get-tuple-element.40.rest_2_), channel_id=1, source_target_pairs={{0,2},{2,0},{1,3},{3,1},{4,6},{6,4},{5,7},{7,5},{8,10},{10,8},{9,1... | collective-permute-start | bytes 811016 | tf_op jit(solution)/shard_map/ppermute | solution.py:501
  20.2 2.7 %collective-permute-done.2.rest_1_ = f32[180,768]{1,0:T(8,128)S(1)} collective-permute-done((f32[180,768]{1,0:T(8,128)S(1)}, f32[180,768]{1,0:T(8,128)S(1)}, u32[]{:S(2)}, u32[]{:S(2)}) %collective-permute-start.2) | collective-permute-done | bytes 552992 | tf_op jit(solution)/shard_map/ppermute | solution.py:501
  22.9 0.0 copy-done
  22.9 0.0 copy-done.1
  22.9 0.0 copy-done.4
  22.9 4.1 %shard_map.157 = (f32[90,2,1440]{2,1,0:T(2,128)}, f32[180,1440]{1,0:T(8,128)S(1)}, f32[45,2,360]{2,1,0:T(2,128)S(1)}, f32[45,2,360]{2,1,0:T(2,128)S(1)}) custom-call(f32[2]{0:T(128)S(1)} %copy-done.4, f32[90,2,1440]{2,1,0:T(2,128)S(1)} %get-tuple-element.26.we_ref, f32[90,2,1440]{2,1,0:T(2,128)S(1)} %get-tuple-element.27.wn_ref, ...), custom_call_target="tpu_custom_call" | custom-call | flops 1150000000 | tf_op jit(solution)/shard_map/pallas_call | solution.py:566
  27.0 2.2 %collective-permute-done.3.rest_1_ = f32[96,768]{1,0:T(8,128)S(1)} collective-permute-done((f32[96,768]{1,0:T(8,128)S(1)}, f32[96,768]{1,0:T(8,128)S(1)}, u32[]{:S(2)}, u32[]{:S(2)}) %collective-permute-start.3) | collective-permute-done | bytes 294944 | tf_op jit(solution)/shard_map/ppermute | solution.py:501
  29.3 0.1 shard_map.159
  29.4 3.8 %collective-permute-start.5 = (f32[2,45,2,360]{3,2,1,0:T(2,128)S(1)}, f32[2,45,2,360]{3,2,1,0:T(2,128)S(1)}, u32[]{:S(2)}, u32[]{:S(2)}) collective-permute-start(f32[2,45,2,360]{3,2,1,0:T(2,128)S(1)} %shard_map.159), channel_id=1, source_target_pairs={{0,8},{12,4},{1,9},{13,5},{2,10},{14,6},{3,11},{15,7},{16,24},{28,... | collective-permute-start | bytes 777608 | tf_op jit(solution)/shard_map/ppermute | solution.py:582
  33.1 1.1 %collective-permute-done.4.rest_3_ = f32[88,768]{1,0:T(8,128)S(1)} collective-permute-done((f32[88,768]{1,0:T(8,128)S(1)}, f32[88,768]{1,0:T(8,128)S(1)}, u32[]{:S(2)}, u32[]{:S(2)}) %collective-permute-start.4) | collective-permute-done | bytes 270368 | tf_op jit(solution)/shard_map/ppermute | solution.py:501
  34.2 4.5 %shard_map.158 = (f32[90,2,1440]{2,1,0:T(2,128)}, f32[90,2,1440]{2,1,0:T(2,128)}, f32[90,1440]{1,0:T(8,128)S(1)}, f32[45,2,360]{2,1,0:T(2,128)S(1)}) custom-call(f32[2]{0:T(128)S(1)} %copy-done.4, f32[184,1440]{1,0:T(8,128)S(1)} %get-tuple-element.37.north_ref, f32[180,1440]{1,0:T(8,128)S(1)} %get-tuple-element.38.part_ref, ...), custom_call_target="tpu_custom_call" | custom-call | flops 2300000000 | tf_op jit(solution)/shard_map/pallas_call | solution.py:586
  38.8 1.3 %collective-permute-start.6 = (f32[90,1440]{1,0:T(8,128)S(1)}, f32[90,1440]{1,0:T(8,128)S(1)}, u32[]{:S(2)}, u32[]{:S(2)}) collective-permute-start(f32[90,1440]{1,0:T(8,128)S(1)} %get-tuple-element.46), channel_id=1, source_target_pairs={{1,0},{3,2},{5,4},{7,6},{9,8},{11,10},{13,12},{15,14},{17,16},{19,... | collective-permute-start | bytes 1555208 | tf_op jit(solution)/shard_map/ppermute | solution.py:603
  40.0 0.0 collective-permute-done.5.arrived_ref
  40.1 0.0 copy-start.5
  40.1 0.0 copy-start.6
  40.1 0.8 %shard_map.160.spectra_ref = f32[2,45,2,360]{3,2,1,0:T(2,128)} custom-call(f32[45,2,360]{2,1,0:T(2,128)S(1)} %get-tuple-element.43.east_ref, f32[45,2,360]{2,1,0:T(2,128)S(1)} %get-tuple-element.44.north_ref, f32[2,45,2,360]{3,2,1,0:T(2,128)S(1)} %collective-permute-done.5.arrived_ref), custom_call_target="tpu_custom_call" | custom-call | flops 4830000128 | tf_op jit(solution)/shard_map/pallas_call | solution.py:606
  40.9 1.8 %collective-permute-done.6.rest_0_ = f32[90,1440]{1,0:T(8,128)S(1)} collective-permute-done((f32[90,1440]{1,0:T(8,128)S(1)}, f32[90,1440]{1,0:T(8,128)S(1)}, u32[]{:S(2)}, u32[]{:S(2)}) %collective-permute-start.6) | collective-permute-done | bytes 518432 | tf_op jit(solution)/shard_map/ppermute | solution.py:603
  42.6 0.0 copy-done.5
  42.6 0.0 copy-done.6
  42.7 0.0 copy-start.7
  42.7 1.0 %copy-done.7 = f32[2,45,2,360]{3,2,1,0:T(2,128)S(1)} copy-done((f32[2,45,2,360]{3,2,1,0:T(2,128)S(1)}, f32[2,45,2,360]{3,2,1,0:T(2,128)}, u32[]{:S(2)}) %copy-start.7) | copy-done | bytes 259224
  43.6 1.5 %shard_map.161 = f32[90,2,1440]{2,1,0:T(2,128)} custom-call(f32[90,2,1440]{2,1,0:T(2,128)S(1)} %copy-done.6, f32[90,1440]{1,0:T(8,128)S(1)} %copy-done.5, f32[2,45,2,360]{3,2,1,0:T(2,128)S(1)} %copy-done.7, f32[90,1440]{1,0:T(8,128)S(1)} %collective-permute-done.6.rest_0_), custom_call_target="tpu_custom_call" | custom-call | flops 1150000000 | tf_op jit(solution)/shard_map/pallas_call | solution.py:609
Async XLA Ops:
  0.6 12.8 %copy-start.2 = (s32[180]{0:T(256)S(1)}, s32[180]{0:T(256)}, u32[]{:S(2)}) copy-start(s32[180]{0:T(256)} %param.18) | copy-start | bytes 2164
  0.6 12.8 %copy-start.3 = (s32[180]{0:T(256)S(1)}, s32[180]{0:T(256)}, u32[]{:S(2)}) copy-start(s32[180]{0:T(256)} %param.19) | copy-start | bytes 2164
  6.3 16.6 %collective-permute-start.2 = (f32[180,768]{1,0:T(8,128)S(1)}, f32[180,768]{1,0:T(8,128)S(1)}, u32[]{:S(2)}, u32[]{:S(2)}) collective-permute-start(f32[180,768]{1,0:T(8,128)S(1)} %get-tuple-element.35.rest_0_), channel_id=1, source_target_pairs={{0,2},{2,0},{1,3},{3,1},{4,6},{6,4},{5,7},{7,5},{8,10},{10,8},{9,1... | collective-permute-start | bytes 1658888 | tf_op jit(solution)/shard_map/ppermute | solution.py:501
  9.3 4.1 %collective-permute-start = (f32[8,1440]{1,0:T(8,128)S(1)}, f32[8,1440]{1,0:T(8,128)S(1)}, u32[]{:S(2)}, u32[]{:S(2)}) collective-permute-start(f32[8,1440]{1,0:T(8,128)S(1)} %get-tuple-element.31), channel_id=1, source_target_pairs={{0,4},{8,12},{4,0},{12,8},{1,5},{9,13},{5,1},{13,9},{2,6},{10,14},... | collective-permute-start | bytes 138248 | tf_op jit(solution)/shard_map/ppermute | solution.py:548
  9.3 4.1 %collective-permute-start.1 = (f32[8,1440]{1,0:T(8,128)S(1)}, f32[8,1440]{1,0:T(8,128)S(1)}, u32[]{:S(2)}, u32[]{:S(2)}) collective-permute-start(f32[8,1440]{1,0:T(8,128)S(1)} %get-tuple-element.32), channel_id=1, source_target_pairs={{4,8},{8,4},{5,9},{9,5},{6,10},{10,6},{7,11},{11,7},{20,24},{24,20... | collective-permute-start | bytes 138248 | tf_op jit(solution)/shard_map/ppermute | solution.py:548
  13.4 9.5 %copy-start = (bf16[2304,768]{1,0:T(8,128)(2,1)S(1)}, bf16[2304,768]{1,0:T(8,128)(2,1)}, u32[]{:S(2)}) copy-start(bf16[2304,768]{1,0:T(8,128)(2,1)} %constant.9.clone.rest_2_.rest_4_) | copy-start | bytes 10616836
  13.4 9.5 %copy-start.1 = (f32[2,90,1440]{2,0,1:T(2,128)S(1)}, f32[2,90,1440]{2,0,1:T(2,128)}, u32[]{:S(2)}) copy-start(f32[2,90,1440]{2,0,1:T(2,128)} %param.14) | copy-start | bytes 3110404
  13.4 9.5 %copy-start.4 = (f32[2]{0:T(128)S(1)}, f32[2]{0:T(128)}, u32[]{:S(2)}) copy-start(f32[2]{0:T(128)} %depth_ref.3) | copy-start | bytes 28
  18.1 11.1 %collective-permute-start.3 = (f32[96,768]{1,0:T(8,128)S(1)}, f32[96,768]{1,0:T(8,128)S(1)}, u32[]{:S(2)}, u32[]{:S(2)}) collective-permute-start(f32[96,768]{1,0:T(8,128)S(1)} %get-tuple-element.39.rest_0_), channel_id=1, source_target_pairs={{0,2},{2,0},{1,3},{3,1},{4,6},{6,4},{5,7},{7,5},{8,10},{10,8},{9,1... | collective-permute-start | bytes 884744 | tf_op jit(solution)/shard_map/ppermute | solution.py:501
  18.3 15.9 %collective-permute-start.4 = (f32[88,768]{1,0:T(8,128)S(1)}, f32[88,768]{1,0:T(8,128)S(1)}, u32[]{:S(2)}, u32[]{:S(2)}) collective-permute-start(f32[88,768]{1,0:T(8,128)S(1)} %get-tuple-element.40.rest_2_), channel_id=1, source_target_pairs={{0,2},{2,0},{1,3},{3,1},{4,6},{6,4},{5,7},{7,5},{8,10},{10,8},{9,1... | collective-permute-start | bytes 811016 | tf_op jit(solution)/shard_map/ppermute | solution.py:501
  29.4 10.7 %collective-permute-start.5 = (f32[2,45,2,360]{3,2,1,0:T(2,128)S(1)}, f32[2,45,2,360]{3,2,1,0:T(2,128)S(1)}, u32[]{:S(2)}, u32[]{:S(2)}) collective-permute-start(f32[2,45,2,360]{3,2,1,0:T(2,128)S(1)} %shard_map.159), channel_id=1, source_target_pairs={{0,8},{12,4},{1,9},{13,5},{2,10},{14,6},{3,11},{15,7},{16,24},{28,... | collective-permute-start | bytes 777608 | tf_op jit(solution)/shard_map/ppermute | solution.py:582
  38.8 3.9 %collective-permute-start.6 = (f32[90,1440]{1,0:T(8,128)S(1)}, f32[90,1440]{1,0:T(8,128)S(1)}, u32[]{:S(2)}, u32[]{:S(2)}) collective-permute-start(f32[90,1440]{1,0:T(8,128)S(1)} %get-tuple-element.46), channel_id=1, source_target_pairs={{1,0},{3,2},{5,4},{7,6},{9,8},{11,10},{13,12},{15,14},{17,16},{19,... | collective-permute-start | bytes 1555208 | tf_op jit(solution)/shard_map/ppermute | solution.py:603
  40.1 2.6 %copy-start.5 = (f32[90,1440]{1,0:T(8,128)S(1)}, f32[90,1440]{1,0:T(8,128)}, u32[]{:S(2)}) copy-start(f32[90,1440]{1,0:T(8,128)} %surface_ref.1) | copy-start | bytes 1555204
  40.1 2.6 %copy-start.6 = (f32[90,2,1440]{2,1,0:T(2,128)S(1)}, f32[90,2,1440]{2,1,0:T(2,128)}, u32[]{:S(2)}) copy-start(f32[90,2,1440]{2,1,0:T(2,128)} %get-tuple-element.42.thick_ref) | copy-start | bytes 3110404
  42.7 1.0 %copy-start.7 = (f32[2,45,2,360]{3,2,1,0:T(2,128)S(1)}, f32[2,45,2,360]{3,2,1,0:T(2,128)}, u32[]{:S(2)}) copy-start(f32[2,45,2,360]{3,2,1,0:T(2,128)} %shard_map.160.spectra_ref) | copy-start | bytes 777604

commit v3 on v2

--- a/solution.py
+++ b/solution.py
@@ -47,7 +47,8 @@
         assert self.ext % self.inverse_block == 0
         self.spec_width = 2 * KMAX // self.n_lon
         self.helped = self.help * self.lev
-        self.ahead = round_up(self.helped, 8)
+        self.ahead = round_up(self.helped, 16)
+        self.first = min(round_up(self.own * 4 // 9, 8 * self.lev), self.own)
 
 
 def high_low(x):
@@ -113,10 +114,14 @@
     return (lat_index < z.n_lat // 4) | (lat_index >= z.n_lat - z.n_lat // 4)
 
 
+def split(x):
+    high = x.astype(jnp.bfloat16)
+    return high, (x - high.astype(jnp.float32)).astype(jnp.bfloat16)
+
+
 def store_split(lhs_ref, first_row, x):
     rows, width = x.shape
-    high = x.astype(jnp.bfloat16)
-    low = (x - high.astype(jnp.float32)).astype(jnp.bfloat16)
+    high, low = split(x)
     at = slice(first_row, first_row + rows)
     lhs_ref[at, :width] = high
     lhs_ref[at, width : 2 * width] = low
@@ -124,6 +129,8 @@
 
 
 def pad_rows(x, rows):
+    if x.shape[0] == rows:
+        return x
     return jnp.concatenate([x, jnp.zeros((rows - x.shape[0], x.shape[1]), x.dtype)], axis=0)
 
 
@@ -131,12 +138,16 @@
     return phase_ref[2 * n : 2 * n + 1], phase_ref[2 * n + 1 : 2 * n + 2]
 
 
-def forward_sums(z, x, basis_ref, phase_ref, lhs_ref, out_ref, at=slice(None)):
+def forward_sums(
+    z, x, basis_ref, phase_ref, lhs_ref, out_ref, at=slice(None), basis_here=None
+):
     count = round_up(x.shape[0], 16)
     for block in range(z.blocks):
         part = pad_rows(x[:, block * BLOCK : (block + 1) * BLOCK], count)
         store_split(lhs_ref, block * count, part)
     lhs = lhs_ref[: z.blocks * count]
+    if basis_here is not None:
+        basis_here()
     sums = jnp.dot(lhs, basis_ref[...], preferred_element_type=jnp.float32)
     real = imag = None
     for block in range(z.blocks):
@@ -225,13 +236,16 @@
 
 
 def reorder(chosen, values):
-    return lax.dot_general(
-        chosen,
-        values,
-        (((0,), (0,)), ((), ())),
-        precision=lax.Precision.HIGHEST,
-        preferred_element_type=jnp.float32,
-    )
+    high, low = (
+        lax.dot_general(
+            chosen.astype(jnp.bfloat16),
+            part,
+            (((0,), (0,)), ((), ())),
+            preferred_element_type=jnp.float32,
+        )
+        for part in split(values)
+    )
+    return high + low
 
 
 def sector_part(z, coef, place):
@@ -259,24 +273,74 @@
     ref[edge + z.lev :] = wn[z.own - z.lev :] if last else wn[: z.lev]
 
 
-def east_forward(
+def east_shares_of(
+    z, at, we_ref, wn_ref, g_ref, row_ref, phase_ref, basis_ref, share_ref, lhs_ref, basis_here=None
+):
+    inner = slice(at.start // z.lev, at.stop // z.lev)
+    g, we, wn = (ref[inner].reshape(at.stop - at.start, z.lon) for ref in (g_ref, we_ref, wn_ref))
+
+    @pl.when(on_polar_band(z))
+    def _():
+        coef, sine = column_of(row_ref, EAST_COEF)[at], column_of(row_ref, SINE)[at]
+        new = widen(z, we + CORIOLIS * sine * wn) - coef * east_diff(widen(z, g))
+        tail = put_lane(new[:, z.ext - 128 :], 127, 0.0)
+        new = jnp.concatenate([new[:, : z.ext - 128], tail], axis=1)
+        forward_sums(z, new, basis_ref, phase_ref, lhs_ref, share_ref, basis_here=basis_here)
+        cos, sin = phase_of(phase_ref, z.blocks)
+        before = -coef * g[:, 0:1]
+        share_ref[:, :HALF] += before * cos
+        share_ref[:, HALF:] += before * sin
+
+    @pl.when(jnp.logical_not(on_polar_band(z)))
+    def _():
+        if basis_here is not None:
+            basis_here()
+        share_ref[...] = jnp.zeros_like(share_ref)
+
+    last = z.lon - 1
+    spare = share_ref[:, SPARE:HALF]
+    edges = ((g, last - 1), (g, last), (we, last), (wn, last), (g, 0), (g, 1), (we, 0), (wn, 0))
+    for n, (x, column) in enumerate(edges):
+        spare = put_lane(spare, KMAX - SPARE + n, x[:, column : column + 1])
+    share_ref[:, SPARE:HALF] = spare
+
+
+def east_first(
     z, we_hbm, wn_hbm, g_hbm, row_hbm, phase_hbm, basis_hbm,
     share_ref, even_ref, odd_ref, we_ref, wn_ref, g_ref, row_ref, phase_ref, basis_ref, lhs_ref, sems,
 ):
-    pairs = (
-        (row_hbm.at[lax.axis_index("lat")], row_ref),
-        (phase_hbm.at[lax.axis_index("lon")], phase_ref),
-        (g_hbm, g_ref),
-        (we_hbm, we_ref),
-        (wn_hbm, wn_ref),
-        (basis_hbm, basis_ref),
-    )
-    copies = [pltpu.make_async_copy(*pair, sems.at[n]) for n, pair in enumerate(pairs)]
-    for copy in copies:
+    fields = ((g_hbm, g_ref), (we_hbm, we_ref), (wn_hbm, wn_ref))
+    cut, rim = z.first // z.lev, z.lat - 2
+
+    def copies(first_sem, pairs):
+        return [pltpu.make_async_copy(*pair, sems.at[first_sem + n]) for n, pair in enumerate(pairs)]
+
+    tables = copies(
+        0,
+        (
+            (row_hbm.at[lax.axis_index("lat")], row_ref),
+            (phase_hbm.at[lax.axis_index("lon")], phase_ref),
+        ),
+    )
+    first = copies(2, [(a.at[:cut], b.at[:cut]) for a, b in fields])
+    basis = copies(5, [(basis_hbm, basis_ref)])
+    edge = copies(6, [(a.at[rim:], b.at[rim:]) for a, b in fields])
+    between = copies(9, [(a.at[cut:rim], b.at[cut:rim]) for a, b in fields])
+    for copy in first + tables + basis + edge:
         copy.start()
-    for copy in copies[:-1]:
+    for copy in first + tables:
         copy.wait()
-    g, we, wn = flat_rows(z, g_ref), flat_rows(z, we_ref), flat_rows(z, wn_ref)
+
+    def basis_here():
+        for copy in basis + edge:
+            copy.wait()
+        for copy in between:
+            copy.start()
+
+    east_shares_of(
+        z, slice(0, z.first), we_ref, wn_ref, g_ref, row_ref, phase_ref, basis_ref, share_ref, lhs_ref,
+        basis_here,
+    )
     odd = lax.rem(lax.axis_index("lat"), 2) == 1
     last, flat = z.lat - 1, (z.lev, z.lon)
     far = (g_ref[last - 1], g_ref[last], we_ref[last], wn_ref[last])
@@ -285,31 +349,8 @@
         at = slice(n * z.lev, (n + 1) * z.lev)
         even_ref[at] = jnp.where(odd, top, bottom).reshape(flat)
         odd_ref[at] = jnp.where(odd, bottom, top).reshape(flat)
-
-    copies[-1].wait()
-
-    @pl.when(on_polar_band(z))
-    def _():
-        coef, sine = column_of(row_ref, EAST_COEF)[: z.own], column_of(row_ref, SINE)[: z.own]
-        new = widen(z, we + CORIOLIS * sine * wn) - coef * east_diff(widen(z, g))
-        tail = put_lane(new[:, z.ext - 128 :], 127, 0.0)
-        new = jnp.concatenate([new[:, : z.ext - 128], tail], axis=1)
-        forward_sums(z, new, basis_ref, phase_ref, lhs_ref, share_ref)
-        cos, sin = phase_of(phase_ref, z.blocks)
-        before = -coef * g[:, 0:1]
-        share_ref[:, :HALF] += before * cos
-        share_ref[:, HALF:] += before * sin
-
-    @pl.when(jnp.logical_not(on_polar_band(z)))
-    def _():
-        share_ref[...] = jnp.zeros_like(share_ref)
-
-    spare = share_ref[:, SPARE:HALF]
-    last = z.lon - 1
-    edges = ((g, last - 1), (g, last), (we, last), (wn, last), (g, 0), (g, 1), (we, 0), (wn, 0))
-    for n, (x, column) in enumerate(edges):
-        spare = put_lane(spare, KMAX - SPARE + n, x[:, column : column + 1])
-    share_ref[:, SPARE:HALF] = spare
+    for copy in between:
+        copy.wait()
 
 
 def north_forward(
@@ -360,17 +401,25 @@
         )
 
 
+def arrival(arrived_ref, out_ref):
+    out_ref[...] = arrived_ref[:8, :128]
+
+
 def east_inverse(
-    z, depth_ref, we_ref, wn_ref, g_ref, thick_ref, row_ref, phase_ref, kept_ref, chosen_ref, *rest
+    z, depth_ref, we_ref, wn_ref, g_ref, thick_ref, row_ref, phase_ref, kept_ref, chosen_ref, first_here,
+    *rest,
 ):
-    shares, rest = rest[: z.n_lon], rest[z.n_lon :]
-    basis_ref, final_ref, part_ref, keep_ref, send_ref, lhs_ref, rows_ref = rest
+    del first_here
+    firsts, seconds, rest = rest[: z.n_lon], rest[z.n_lon : 2 * z.n_lon], rest[2 * z.n_lon :]
+    basis_ref, final_ref, part_ref, keep_ref, send_ref, lhs_ref, rows_ref, sums_ref = rest
     coef, sine = column_of(row_ref, EAST_COEF)[: z.own], column_of(row_ref, SINE)[: z.own]
 
     @pl.when(on_polar_band(z))
     def _():
         number = column_of(row_ref, NUMBER)[: z.own].astype(jnp.int32)
-        waves = coefficients(z, sum(ref[...] for ref in shares), look_up(number, kept_ref))
+        sums_ref[: z.first] = sum(ref[...] for ref in firsts)
+        sums_ref[z.first :] = sum(ref[...] for ref in seconds)
+        waves = coefficients(z, sums_ref[...], look_up(number, kept_ref))
         part = sector_part(z, waves, lax.axis_index("lon"))
         ordered = reorder(chosen_ref[: z.own], part)
         send_ref[...] = ordered[: z.helped].reshape(send_ref.shape)
@@ -385,7 +434,10 @@
         send_ref[...] = jnp.zeros_like(send_ref)
         keep_ref[...] = jnp.zeros_like(keep_ref)
         first = KMAX - SPARE
-        left, right = shares[1][:, SPARE:HALF], shares[-1][:, SPARE:HALF]
+        left, right = (
+            jnp.concatenate([firsts[n][:, SPARE:HALF], seconds[n][:, SPARE:HALF]], axis=0)
+            for n in (1, -1)
+        )
         at_right = z.lon - (z.ext - 128)
 
         def rimmed(ref, left_of, right_of):
@@ -416,27 +468,41 @@
     send_ref[1] = part[: z.helped].reshape(east_ref.shape)
 
 
-def north_inverse(z, depth_ref, north_ref, part_ref, row_ref, phase_ref, chosen_ref, *rest):
+def ahead_inverse(z, phase_ref, *rest):
+    shares, (basis_ref, high_ref, low_ref, lhs_ref, rows_ref) = rest[: z.n_lon], rest[z.n_lon :]
+
+    @pl.when(on_polar_band(z))
+    def _():
+        kept = shares[0][:, KMAX : KMAX + 1]
+        waves = coefficients(z, sum(ref[...] for ref in shares), kept)
+        inverse_rows(z, waves, basis_ref, phase_ref, lhs_ref, rows_ref)
+        high_ref[...], low_ref[...] = split(rows_ref[...])
+
+
+def north_inverse(
+    z, depth_ref, north_ref, part_ref, row_ref, phase_ref, chosen_ref, high_ahead, low_ahead, *rest
+):
     ahead, shares, rest = rest[: z.n_lon], rest[z.n_lon : 2 * z.n_lon], rest[2 * z.n_lon :]
-    basis_ref, final_ref, thick_ref, column_ref, keep_ref, lhs_ref, sums_ref, rows_ref = rest
+    basis_ref, final_ref, thick_ref, column_ref, keep_ref, lhs_ref, rows_ref, high_ref, low_ref = rest
 
     @pl.when(on_polar_band(z))
     def _():
-        sums_ref[: z.ahead] = sum(ref[...] for ref in ahead)
-        sums_ref[z.ahead : z.rows] = sum(ref[...] for ref in shares)
-        sums_ref[z.rows :] = jnp.zeros((sums_ref.shape[0] - z.rows, WIDE), jnp.float32)
-        sums = sums_ref[...]
-        kept = [ahead[0][:, KMAX : KMAX + 1], shares[0][:, KMAX : KMAX + 1]]
-        waves = coefficients(z, sums, pad_rows(jnp.concatenate(kept, axis=0), sums.shape[0]))
+        more = z.ahead - 8
+        kept = [ahead[0][more:, KMAX : KMAX + 1], shares[0][:, KMAX : KMAX + 1]]
+        sums = [sum(ref[more:] for ref in ahead), sum(ref[...] for ref in shares)]
+        waves = coefficients(z, jnp.concatenate(sums, axis=0), jnp.concatenate(kept, axis=0))
         part = sector_part(z, waves, lax.axis_index("lon"))
-        keep_ref[...] = part[z.helped : 2 * z.helped].reshape(keep_ref.shape)
-        high = waves.astype(jnp.bfloat16)
-        low = (waves - high.astype(jnp.float32)).astype(jnp.bfloat16)
+        first = z.helped - more
+        keep_ref[...] = part[first : first + z.helped].reshape(keep_ref.shape)
+        inverse_rows(z, waves[8:], basis_ref, phase_ref, lhs_ref, rows_ref, slice(z.rows - z.ahead))
+        count = high_ref.shape[0] - z.ahead
+        rest_high, rest_low = split(pad_rows(rows_ref[: z.rows - z.ahead], count))
+        high_ref[: z.ahead], low_ref[: z.ahead] = high_ahead[...], low_ahead[...]
+        high_ref[z.ahead :], low_ref[z.ahead :] = rest_high, rest_low
         chosen = chosen_ref[...].astype(jnp.bfloat16)
-        waves = jnp.dot(chosen, high, preferred_element_type=jnp.float32) + jnp.dot(
-            chosen, low, preferred_element_type=jnp.float32
-        )
-        inverse_rows(z, waves, basis_ref, phase_ref, lhs_ref, rows_ref)
+        rows_ref[...] = jnp.dot(
+            chosen, high_ref[...], preferred_element_type=jnp.float32
+        ) + jnp.dot(chosen, low_ref[...], preferred_element_type=jnp.float32)
         beyond = slice(z.own, z.rows)
         polar = column_of(row_ref, POLAR)[beyond] > 0.0
         rows_ref[beyond, : z.lon] = jnp.where(polar, rows_ref[beyond, : z.lon], north_ref[beyond])
@@ -461,22 +527,35 @@
     column_ref[...] = sum(thick_ref[:, lev, :] for lev in range(z.lev))
 
 
-def join_spectra(z, east_ref, north_ref, arrived_ref, spectra_ref):
+def store_results(z, east_keep, north_keep, arrived_ref, surface_ref, *rest):
+    fields, outs = rest[:2], rest[2:4]
+    spectra_ref, geo_ref, sems = rest[4:]
+    copies = [
+        pltpu.make_async_copy(*pair, sems.at[n])
+        for n, pair in enumerate(zip(fields, outs, strict=True))
+    ]
+    for copy in copies:
+        copy.start()
+    column = None
+    for lev in reversed(range(z.lev)):
+        one = fields[1][:, lev, :]
+        column = one if column is None else column + one
+        geo_ref[:, lev, :] = surface_ref[...] + GRAVITY * column
     polar = on_polar_band(z)
-    spectra_ref[0] = jnp.where(polar, east_ref[...], arrived_ref[0])
-    spectra_ref[1] = jnp.where(polar, north_ref[...], arrived_ref[1])
-
-
-def close(z, thick_ref, surface_ref, spectra_ref, *rest):
-    del spectra_ref
+    spectra_ref[0] = jnp.where(polar, east_keep[...], arrived_ref[0])
+    spectra_ref[1] = jnp.where(polar, north_keep[...], arrived_ref[1])
+    for copy in copies:
+        copy.wait()
+
+
+def add_deeper(z, own_ref, *rest):
     deeper, geo_ref = rest[:-1], rest[-1]
-    column = sum(ref[...] for ref in deeper) if deeper else 0.0
-    for lev in reversed(range(z.lev)):
-        column = column + thick_ref[:, lev, :]
-        geo_ref[:, lev, :] = surface_ref[...] + GRAVITY * column
-
-
-def call(kernel, n_in, out_shape, scratch, micros, spaces=None, vmem=24):
+    deeper = GRAVITY * sum(ref[...] for ref in deeper)
+    for lev in range(z.lev):
+        geo_ref[:, lev, :] = own_ref[:, lev, :] + deeper
+
+
+def call(kernel, n_in, out_shape, scratch, micros, spaces=None, in_hbm=0, vmem=24):
     vmem_spec = pl.BlockSpec(memory_space=pltpu.VMEM)
     spaces = spaces or {}
     return pl.pallas_call(
@@ -484,7 +563,8 @@
         in_specs=[
             pl.BlockSpec(memory_space=spaces[n]) if n in spaces else vmem_spec for n in range(n_in)
         ],
-        out_specs=[vmem_spec] * len(out_shape),
+        out_specs=[pl.BlockSpec(memory_space=pltpu.HBM)] * in_hbm
+        + [vmem_spec] * (len(out_shape) - in_hbm),
         out_shape=[
             jax.ShapeDtypeStruct(s, jnp.float32) if isinstance(s, tuple) else s for s in out_shape
         ],
@@ -524,24 +604,33 @@
     waves_lhs = pltpu.VMEM((z.ext // z.inverse_block * z.mm_rows, 3 * WIDE), jnp.bfloat16)
 
     row_shape, phase_shape = per_row.shape[1:], phase.shape[1:]
-    in_hbm = [
+    pinned = [
         pltpu.with_memory_space_constraint(x, pltpu.HBM)
         for x in (wind_east, wind_north, geopot, per_row, phase, forward)
     ]
     columns_lhs = pltpu.VMEM((z.blocks * z.mm_rows, 3 * BLOCK), jnp.bfloat16)
     waves_lhs = pltpu.VMEM((z.ext // z.inverse_block * z.mm_rows, 3 * WIDE), jnp.bfloat16)
 
-    east_share, to_even, to_odd, wind_east, wind_north, geopot, per_row, phase, forward = call(
-        functools.partial(east_forward, z),
+    share_first, to_even, to_odd, wind_east, wind_north, geopot, per_row, phase, forward = call(
+        functools.partial(east_first, z),
         6,
-        [(z.own, WIDE), rims, rims]
-        + [field, field, field, row_shape, phase_shape]
-        + [jax.ShapeDtypeStruct(forward.shape, forward.dtype)],
-        [columns_lhs, pltpu.SemaphoreType.DMA((6,))],
-        4,
+        [(z.first, WIDE), rims, rims]
+        + [pltpu.VMEM(s, jnp.float32) for s in (field, field, field, row_shape, phase_shape)]
+        + [pltpu.VMEM(forward.shape, forward.dtype)],
+        [columns_lhs, pltpu.SemaphoreType.DMA((12,))],
+        1,
         {n: pltpu.HBM for n in range(6)},
-    )(*in_hbm)
-    east_shares = [east_share] + [shifted(east_share, "lon", s) for s in range(1, z.n_lon)]
+    )(*pinned)
+    (share_second,) = call(
+        functools.partial(east_shares_of, z, slice(z.first, z.own)),
+        6,
+        [(z.own - z.first, WIDE)],
+        [columns_lhs],
+        0.18,
+    )(wind_east, wind_north, geopot, per_row, phase, forward)
+    east_firsts, east_seconds = (
+        [x] + [shifted(x, "lon", s) for s in range(1, z.n_lon)] for x in (share_first, share_second)
+    )
     met = []
     for start, rim in enumerate((to_even, to_odd)):
         pairs = [(i, i + 1) for i in range(start, z.n_lat - 1, 2)]
@@ -557,25 +646,38 @@
             columns_lhs,
             pltpu.VMEM((z.rows, WIDE), jnp.float32),
         ],
-        0.2,
-    )(wind_east, wind_north, geopot, *met, per_row, phase, forward, kept, slots)
-    north_aheads, north_rests = (
-        [x] + [shifted(x, "lon", s) for s in range(1, z.n_lon)] for x in (north_ahead, north_rest)
-    )
-
+        0.8,
+    )(
+        wind_east, wind_north, geopot, *met, per_row, phase, forward, kept, slots
+    )
+    north_rests = [north_rest] + [shifted(north_rest, "lon", s) for s in range(1, z.n_lon)]
+    polar_bands = [i for i in range(z.n_lat) if i < z.n_lat // 4 or i >= z.n_lat - z.n_lat // 4]
+    north_aheads = [north_ahead]
+    for distance in range(1, z.n_lon):
+        route = [
+            (band * z.n_lon + lon, band * z.n_lon + (lon + distance) % z.n_lon)
+            for band in polar_bands
+            for lon in range(z.n_lon)
+        ]
+        north_aheads.append(lax.ppermute(north_ahead, ("lat", "lon"), route))
+
+    (first_here,) = call(arrival, 1, [(8, 128)], [], 0.95)(east_firsts[1])
     east_final, thick_part, east_keep, east_send = call(
         functools.partial(east_inverse, z),
-        10 + z.n_lon,
+        11 + 2 * z.n_lon,
         [field, (z.own, z.lon), spec, spec],
-        [waves_lhs, pltpu.VMEM((z.own, z.ext), jnp.float32)],
+        [
+            waves_lhs,
+            pltpu.VMEM((z.own, z.ext), jnp.float32),
+            pltpu.VMEM((z.own, WIDE), jnp.float32),
+        ],
         1,
         {0: pltpu.SMEM},
     )(
         mean_depth, wind_east, wind_north, geopot, thickness, per_row, phase, kept, chosen,
-        *east_shares, inverse,
-    )
-
-    polar_bands = [i for i in range(z.n_lat) if i < z.n_lat // 4 or i >= z.n_lat - z.n_lat // 4]
+        first_here, *east_firsts, *east_seconds, inverse,
+    )
+
     (to_helper,) = call(
         functools.partial(send_spectra, z), 1 + z.n_lon, [(2, *spec)], [], 0.1
     )(east_send, *north_aheads)
@@ -583,19 +685,25 @@
         to_helper, "lat", [(i, (i + z.half_axis) % z.n_lat) for i in polar_bands]
     )
 
+    ahead_rows = jax.ShapeDtypeStruct((z.ahead, z.ext), jnp.bfloat16)
+    ahead_high, ahead_low = call(
+        functools.partial(ahead_inverse, z),
+        2 + z.n_lon,
+        [ahead_rows] * 2,
+        [waves_lhs, pltpu.VMEM((z.ahead, z.ext), jnp.float32)],
+        0.5,
+    )(phase, *north_aheads, inverse)
+
     north_final, thick_new, column, north_keep = call(
         functools.partial(north_inverse, z),
-        7 + 2 * z.n_lon,
-        [field, field, (z.lat, z.lon), spec],
-        [
-            waves_lhs,
-            pltpu.VMEM((places, WIDE), jnp.float32),
-            pltpu.VMEM((z.rows, z.ext), jnp.float32),
-        ],
+        9 + 2 * z.n_lon,
+        [pltpu.VMEM(field, jnp.float32)] * 2 + [(z.lat, z.lon), spec],
+        [waves_lhs, pltpu.VMEM((z.rows, z.ext), jnp.float32)]
+        + [pltpu.VMEM((places, z.ext), jnp.bfloat16)] * 2,
         2,
         {0: pltpu.SMEM},
     )(
-        mean_depth, north_new, thick_part, per_row, phase, chosen,
+        mean_depth, north_new, thick_part, per_row, phase, chosen, ahead_high, ahead_low,
         *north_aheads, *north_rests, inverse,
     )
 
@@ -603,13 +711,18 @@
         lax.ppermute(column, "lev", [(i, i - distance) for i in range(distance, z.n_lev)])
         for distance in range(1, z.n_lev)
     ]
-    (spectra,) = call(functools.partial(join_spectra, z), 3, [(2, *spec)], [], 4.2)(
-        east_keep, north_keep, arrived
-    )
-    (geo_new,) = call(functools.partial(close, z), 3 + len(deeper), [field], [], 1)(
-        thick_new, surface_geopot, spectra, *deeper
-    )
-    return tuple(level_inside(x) for x in (east_final, north_final, thick_new, geo_new, spectra))
+    north_final, thick_out, spectra, geo_own = call(
+        functools.partial(store_results, z),
+        6,
+        [pltpu.HBM(field, jnp.float32)] * 2 + [(2, *spec), pltpu.VMEM(field, jnp.float32)],
+        [pltpu.SemaphoreType.DMA((2,))],
+        5,
+        in_hbm=2,
+    )(east_keep, north_keep, arrived, surface_geopot, north_final, thick_new)
+    (geo_new,) = call(functools.partial(add_deeper, z), 1 + len(deeper), [field], [], 1)(
+        geo_own, *deeper
+    )
+    return tuple(level_inside(x) for x in (east_final, north_final, thick_out, geo_new, spectra))
 
 
 def solution(mesh):

time: 45.3 us -> 41.3 us (0.912)
  waiting for transfers between devices: 11.2 us -> 5.95 us
  starting transfers between devices: 10.8 us -> 13 us
  local copies, waits for them, and re-layouts: 1 us -> 0.04 us
    ppermute x2, waiting for transfers between devices: 3.43 us -> 0.01 us  [local(): met.append(lax.ppermute(rim, 'lat', pairs + [(b, a) for a, b in pairs]))]
    ppermute x0 -> x1, starting transfers between devices: none -> 3.4 us  [local(): north_aheads.append(lax.ppermute(north_ahead, ('lat', 'lon'), route))]
    ppermute x3, waiting for transfers between devices: 5.97 us -> 3 us  [shifted(): lax.ppermute(block, axis, [(i, (i + distance) % count) for i in range(cou...]
    ppermute x0 -> x1, waiting for transfers between devices: none -> 2.45 us  [local(): north_aheads.append(lax.ppermute(north_ahead, ('lat', 'lon'), route))]
    ppermute x1, starting transfers between devices: 3.77 us -> 2.07 us  [local(): lax.ppermute(to_helper, 'lat', [(i, (i + z.half_axis) % z.n_lat) for i in...]
    ppermute x2, starting transfers between devices: 0.65 us -> 2.05 us  [local(): met.append(lax.ppermute(rim, 'lat', pairs + [(b, a) for a, b in pairs]))]
    ppermute x1, waiting for transfers between devices: 1.8 us -> 0.49 us  [local(): lax.ppermute(column, 'lev', [(i, i - distance) for i in range(distance, z...]
    pallas_call x1, Pallas kernels: 4.7 us -> 3.52 us  [local(): call(functools.partial(north_forward, z), 10, [(z.ahead, WIDE), (z.rows -...]
  transfers between devices with their start and end apart: 7 -> 8, of which waited for: 5 -> 4; matrix products, arithmetic and copies ran while one was open for 0% -> 0% of each run, Pallas kernels for 32% -> 39%
where the time goes in v3:
time: 41.3 us; the launch traced here: 40.9 us
  Pallas kernels  21.1 us (51%)
  starting transfers between devices  13 us (31%)
  waiting for transfers between devices  5.95 us (14%)
  between operations  0.79 us (2%)
    ppermute x3, starting transfers between devices, shifted(): lax.ppermute(block, axis, [(i, (i + distance) % count) for i in range(cou...  4.21 us
    pallas_call x1, Pallas kernels, local(): call(functools.partial(east_inverse, z), 11 + 2 * z.n_lon, [field, (z.own...  3.86 us
    pallas_call x1, Pallas kernels, local(): call(functools.partial(north_forward, z), 10, [(z.ahead, WIDE), (z.rows -...  3.52 us
    pallas_call x1, Pallas kernels, local(): call(functools.partial(east_first, z), 6, [(z.first, WIDE), rims, rims] +...  3.48 us
    ppermute x1, starting transfers between devices, local(): north_aheads.append(lax.ppermute(north_ahead, ('lat', 'lon'), route))  3.4 us
    pallas_call x1, Pallas kernels, local(): call(functools.partial(north_inverse, z), 9 + 2 * z.n_lon, [pltpu.VMEM(fi...  3.31 us
    ppermute x3, waiting for transfers between devices, shifted(): lax.ppermute(block, axis, [(i, (i + distance) % count) for i in range(cou...  3 us
    ppermute x1, waiting for transfers between devices, local(): north_aheads.append(lax.ppermute(north_ahead, ('lat', 'lon'), route))  2.45 us
  transfers between devices with their start and end apart: 8, of which 4 were waited for; matrix products, arithmetic and copies ran while one was open for 0% of the time, Pallas kernels for 39%

profile of v3, /device:TPU:0, one launch (start us, length us, event | category | flops | bytes accessed | tf_op | source)
XLA Modules:
  0.0 40.9 jit_solution(2831230705341084284)
XLA Ops:
  0.6 3.5 %shard_map.155 = (f32[80,768]{1,0:T(8,128)S(1)}, f32[8,1440]{1,0:T(8,128)S(1)}, f32[8,1440]{1,0:T(8,128)S(1)}, f32[90,2,1440]{2,1,0:T(2,128)S(1)}, f32[90,2,1440...) custom-call(f32[90,2,1440]{2,1,0:T(2,128)} %bitcast.15, ...), custom_call_target="tpu_custom_call" | custom-call | flops 1150000000 | tf_op jit(solution)/shard_map/pallas_call | solution.py:614
  4.1 3.0 %collective-permute-start.2 = (f32[80,768]{1,0:T(8,128)S(1)}, f32[80,768]{1,0:T(8,128)S(1)}, u32[]{:S(2)}, u32[]{:S(2)}) collective-permute-start(f32[80,768]{1,0:T(8,128)S(1)} %get-tuple-element.41.rest_0_), channel_id=1, source_target_pairs={{0,2},{2,0},{1,3},{3,1},{4,6},{6,4},{5,7},{7,5},{8,10},{10,8},{9,1... | collective-permute-start | bytes 737288 | tf_op jit(solution)/shard_map/ppermute | solution.py:581
  7.1 1.4 %collective-permute-start = (f32[8,1440]{1,0:T(8,128)S(1)}, f32[8,1440]{1,0:T(8,128)S(1)}, u32[]{:S(2)}, u32[]{:S(2)}) collective-permute-start(f32[8,1440]{1,0:T(8,128)S(1)} %get-tuple-element.37), channel_id=1, source_target_pairs={{0,4},{8,12},{4,0},{12,8},{1,5},{9,13},{5,1},{13,9},{2,6},{10,14},... | collective-permute-start | bytes 138248 | tf_op jit(solution)/shard_map/ppermute | solution.py:637
  8.5 0.7 %collective-permute-start.1 = (f32[8,1440]{1,0:T(8,128)S(1)}, f32[8,1440]{1,0:T(8,128)S(1)}, u32[]{:S(2)}, u32[]{:S(2)}) collective-permute-start(f32[8,1440]{1,0:T(8,128)S(1)} %get-tuple-element.38), channel_id=1, source_target_pairs={{4,8},{8,4},{5,9},{9,5},{6,10},{10,6},{7,11},{11,7},{20,24},{24,20... | collective-permute-start | bytes 138248 | tf_op jit(solution)/shard_map/ppermute | solution.py:637
  9.2 0.0 copy-start.2
  9.2 0.0 copy-start.3
  9.2 2.1 %shard_map.158.rest_2_ = f32[100,768]{1,0:T(8,128)S(1)} custom-call(f32[90,2,1440]{2,1,0:T(2,128)S(1)} %get-tuple-element.32.we_ref, f32[90,2,1440]{2,1,0:T(2,128)S(1)} %get-tuple-element.33.wn_ref, f32[90,2,1440]{2,1,0:T(2,128)S(1)} %get-tuple-element.34.g_ref, f32[184,8]{1,0:T(8,128)S(1)} %get-tuple-element.35.row_ref, ...), custom_call_target="tpu_custom_call" | custom-call | flops 207000000 | tf_op jit(solution)/shard_map/pallas_call | solution.py:624
  11.3 0.6 %collective-permute-start.3 = (f32[100,768]{1,0:T(8,128)S(1)}, f32[100,768]{1,0:T(8,128)S(1)}, u32[]{:S(2)}, u32[]{:S(2)}) collective-permute-start(f32[100,768]{1,0:T(8,128)S(1)} %shard_map.158.rest_2_), channel_id=1, source_target_pairs={{0,2},{2,0},{1,3},{3,1},{4,6},{6,4},{5,7},{7,5},{8,10},{10,8},{9,1... | collective-permute-start | bytes 921608 | tf_op jit(solution)/shard_map/ppermute | solution.py:581
  11.9 0.0 collective-permute-done.even_ref
  11.9 0.0 collective-permute-done.1.odd_ref
  11.9 0.0 copy-done.2
  11.9 0.0 copy-done.3
  11.9 0.0 copy-start.1
  11.9 3.5 %shard_map.156 = (f32[96,768]{1,0:T(8,128)S(1)}, f32[88,768]{1,0:T(8,128)S(1)}, f32[184,1440]{1,0:T(8,128)S(1)}, f32[184,256]{1,0:T(8,128)S(1)}) custom-call(f32[90,2,1440]{2,1,0:T(2,128)S(1)} %get-tuple-element.32.we_ref, f32[90,2,1440]{2,1,0:T(2,128)S(1)} %get-tuple-element.33.wn_ref, f32[90,2,1440]{2,1,0:T(2,128)S(1)} %get-tuple-element.34.g_ref, ...), custom_call_target="tpu_custom_call" | custom-call | flops 920000000 | tf_op jit(solution)/shard_map/pallas_call | solution.py:640
  15.4 3.4 %collective-permute-start.4 = (f32[96,768]{1,0:T(8,128)S(1)}, f32[96,768]{1,0:T(8,128)S(1)}, u32[]{:S(2)}, u32[]{:S(2)}) collective-permute-start(f32[96,768]{1,0:T(8,128)S(1)} %get-tuple-element.46.rest_0_), channel_id=1, source_target_pairs={{0,2},{2,0},{12,14},{14,12},{1,3},{3,1},{13,15},{15,13},{16,18},{1... | collective-permute-start | bytes 884744 | tf_op jit(solution)/shard_map/ppermute | solution.py:662
  18.8 0.0 copy-start
  18.8 0.0 copy-start.4
  18.9 0.6 %collective-permute-start.5 = (f32[88,768]{1,0:T(8,128)S(1)}, f32[88,768]{1,0:T(8,128)S(1)}, u32[]{:S(2)}, u32[]{:S(2)}) collective-permute-start(f32[88,768]{1,0:T(8,128)S(1)} %get-tuple-element.49.rest_2_), channel_id=1, source_target_pairs={{0,2},{2,0},{1,3},{3,1},{4,6},{6,4},{5,7},{7,5},{8,10},{10,8},{9,1... | collective-permute-start | bytes 811016 | tf_op jit(solution)/shard_map/ppermute | solution.py:581
  19.5 0.0 collective-permute-done.2.arrived_ref.rest_1_
  19.5 1.7 %collective-permute-done.3.rest_3_ = f32[100,768]{1,0:T(8,128)S(1)} collective-permute-done((f32[100,768]{1,0:T(8,128)S(1)}, f32[100,768]{1,0:T(8,128)S(1)}, u32[]{:S(2)}, u32[]{:S(2)}) %collective-permute-start.3) | collective-permute-done | bytes 307232 | tf_op jit(solution)/shard_map/ppermute | solution.py:581
  21.1 0.0 copy-done.1
  21.1 0.0 copy-done
  21.1 0.0 copy-done.4
  21.1 3.9 %shard_map.159 = (f32[90,2,1440]{2,1,0:T(2,128)}, f32[180,1440]{1,0:T(8,128)S(1)}, f32[45,2,360]{2,1,0:T(2,128)S(1)}, f32[45,2,360]{2,1,0:T(2,128)S(1)}) custom-call(f32[2]{0:T(128)S(1)} %copy-done.4, f32[90,2,1440]{2,1,0:T(2,128)S(1)} %get-tuple-element.32.we_ref, f32[90,2,1440]{2,1,0:T(2,128)S(1)} %get-tuple-element.33.wn_ref, ...), custom_call_target="tpu_custom_call" | custom-call | flops 1150000000 | tf_op jit(solution)/shard_map/pallas_call | solution.py:665
  25.0 2.4 %collective-permute-done.4.rest_1_ = f32[96,768]{1,0:T(8,128)S(1)} collective-permute-done((f32[96,768]{1,0:T(8,128)S(1)}, f32[96,768]{1,0:T(8,128)S(1)}, u32[]{:S(2)}, u32[]{:S(2)}) %collective-permute-start.4) | collective-permute-done | bytes 294944 | tf_op jit(solution)/shard_map/ppermute | solution.py:662
  27.4 0.1 shard_map.162
  27.6 2.1 %collective-permute-start.6 = (f32[2,45,2,360]{3,2,1,0:T(2,128)S(1)}, f32[2,45,2,360]{3,2,1,0:T(2,128)S(1)}, u32[]{:S(2)}, u32[]{:S(2)}) collective-permute-start(f32[2,45,2,360]{3,2,1,0:T(2,128)S(1)} %shard_map.162), channel_id=1, source_target_pairs={{0,8},{12,4},{1,9},{13,5},{2,10},{14,6},{3,11},{15,7},{16,24},{28,... | collective-permute-start | bytes 777608 | tf_op jit(solution)/shard_map/ppermute | solution.py:684
  29.6 1.2 %shard_map.160 = (bf16[96,1536]{1,0:T(8,128)(2,1)S(1)}, bf16[96,1536]{1,0:T(8,128)(2,1)S(1)}) custom-call(f32[16,384]{1,0:T(8,128)S(1)} %get-tuple-element.36.phase_ref, f32[96,768]{1,0:T(8,128)S(1)} %get-tuple-element.46.rest_0_, f32[96,768]{1,0:T(8,128)S(1)} %collective-permute-done.4.rest_1_, bf16[2304,768]{1,0:T(8,128)(2,1)S(1)} %copy-done), custom_call_target="tpu_custom_call" | custom-call | flops 575000000 | tf_op jit(solution)/shard_map/pallas_call | solution.py:689
  30.8 1.3 %collective-permute-done.5.rest_3_ = f32[88,768]{1,0:T(8,128)S(1)} collective-permute-done((f32[88,768]{1,0:T(8,128)S(1)}, f32[88,768]{1,0:T(8,128)S(1)}, u32[]{:S(2)}, u32[]{:S(2)}) %collective-permute-start.5) | collective-permute-done | bytes 270368 | tf_op jit(solution)/shard_map/ppermute | solution.py:581
  32.2 0.0 copy-start.5
  32.2 3.3 %shard_map.161 = (f32[90,2,1440]{2,1,0:T(2,128)S(1)}, f32[90,2,1440]{2,1,0:T(2,128)S(1)}, f32[90,1440]{1,0:T(8,128)S(1)}, f32[45,2,360]{2,1,0:T(2,128)S(1)}) custom-call(f32[2]{0:T(128)S(1)} %copy-done.4, f32[184,1440]{1,0:T(8,128)S(1)} %get-tuple-element.44.north_ref, f32[180,1440]{1,0:T(8,128)S(1)} %get-tuple-element.45.part_ref, ...), custom_call_target="tpu_custom_call" | custom-call | flops 2300000000 | tf_op jit(solution)/shard_map/pallas_call | solution.py:697
  35.5 1.3 %collective-permute-start.7 = (f32[90,1440]{1,0:T(8,128)S(1)}, f32[90,1440]{1,0:T(8,128)S(1)}, u32[]{:S(2)}, u32[]{:S(2)}) collective-permute-start(f32[90,1440]{1,0:T(8,128)S(1)} %get-tuple-element.57), channel_id=1, source_target_pairs={{1,0},{3,2},{5,4},{7,6},{9,8},{11,10},{13,12},{15,14},{17,16},{19,... | collective-permute-start | bytes 1555208 | tf_op jit(solution)/shard_map/ppermute | solution.py:711
  36.8 0.0 collective-permute-done.6.arrived_ref
  36.8 0.0 copy-done.5
  36.8 2.1 %shard_map.163 = (f32[90,2,1440]{2,1,0:T(2,128)}, f32[90,2,1440]{2,1,0:T(2,128)}, f32[2,45,2,360]{3,2,1,0:T(2,128)}, f32[90,2,1440]{2,1,0:T(2,128)S(1)}) custom-call(f32[45,2,360]{2,1,0:T(2,128)S(1)} %get-tuple-element.43.east_keep, f32[45,2,360]{2,1,0:T(2,128)S(1)} %get-tuple-element.50.north_keep, ...), custom_call_target="tpu_custom_call" | custom-call | flops 5750000128 | tf_op jit(solution)/shard_map/pallas_call | solution.py:714
  38.9 0.5 %collective-permute-done.7.rest_0_ = f32[90,1440]{1,0:T(8,128)S(1)} collective-permute-done((f32[90,1440]{1,0:T(8,128)S(1)}, f32[90,1440]{1,0:T(8,128)S(1)}, u32[]{:S(2)}, u32[]{:S(2)}) %collective-permute-start.7) | collective-permute-done | bytes 518432 | tf_op jit(solution)/shard_map/ppermute | solution.py:711
  39.4 1.5 %shard_map.164 = f32[90,2,1440]{2,1,0:T(2,128)} custom-call(f32[90,2,1440]{2,1,0:T(2,128)S(1)} %get-tuple-element.56.own_ref, f32[90,1440]{1,0:T(8,128)S(1)} %collective-permute-done.7.rest_0_), custom_call_target="tpu_custom_call" | custom-call | flops 1150000000 | tf_op jit(solution)/shard_map/pallas_call | solution.py:722
  (1 shorter events, 0.0 us)
Async XLA Ops:
  4.1 15.3 %collective-permute-start.2 = (f32[80,768]{1,0:T(8,128)S(1)}, f32[80,768]{1,0:T(8,128)S(1)}, u32[]{:S(2)}, u32[]{:S(2)}) collective-permute-start(f32[80,768]{1,0:T(8,128)S(1)} %get-tuple-element.41.rest_0_), channel_id=1, source_target_pairs={{0,2},{2,0},{1,3},{3,1},{4,6},{6,4},{5,7},{7,5},{8,10},{10,8},{9,1... | collective-permute-start | bytes 737288 | tf_op jit(solution)/shard_map/ppermute | solution.py:581
  7.1 4.7 %collective-permute-start = (f32[8,1440]{1,0:T(8,128)S(1)}, f32[8,1440]{1,0:T(8,128)S(1)}, u32[]{:S(2)}, u32[]{:S(2)}) collective-permute-start(f32[8,1440]{1,0:T(8,128)S(1)} %get-tuple-element.37), channel_id=1, source_target_pairs={{0,4},{8,12},{4,0},{12,8},{1,5},{9,13},{5,1},{13,9},{2,6},{10,14},... | collective-permute-start | bytes 138248 | tf_op jit(solution)/shard_map/ppermute | solution.py:637
  8.5 3.4 %collective-permute-start.1 = (f32[8,1440]{1,0:T(8,128)S(1)}, f32[8,1440]{1,0:T(8,128)S(1)}, u32[]{:S(2)}, u32[]{:S(2)}) collective-permute-start(f32[8,1440]{1,0:T(8,128)S(1)} %get-tuple-element.38), channel_id=1, source_target_pairs={{4,8},{8,4},{5,9},{9,5},{6,10},{10,6},{7,11},{11,7},{20,24},{24,20... | collective-permute-start | bytes 138248 | tf_op jit(solution)/shard_map/ppermute | solution.py:637
  9.2 2.7 %copy-start.2 = (s32[180]{0:T(256)S(1)}, s32[180]{0:T(256)}, u32[]{:S(2)}) copy-start(s32[180]{0:T(256)} %param.18) | copy-start | bytes 2164
  9.2 2.7 %copy-start.3 = (s32[180]{0:T(256)S(1)}, s32[180]{0:T(256)}, u32[]{:S(2)}) copy-start(s32[180]{0:T(256)} %param.19) | copy-start | bytes 2164
  11.3 9.8 %collective-permute-start.3 = (f32[100,768]{1,0:T(8,128)S(1)}, f32[100,768]{1,0:T(8,128)S(1)}, u32[]{:S(2)}, u32[]{:S(2)}) collective-permute-start(f32[100,768]{1,0:T(8,128)S(1)} %shard_map.158.rest_2_), channel_id=1, source_target_pairs={{0,2},{2,0},{1,3},{3,1},{4,6},{6,4},{5,7},{7,5},{8,10},{10,8},{9,1... | collective-permute-start | bytes 921608 | tf_op jit(solution)/shard_map/ppermute | solution.py:581
  11.9 9.2 %copy-start.1 = (f32[2,90,1440]{2,0,1:T(2,128)S(1)}, f32[2,90,1440]{2,0,1:T(2,128)}, u32[]{:S(2)}) copy-start(f32[2,90,1440]{2,0,1:T(2,128)} %param.14) | copy-start | bytes 3110404
  15.4 12.0 %collective-permute-start.4 = (f32[96,768]{1,0:T(8,128)S(1)}, f32[96,768]{1,0:T(8,128)S(1)}, u32[]{:S(2)}, u32[]{:S(2)}) collective-permute-start(f32[96,768]{1,0:T(8,128)S(1)} %get-tuple-element.46.rest_0_), channel_id=1, source_target_pairs={{0,2},{2,0},{12,14},{14,12},{1,3},{3,1},{13,15},{15,13},{16,18},{1... | collective-permute-start | bytes 884744 | tf_op jit(solution)/shard_map/ppermute | solution.py:662
  18.8 2.3 %copy-start = (bf16[2304,768]{1,0:T(8,128)(2,1)S(1)}, bf16[2304,768]{1,0:T(8,128)(2,1)}, u32[]{:S(2)}) copy-start(bf16[2304,768]{1,0:T(8,128)(2,1)} %constant.9.clone.rest_4_.rest_2_) | copy-start | bytes 10616836
  18.8 2.3 %copy-start.4 = (f32[2]{0:T(128)S(1)}, f32[2]{0:T(128)}, u32[]{:S(2)}) copy-start(f32[2]{0:T(128)} %depth_ref.3) | copy-start | bytes 28
  18.9 13.3 %collective-permute-start.5 = (f32[88,768]{1,0:T(8,128)S(1)}, f32[88,768]{1,0:T(8,128)S(1)}, u32[]{:S(2)}, u32[]{:S(2)}) collective-permute-start(f32[88,768]{1,0:T(8,128)S(1)} %get-tuple-element.49.rest_2_), channel_id=1, source_target_pairs={{0,2},{2,0},{1,3},{3,1},{4,6},{6,4},{5,7},{7,5},{8,10},{10,8},{9,1... | collective-permute-start | bytes 811016 | tf_op jit(solution)/shard_map/ppermute | solution.py:581
  27.6 9.2 %collective-permute-start.6 = (f32[2,45,2,360]{3,2,1,0:T(2,128)S(1)}, f32[2,45,2,360]{3,2,1,0:T(2,128)S(1)}, u32[]{:S(2)}, u32[]{:S(2)}) collective-permute-start(f32[2,45,2,360]{3,2,1,0:T(2,128)S(1)} %shard_map.162), channel_id=1, source_target_pairs={{0,8},{12,4},{1,9},{13,5},{2,10},{14,6},{3,11},{15,7},{16,24},{28,... | collective-permute-start | bytes 777608 | tf_op jit(solution)/shard_map/ppermute | solution.py:684
  32.2 4.6 %copy-start.5 = (f32[90,1440]{1,0:T(8,128)S(1)}, f32[90,1440]{1,0:T(8,128)}, u32[]{:S(2)}) copy-start(f32[90,1440]{1,0:T(8,128)} %surface_ref.1) | copy-start | bytes 1555204
  35.5 3.9 %collective-permute-start.7 = (f32[90,1440]{1,0:T(8,128)S(1)}, f32[90,1440]{1,0:T(8,128)S(1)}, u32[]{:S(2)}, u32[]{:S(2)}) collective-permute-start(f32[90,1440]{1,0:T(8,128)S(1)} %get-tuple-element.57), channel_id=1, source_target_pairs={{1,0},{3,2},{5,4},{7,6},{9,8},{11,10},{13,12},{15,14},{17,16},{19,... | collective-permute-start | bytes 1555208 | tf_op jit(solution)/shard_map/ppermute | solution.py:711

commit v4 on v3

--- a/solution.py
+++ b/solution.py
@@ -48,6 +48,7 @@
         self.spec_width = 2 * KMAX // self.n_lon
         self.helped = self.help * self.lev
         self.ahead = round_up(self.helped, 16)
+        self.cuts = 2
         self.first = min(round_up(self.own * 4 // 9, 8 * self.lev), self.own)
 
 
@@ -480,12 +481,13 @@
 
 
 def north_inverse(
-    z, depth_ref, north_ref, part_ref, row_ref, phase_ref, chosen_ref, high_ahead, low_ahead, *rest
+    z, active, depth_ref, north_ref, part_ref, row_ref, phase_ref, chosen_ref, high_ahead, low_ahead,
+    *rest,
 ):
     ahead, shares, rest = rest[: z.n_lon], rest[z.n_lon : 2 * z.n_lon], rest[2 * z.n_lon :]
     basis_ref, final_ref, thick_ref, column_ref, keep_ref, lhs_ref, rows_ref, high_ref, low_ref = rest
 
-    @pl.when(on_polar_band(z))
+    @pl.when(active & on_polar_band(z))
     def _():
         more = z.ahead - 8
         kept = [ahead[0][more:, KMAX : KMAX + 1], shares[0][:, KMAX : KMAX + 1]]
@@ -507,7 +509,7 @@
         polar = column_of(row_ref, POLAR)[beyond] > 0.0
         rows_ref[beyond, : z.lon] = jnp.where(polar, rows_ref[beyond, : z.lon], north_ref[beyond])
 
-    @pl.when(jnp.logical_not(on_polar_band(z)))
+    @pl.when(active & jnp.logical_not(on_polar_band(z)))
     def _():
         keep_ref[...] = jnp.zeros_like(keep_ref)
         beyond = slice(z.own, z.rows)
@@ -518,41 +520,68 @@
         rows_ref[beyond, : z.lon] = jnp.where(polar, rows_ref[beyond, : z.lon], north_ref[beyond])
         rows_ref[: z.own, : z.lon] = north_ref[: z.own]
 
-    final = rows_ref[:, : z.lon]
-    final_ref[...] = final[: z.own].reshape(final_ref.shape)
-    scaled = final * column_of(row_ref, COSINE)
-    diff = (roll(scaled, -z.lev, 0) - roll(scaled, z.lev, 0))[: z.own]
-    scale = depths(z, depth_ref, row_ref) * column_of(row_ref, NORTH_COEF)[: z.own]
-    thick_ref[...] = (part_ref[...] - scale * diff).reshape(thick_ref.shape)
-    column_ref[...] = sum(thick_ref[:, lev, :] for lev in range(z.lev))
-
-
-def store_results(z, east_keep, north_keep, arrived_ref, surface_ref, *rest):
-    fields, outs = rest[:2], rest[2:4]
-    spectra_ref, geo_ref, sems = rest[4:]
-    copies = [
-        pltpu.make_async_copy(*pair, sems.at[n])
-        for n, pair in enumerate(zip(fields, outs, strict=True))
-    ]
-    for copy in copies:
-        copy.start()
-    column = None
-    for lev in reversed(range(z.lev)):
-        one = fields[1][:, lev, :]
-        column = one if column is None else column + one
-        geo_ref[:, lev, :] = surface_ref[...] + GRAVITY * column
+    @pl.when(active)
+    def _():
+        final = rows_ref[:, : z.lon]
+        final_ref[...] = final[: z.own].reshape(final_ref.shape)
+        scaled = final * column_of(row_ref, COSINE)
+        diff = (roll(scaled, -z.lev, 0) - roll(scaled, z.lev, 0))[: z.own]
+        scale = depths(z, depth_ref, row_ref) * column_of(row_ref, NORTH_COEF)[: z.own]
+        thick_ref[...] = (part_ref[...] - scale * diff).reshape(thick_ref.shape)
+        column_ref[...] = sum(thick_ref[:, lev, :] for lev in range(z.lev))
+
+
+def sends_column():
+    return lax.axis_index("lev") > 0
+
+
+def north_deeper(z, *refs):
+    north_inverse(z, sends_column(), *refs)
+
+
+def north_shallowest(z, east_keep, north_keep, arrived_ref, *rest):
+    *refs, spectra_ref, column_ref, keep_ref, lhs_ref, rows_ref, high_ref, low_ref = rest
+    active = jnp.logical_not(sends_column())
+    north_inverse(z, active, *refs, column_ref, keep_ref, lhs_ref, rows_ref, high_ref, low_ref)
+
+    @pl.when(sends_column())
+    def _():
+        keep_ref[...] = north_keep[...]
+
     polar = on_polar_band(z)
     spectra_ref[0] = jnp.where(polar, east_keep[...], arrived_ref[0])
-    spectra_ref[1] = jnp.where(polar, north_keep[...], arrived_ref[1])
-    for copy in copies:
-        copy.wait()
-
-
-def add_deeper(z, own_ref, *rest):
-    deeper, geo_ref = rest[:-1], rest[-1]
-    deeper = GRAVITY * sum(ref[...] for ref in deeper)
-    for lev in range(z.lev):
-        geo_ref[:, lev, :] = own_ref[:, lev, :] + deeper
+    spectra_ref[1] = jnp.where(polar, keep_ref[...], arrived_ref[1])
+
+
+def finish(z, surface_ref, *rest):
+    deeper_fields, own_fields, deeper, outs = rest[:2], rest[2:4], rest[4 : 3 + z.n_lev], rest[3 + z.n_lev :]
+    final_out, thick_out, geo_out, geo_ref, sems = outs
+
+    def store(fields):
+        copies = [
+            pltpu.make_async_copy(*pair, sems.at[n])
+            for n, pair in enumerate(zip(fields, (final_out, thick_out), strict=True))
+        ]
+        for copy in copies:
+            copy.start()
+        for n in range(z.cuts):
+            at = slice(n * z.lat // z.cuts, (n + 1) * z.lat // z.cuts)
+            column = sum(ref[at] for ref in deeper)
+            for lev in reversed(range(z.lev)):
+                column = column + fields[1][at, lev, :]
+                geo_ref[at, lev, :] = surface_ref[at] + GRAVITY * column
+            copies.append(pltpu.make_async_copy(geo_ref.at[at], geo_out.at[at], sems.at[2 + n]))
+            copies[-1].start()
+        for copy in copies:
+            copy.wait()
+
+    @pl.when(sends_column())
+    def _():
+        store(deeper_fields)
+
+    @pl.when(jnp.logical_not(sends_column()))
+    def _():
+        store(own_fields)
 
 
 def call(kernel, n_in, out_shape, scratch, micros, spaces=None, in_hbm=0, vmem=24):
@@ -694,35 +723,42 @@
         0.5,
     )(phase, *north_aheads, inverse)
 
-    north_final, thick_new, column, north_keep = call(
-        functools.partial(north_inverse, z),
-        9 + 2 * z.n_lon,
-        [pltpu.VMEM(field, jnp.float32)] * 2 + [(z.lat, z.lon), spec],
-        [waves_lhs, pltpu.VMEM((z.rows, z.ext), jnp.float32)]
-        + [pltpu.VMEM((places, z.ext), jnp.bfloat16)] * 2,
+    operands = (
+        mean_depth, north_new, thick_part, per_row, phase, chosen, ahead_high, ahead_low,
+        *north_aheads, *north_rests, inverse,
+    )
+    in_vmem = pltpu.VMEM(field, jnp.float32)
+    scratch = [waves_lhs, pltpu.VMEM((z.rows, z.ext), jnp.float32)]
+    scratch += [pltpu.VMEM((places, z.ext), jnp.bfloat16)] * 2
+    final_deeper, thick_deeper, column, north_keep = call(
+        functools.partial(north_deeper, z),
+        len(operands),
+        [in_vmem, in_vmem, (z.lat, z.lon), spec],
+        scratch,
         2,
         {0: pltpu.SMEM},
-    )(
-        mean_depth, north_new, thick_part, per_row, phase, chosen, ahead_high, ahead_low,
-        *north_aheads, *north_rests, inverse,
-    )
-
+    )(*operands)
     deeper = [
         lax.ppermute(column, "lev", [(i, i - distance) for i in range(distance, z.n_lev)])
         for distance in range(1, z.n_lev)
     ]
-    north_final, thick_out, spectra, geo_own = call(
-        functools.partial(store_results, z),
-        6,
-        [pltpu.HBM(field, jnp.float32)] * 2 + [(2, *spec), pltpu.VMEM(field, jnp.float32)],
-        [pltpu.SemaphoreType.DMA((2,))],
-        5,
-        in_hbm=2,
-    )(east_keep, north_keep, arrived, surface_geopot, north_final, thick_new)
-    (geo_new,) = call(functools.partial(add_deeper, z), 1 + len(deeper), [field], [], 1)(
-        geo_own, *deeper
-    )
-    return tuple(level_inside(x) for x in (east_final, north_final, thick_out, geo_new, spectra))
+    final_own, thick_own, spectra = call(
+        functools.partial(north_shallowest, z),
+        3 + len(operands),
+        [in_vmem, in_vmem, (2, *spec)],
+        [pltpu.VMEM((z.lat, z.lon), jnp.float32), pltpu.VMEM(spec, jnp.float32)] + scratch,
+        3.2,
+        {3: pltpu.SMEM},
+    )(east_keep, north_keep, arrived, *operands)
+    north_final, thick_new, geo_new = call(
+        functools.partial(finish, z),
+        5 + len(deeper),
+        [pltpu.HBM(field, jnp.float32)] * 3,
+        [pltpu.VMEM(field, jnp.float32), pltpu.SemaphoreType.DMA((2 + z.cuts,))],
+        1,
+        in_hbm=3,
+    )(surface_geopot, final_deeper, thick_deeper, final_own, thick_own, *deeper)
+    return tuple(level_inside(x) for x in (east_final, north_final, thick_new, geo_new, spectra))
 
 
 def solution(mesh):

time: 41.3 us -> 40.2 us (0.973)
  Pallas kernels: 21.1 us -> 20.4 us
  waiting for transfers between devices: 5.95 us -> 5.48 us
    pallas_call x3, Pallas kernels: 6.86 us -> 6.25 us  [the longest x1 3.94 us: local(): call(functools.partial(north_shallowest, z), 3 + len(operands), [in_vmem,...]
    ppermute x1, waiting for transfers between devices: 0.49 us -> 0.01 us  [local(): lax.ppermute(column, 'lev', [(i, i - distance) for i in range(distance, z...]
  transfers between devices with their start and end apart: 8 -> 8, of which waited for: 4 -> 3; matrix products, arithmetic and copies ran while one was open for 0% -> 0% of each run, Pallas kernels for 39% -> 38%
where the time goes in v4:
time: 40.2 us; the launch traced here: 39.9 us
  Pallas kernels  20.4 us (51%)
  starting transfers between devices  13 us (32%)
  waiting for transfers between devices  5.48 us (14%)
  between operations  0.94 us (2%)
    ppermute x3, starting transfers between devices, shifted(): lax.ppermute(block, axis, [(i, (i + distance) % count) for i in range(cou...  4.21 us
    pallas_call x1, Pallas kernels, local(): call(functools.partial(north_shallowest, z), 3 + len(operands), [in_vmem,...  3.94 us
    pallas_call x1, Pallas kernels, local(): call(functools.partial(east_inverse, z), 11 + 2 * z.n_lon, [field, (z.own...  3.86 us
    pallas_call x1, Pallas kernels, local(): call(functools.partial(north_forward, z), 10, [(z.ahead, WIDE), (z.rows -...  3.51 us
    pallas_call x1, Pallas kernels, local(): call(functools.partial(east_first, z), 6, [(z.first, WIDE), rims, rims] +...  3.48 us
    ppermute x1, starting transfers between devices, local(): north_aheads.append(lax.ppermute(north_ahead, ('lat', 'lon'), route))  3.4 us
    ppermute x3, waiting for transfers between devices, shifted(): lax.ppermute(block, axis, [(i, (i + distance) % count) for i in range(cou...  3.02 us
    ppermute x1, waiting for transfers between devices, local(): north_aheads.append(lax.ppermute(north_ahead, ('lat', 'lon'), route))  2.45 us
  transfers between devices with their start and end apart: 8, of which 3 were waited for; matrix products, arithmetic and copies ran while one was open for 0% of the time, Pallas kernels for 38%

profile of v4, /device:TPU:0, one launch (start us, length us, event | category | flops | bytes accessed | tf_op | source)
XLA Modules:
  0.0 39.9 jit_solution(1699852947344390836)
XLA Ops:
  0.6 3.5 %shard_map.155 = (f32[80,768]{1,0:T(8,128)S(1)}, f32[8,1440]{1,0:T(8,128)S(1)}, f32[8,1440]{1,0:T(8,128)S(1)}, f32[90,2,1440]{2,1,0:T(2,128)S(1)}, f32[90,2,1440...) custom-call(f32[90,2,1440]{2,1,0:T(2,128)} %bitcast.15, ...), custom_call_target="tpu_custom_call" | custom-call | flops 1150000000 | tf_op jit(solution)/shard_map/pallas_call | solution.py:643
  4.1 3.0 %collective-permute-start.2 = (f32[80,768]{1,0:T(8,128)S(1)}, f32[80,768]{1,0:T(8,128)S(1)}, u32[]{:S(2)}, u32[]{:S(2)}) collective-permute-start(f32[80,768]{1,0:T(8,128)S(1)} %get-tuple-element.43.rest_0_), channel_id=1, source_target_pairs={{0,2},{2,0},{1,3},{3,1},{4,6},{6,4},{5,7},{7,5},{8,10},{10,8},{9,1... | collective-permute-start | bytes 737288 | tf_op jit(solution)/shard_map/ppermute | solution.py:610
  7.1 1.4 %collective-permute-start = (f32[8,1440]{1,0:T(8,128)S(1)}, f32[8,1440]{1,0:T(8,128)S(1)}, u32[]{:S(2)}, u32[]{:S(2)}) collective-permute-start(f32[8,1440]{1,0:T(8,128)S(1)} %get-tuple-element.39), channel_id=1, source_target_pairs={{0,4},{8,12},{4,0},{12,8},{1,5},{9,13},{5,1},{13,9},{2,6},{10,14},... | collective-permute-start | bytes 138248 | tf_op jit(solution)/shard_map/ppermute | solution.py:666
  8.5 0.7 %collective-permute-start.1 = (f32[8,1440]{1,0:T(8,128)S(1)}, f32[8,1440]{1,0:T(8,128)S(1)}, u32[]{:S(2)}, u32[]{:S(2)}) collective-permute-start(f32[8,1440]{1,0:T(8,128)S(1)} %get-tuple-element.40), channel_id=1, source_target_pairs={{4,8},{8,4},{5,9},{9,5},{6,10},{10,6},{7,11},{11,7},{20,24},{24,20... | collective-permute-start | bytes 138248 | tf_op jit(solution)/shard_map/ppermute | solution.py:666
  9.2 0.0 copy-start.3
  9.2 0.0 copy-start.4
  9.2 2.1 %shard_map.158.rest_2_ = f32[100,768]{1,0:T(8,128)S(1)} custom-call(f32[90,2,1440]{2,1,0:T(2,128)S(1)} %get-tuple-element.34.we_ref, f32[90,2,1440]{2,1,0:T(2,128)S(1)} %get-tuple-element.35.wn_ref, f32[90,2,1440]{2,1,0:T(2,128)S(1)} %get-tuple-element.36.g_ref, f32[184,8]{1,0:T(8,128)S(1)} %get-tuple-element.37.row_ref.refs_3_.rest_3_, ...), custom_call_target="tpu_custom_call" | custom-call | flops 207000000 | tf_op jit(solution)/shard_map/pallas_call | solution.py:653
  11.3 0.6 %collective-permute-start.3 = (f32[100,768]{1,0:T(8,128)S(1)}, f32[100,768]{1,0:T(8,128)S(1)}, u32[]{:S(2)}, u32[]{:S(2)}) collective-permute-start(f32[100,768]{1,0:T(8,128)S(1)} %shard_map.158.rest_2_), channel_id=1, source_target_pairs={{0,2},{2,0},{1,3},{3,1},{4,6},{6,4},{5,7},{7,5},{8,10},{10,8},{9,1... | collective-permute-start | bytes 921608 | tf_op jit(solution)/shard_map/ppermute | solution.py:610
  11.9 0.0 collective-permute-done.even_ref
  11.9 0.0 collective-permute-done.1.odd_ref
  11.9 0.0 copy-done.3
  11.9 0.0 copy-done.4
  11.9 0.0 copy-start.1
  11.9 3.5 %shard_map.156 = (f32[96,768]{1,0:T(8,128)S(1)}, f32[88,768]{1,0:T(8,128)S(1)}, f32[184,1440]{1,0:T(8,128)S(1)}, f32[184,256]{1,0:T(8,128)S(1)}) custom-call(f32[90,2,1440]{2,1,0:T(2,128)S(1)} %get-tuple-element.34.we_ref, f32[90,2,1440]{2,1,0:T(2,128)S(1)} %get-tuple-element.35.wn_ref, f32[90,2,1440]{2,1,0:T(2,128)S(1)} %get-tuple-element.36.g_ref, ...), custom_call_target="tpu_custom_call" | custom-call | flops 920000000 | tf_op jit(solution)/shard_map/pallas_call | solution.py:669
  15.4 3.4 %collective-permute-start.4 = (f32[96,768]{1,0:T(8,128)S(1)}, f32[96,768]{1,0:T(8,128)S(1)}, u32[]{:S(2)}, u32[]{:S(2)}) collective-permute-start(f32[96,768]{1,0:T(8,128)S(1)} %get-tuple-element.47.rest_0_.refs_8_.rest_8_), channel_id=1, source_target_pairs={{0,2},{2,0},{12,14},{14,12},{1,3},{3,1},{13,15},{15,13},{16,18},{1... | collective-permute-start | bytes 884744 | tf_op jit(solution)/shard_map/ppermute | solution.py:691
  18.8 0.0 copy-start
  18.8 0.0 copy-start.5
  18.9 0.6 %collective-permute-start.5 = (f32[88,768]{1,0:T(8,128)S(1)}, f32[88,768]{1,0:T(8,128)S(1)}, u32[]{:S(2)}, u32[]{:S(2)}) collective-permute-start(f32[88,768]{1,0:T(8,128)S(1)} %get-tuple-element.50.refs_10_.rest_10_), channel_id=1, source_target_pairs={{0,2},{2,0},{1,3},{3,1},{4,6},{6,4},{5,7},{7,5},{8,10},{10,8},{9,1... | collective-permute-start | bytes 811016 | tf_op jit(solution)/shard_map/ppermute | solution.py:610
  19.5 0.0 collective-permute-done.2.arrived_ref.rest_1_
  19.5 1.7 %collective-permute-done.3.rest_3_ = f32[100,768]{1,0:T(8,128)S(1)} collective-permute-done((f32[100,768]{1,0:T(8,128)S(1)}, f32[100,768]{1,0:T(8,128)S(1)}, u32[]{:S(2)}, u32[]{:S(2)}) %collective-permute-start.3) | collective-permute-done | bytes 307232 | tf_op jit(solution)/shard_map/ppermute | solution.py:610
  21.1 0.0 copy-done.1
  21.1 0.0 copy-done
  21.1 0.0 copy-done.5
  21.1 3.9 %shard_map.159 = (f32[90,2,1440]{2,1,0:T(2,128)}, f32[180,1440]{1,0:T(8,128)S(1)}, f32[45,2,360]{2,1,0:T(2,128)S(1)}, f32[45,2,360]{2,1,0:T(2,128)S(1)}) custom-call(f32[2]{0:T(128)S(1)} %copy-done.5, f32[90,2,1440]{2,1,0:T(2,128)S(1)} %get-tuple-element.34.we_ref, f32[90,2,1440]{2,1,0:T(2,128)S(1)} %get-tuple-element.35.wn_ref, ...), custom_call_target="tpu_custom_call" | custom-call | flops 1150000000 | tf_op jit(solution)/shard_map/pallas_call | solution.py:694
  25.0 2.5 %collective-permute-done.4.rest_1_.refs_9_.rest_9_ = f32[96,768]{1,0:T(8,128)S(1)} collective-permute-done((f32[96,768]{1,0:T(8,128)S(1)}, f32[96,768]{1,0:T(8,128)S(1)}, u32[]{:S(2)}, u32[]{:S(2)}) %collective-permute-start.4) | collective-permute-done | bytes 294944 | tf_op jit(solution)/shard_map/ppermute | solution.py:691
  27.4 0.1 shard_map.162
  27.6 2.1 %collective-permute-start.6 = (f32[2,45,2,360]{3,2,1,0:T(2,128)S(1)}, f32[2,45,2,360]{3,2,1,0:T(2,128)S(1)}, u32[]{:S(2)}, u32[]{:S(2)}) collective-permute-start(f32[2,45,2,360]{3,2,1,0:T(2,128)S(1)} %shard_map.162), channel_id=1, source_target_pairs={{0,8},{12,4},{1,9},{13,5},{2,10},{14,6},{3,11},{15,7},{16,24},{28,... | collective-permute-start | bytes 777608 | tf_op jit(solution)/shard_map/ppermute | solution.py:713
  29.6 1.2 %shard_map.160 = (bf16[96,1536]{1,0:T(8,128)(2,1)S(1)}, bf16[96,1536]{1,0:T(8,128)(2,1)S(1)}) custom-call(f32[16,384]{1,0:T(8,128)S(1)} %get-tuple-element.38.phase_ref.refs_4_.rest_4_, f32[96,768]{1,0:T(8,128)S(1)} %get-tuple-element.47.rest_0_.refs_8_.rest_8_, f32[96,768]{1,0:T(8,128)S(1)} %collective-permute-done.4.rest_1_.refs_9_.rest_9_, ...), custom_call_target="tpu_custom_call" | custom-call | flops 575000000 | tf_op jit(solution)/shard_map/pallas_call | solution.py:718
  30.8 1.4 %collective-permute-done.5.refs_11_.rest_11_ = f32[88,768]{1,0:T(8,128)S(1)} collective-permute-done((f32[88,768]{1,0:T(8,128)S(1)}, f32[88,768]{1,0:T(8,128)S(1)}, u32[]{:S(2)}, u32[]{:S(2)}) %collective-permute-start.5) | collective-permute-done | bytes 270368 | tf_op jit(solution)/shard_map/ppermute | solution.py:610
  32.2 0.6 %shard_map.161 = (f32[90,2,1440]{2,1,0:T(2,128)S(1)}, f32[90,2,1440]{2,1,0:T(2,128)S(1)}, f32[90,1440]{1,0:T(8,128)S(1)}, f32[45,2,360]{2,1,0:T(2,128)S(1)}) custom-call(f32[2]{0:T(128)S(1)} %copy-done.5, f32[184,1440]{1,0:T(8,128)S(1)} %get-tuple-element.45.refs_1_.rest_1_, f32[180,1440]{1,0:T(8,128)S(1)} %get-tuple-element.46.refs_2_.rest_2_, ...), custom_call_target="tpu_custom_call" | custom-call | flops 2300000000 | tf_op jit(solution)/shard_map/pallas_call | solution.py:733
  32.7 1.3 %collective-permute-start.7 = (f32[90,1440]{1,0:T(8,128)S(1)}, f32[90,1440]{1,0:T(8,128)S(1)}, u32[]{:S(2)}, u32[]{:S(2)}) collective-permute-start(f32[90,1440]{1,0:T(8,128)S(1)} %get-tuple-element.58), channel_id=1, source_target_pairs={{1,0},{3,2},{5,4},{7,6},{9,8},{11,10},{13,12},{15,14},{17,16},{19,... | collective-permute-start | bytes 1555208 | tf_op jit(solution)/shard_map/ppermute | solution.py:742
  34.0 0.0 collective-permute-done.6.arrived_ref
  34.0 0.0 copy-start.2
  34.1 3.9 %shard_map.163 = (f32[90,2,1440]{2,1,0:T(2,128)S(1)}, f32[90,2,1440]{2,1,0:T(2,128)S(1)}, f32[2,45,2,360]{3,2,1,0:T(2,128)}) custom-call(f32[45,2,360]{2,1,0:T(2,128)S(1)} %get-tuple-element.53.east_keep, f32[45,2,360]{2,1,0:T(2,128)S(1)} %get-tuple-element.54.north_keep, f32[2,45,2,360]{3,2,1,0:T(2,128)S(1)} %collective-permute-done.6.arrived_ref, ...), custom_call_target="tpu_custom_call" | custom-call | flops 3680000000 | tf_op jit(solution)/shard_map/pallas_call | solution.py:745
  38.0 0.0 collective-permute-done.7.rest_4_
  38.0 0.0 copy-done.2
  38.0 1.7 %shard_map.164 = (f32[90,2,1440]{2,1,0:T(2,128)}, f32[90,2,1440]{2,1,0:T(2,128)}, f32[90,2,1440]{2,1,0:T(2,128)}) custom-call(f32[90,1440]{1,0:T(8,128)S(1)} %copy-done.2, f32[90,2,1440]{2,1,0:T(2,128)S(1)} %get-tuple-element.51.rest_0_, f32[90,2,1440]{2,1,0:T(2,128)S(1)} %get-tuple-element.52.rest_1_, f32[90,2,1440]{2,1,0:T(2,128)S(1)} %get-tuple-element.56.rest_2_, ...), custom_call_target="tpu_custom_call" | custom-call | flops 1150000000 | tf_op jit(solution)/shard_map/pallas_call | solution.py:753
  (1 shorter events, 0.0 us)
Async XLA Ops:
  4.1 15.3 %collective-permute-start.2 = (f32[80,768]{1,0:T(8,128)S(1)}, f32[80,768]{1,0:T(8,128)S(1)}, u32[]{:S(2)}, u32[]{:S(2)}) collective-permute-start(f32[80,768]{1,0:T(8,128)S(1)} %get-tuple-element.43.rest_0_), channel_id=1, source_target_pairs={{0,2},{2,0},{1,3},{3,1},{4,6},{6,4},{5,7},{7,5},{8,10},{10,8},{9,1... | collective-permute-start | bytes 737288 | tf_op jit(solution)/shard_map/ppermute | solution.py:610
  7.1 4.7 %collective-permute-start = (f32[8,1440]{1,0:T(8,128)S(1)}, f32[8,1440]{1,0:T(8,128)S(1)}, u32[]{:S(2)}, u32[]{:S(2)}) collective-permute-start(f32[8,1440]{1,0:T(8,128)S(1)} %get-tuple-element.39), channel_id=1, source_target_pairs={{0,4},{8,12},{4,0},{12,8},{1,5},{9,13},{5,1},{13,9},{2,6},{10,14},... | collective-permute-start | bytes 138248 | tf_op jit(solution)/shard_map/ppermute | solution.py:666
  8.5 3.4 %collective-permute-start.1 = (f32[8,1440]{1,0:T(8,128)S(1)}, f32[8,1440]{1,0:T(8,128)S(1)}, u32[]{:S(2)}, u32[]{:S(2)}) collective-permute-start(f32[8,1440]{1,0:T(8,128)S(1)} %get-tuple-element.40), channel_id=1, source_target_pairs={{4,8},{8,4},{5,9},{9,5},{6,10},{10,6},{7,11},{11,7},{20,24},{24,20... | collective-permute-start | bytes 138248 | tf_op jit(solution)/shard_map/ppermute | solution.py:666
  9.2 2.7 %copy-start.3 = (s32[180]{0:T(256)S(1)}, s32[180]{0:T(256)}, u32[]{:S(2)}) copy-start(s32[180]{0:T(256)} %param.18) | copy-start | bytes 2164
  9.2 2.7 %copy-start.4 = (s32[180]{0:T(256)S(1)}, s32[180]{0:T(256)}, u32[]{:S(2)}) copy-start(s32[180]{0:T(256)} %param.19) | copy-start | bytes 2164
  11.3 9.9 %collective-permute-start.3 = (f32[100,768]{1,0:T(8,128)S(1)}, f32[100,768]{1,0:T(8,128)S(1)}, u32[]{:S(2)}, u32[]{:S(2)}) collective-permute-start(f32[100,768]{1,0:T(8,128)S(1)} %shard_map.158.rest_2_), channel_id=1, source_target_pairs={{0,2},{2,0},{1,3},{3,1},{4,6},{6,4},{5,7},{7,5},{8,10},{10,8},{9,1... | collective-permute-start | bytes 921608 | tf_op jit(solution)/shard_map/ppermute | solution.py:610
  11.9 9.2 %copy-start.1 = (f32[2,90,1440]{2,0,1:T(2,128)S(1)}, f32[2,90,1440]{2,0,1:T(2,128)}, u32[]{:S(2)}) copy-start(f32[2,90,1440]{2,0,1:T(2,128)} %param.14) | copy-start | bytes 3110404
  15.4 12.0 %collective-permute-start.4 = (f32[96,768]{1,0:T(8,128)S(1)}, f32[96,768]{1,0:T(8,128)S(1)}, u32[]{:S(2)}, u32[]{:S(2)}) collective-permute-start(f32[96,768]{1,0:T(8,128)S(1)} %get-tuple-element.47.rest_0_.refs_8_.rest_8_), channel_id=1, source_target_pairs={{0,2},{2,0},{12,14},{14,12},{1,3},{3,1},{13,15},{15,13},{16,18},{1... | collective-permute-start | bytes 884744 | tf_op jit(solution)/shard_map/ppermute | solution.py:691
  18.8 2.3 %copy-start = (bf16[2304,768]{1,0:T(8,128)(2,1)S(1)}, bf16[2304,768]{1,0:T(8,128)(2,1)}, u32[]{:S(2)}) copy-start(bf16[2304,768]{1,0:T(8,128)(2,1)} %constant.9.clone.rest_4_.rest_2_.refs_12_.rest_12_) | copy-start | bytes 10616836
  18.8 2.3 %copy-start.5 = (f32[2]{0:T(128)S(1)}, f32[2]{0:T(128)}, u32[]{:S(2)}) copy-start(f32[2]{0:T(128)} %rest_0_.1) | copy-start | bytes 28
  18.9 13.3 %collective-permute-start.5 = (f32[88,768]{1,0:T(8,128)S(1)}, f32[88,768]{1,0:T(8,128)S(1)}, u32[]{:S(2)}, u32[]{:S(2)}) collective-permute-start(f32[88,768]{1,0:T(8,128)S(1)} %get-tuple-element.50.refs_10_.rest_10_), channel_id=1, source_target_pairs={{0,2},{2,0},{1,3},{3,1},{4,6},{6,4},{5,7},{7,5},{8,10},{10,8},{9,1... | collective-permute-start | bytes 811016 | tf_op jit(solution)/shard_map/ppermute | solution.py:610
  27.6 6.5 %collective-permute-start.6 = (f32[2,45,2,360]{3,2,1,0:T(2,128)S(1)}, f32[2,45,2,360]{3,2,1,0:T(2,128)S(1)}, u32[]{:S(2)}, u32[]{:S(2)}) collective-permute-start(f32[2,45,2,360]{3,2,1,0:T(2,128)S(1)} %shard_map.162), channel_id=1, source_target_pairs={{0,8},{12,4},{1,9},{13,5},{2,10},{14,6},{3,11},{15,7},{16,24},{28,... | collective-permute-start | bytes 777608 | tf_op jit(solution)/shard_map/ppermute | solution.py:713
  32.7 5.3 %collective-permute-start.7 = (f32[90,1440]{1,0:T(8,128)S(1)}, f32[90,1440]{1,0:T(8,128)S(1)}, u32[]{:S(2)}, u32[]{:S(2)}) collective-permute-start(f32[90,1440]{1,0:T(8,128)S(1)} %get-tuple-element.58), channel_id=1, source_target_pairs={{1,0},{3,2},{5,4},{7,6},{9,8},{11,10},{13,12},{15,14},{17,16},{19,... | collective-permute-start | bytes 1555208 | tf_op jit(solution)/shard_map/ppermute | solution.py:742
  34.0 4.0 %copy-start.2 = (f32[90,1440]{1,0:T(8,128)S(1)}, f32[90,1440]{1,0:T(8,128)}, u32[]{:S(2)}) copy-start(f32[90,1440]{1,0:T(8,128)} %surface_ref.1) | copy-start | bytes 1555204

commit v5 on v4

--- a/solution.py
+++ b/solution.py
@@ -13,6 +13,9 @@
 HALF = 384
 WIDE = 2 * HALF
 SPARE = HALF - 128
+MORE = KMAX - SPARE
+MOVED = 128 - MORE
+LEFT = MORE - MOVED
 BLOCK = 256
 INVERSE_BLOCK = 768
 
@@ -139,6 +142,39 @@
     return phase_ref[2 * n : 2 * n + 1], phase_ref[2 * n + 1 : 2 * n + 2]
 
 
+def packed_rows(rows):
+    return 5 * rows + round_up(-(-rows // 2), 8) + 16
+
+
+def lanes_of(x):
+    return lax.broadcasted_iota(jnp.int32, x.shape, 1)
+
+
+def pack(x, out_ref):
+    rows = x.shape[0]
+    half = round_up(-(-rows // 2), 8)
+    tiles = [x[:, n : n + 128] for n in range(0, WIDE, 128)]
+    left = tiles[5]
+    lane = lanes_of(left)
+    tiles[2] = jnp.where(lane < MORE, tiles[2], roll(left, MOVED, 1))
+    for n in range(5):
+        out_ref[n * rows : (n + 1) * rows] = tiles[n]
+    lower = pad_rows(left[half:], half)
+    out_ref[5 * rows : 5 * rows + half] = jnp.where(lane[:half] < 64, left[:half], roll(lower, 64, 1))
+    out_ref[5 * rows + half :] = pad_rows(roll(left, -64, 1), 128).T[:16]
+
+
+def unpack(x, rows):
+    half = round_up(-(-rows // 2), 8)
+    tiles = [x[n * rows : (n + 1) * rows] for n in range(5)]
+    pairs = x[5 * rows : 5 * rows + half]
+    ends = pad_rows(x[5 * rows + half :], 128).T[:rows]
+    left = jnp.concatenate([pairs, roll(pairs, 64, 1)[: rows - half]], axis=0)
+    lane = lanes_of(left)
+    left = jnp.where(lane < 64, left, jnp.where(lane < LEFT, roll(ends, 64, 1), roll(tiles[2], -MOVED, 1)))
+    return jnp.concatenate([*tiles, left], axis=1)
+
+
 def forward_sums(
     z, x, basis_ref, phase_ref, lhs_ref, out_ref, at=slice(None), basis_here=None
 ):
@@ -275,10 +311,11 @@
 
 
 def east_shares_of(
-    z, at, we_ref, wn_ref, g_ref, row_ref, phase_ref, basis_ref, share_ref, lhs_ref, basis_here=None
+    z, at, we_ref, wn_ref, g_ref, row_ref, phase_ref, basis_ref, out_ref, lhs_ref, share_ref,
+    basis_here=None,
 ):
-    inner = slice(at.start // z.lev, at.stop // z.lev)
-    g, we, wn = (ref[inner].reshape(at.stop - at.start, z.lon) for ref in (g_ref, we_ref, wn_ref))
+    inner, rows = slice(at.start // z.lev, at.stop // z.lev), at.stop - at.start
+    g, we, wn = (ref[inner].reshape(rows, z.lon) for ref in (g_ref, we_ref, wn_ref))
 
     @pl.when(on_polar_band(z))
     def _():
@@ -286,29 +323,31 @@
         new = widen(z, we + CORIOLIS * sine * wn) - coef * east_diff(widen(z, g))
         tail = put_lane(new[:, z.ext - 128 :], 127, 0.0)
         new = jnp.concatenate([new[:, : z.ext - 128], tail], axis=1)
-        forward_sums(z, new, basis_ref, phase_ref, lhs_ref, share_ref, basis_here=basis_here)
+        forward_sums(
+            z, new, basis_ref, phase_ref, lhs_ref, share_ref, slice(rows), basis_here=basis_here
+        )
         cos, sin = phase_of(phase_ref, z.blocks)
         before = -coef * g[:, 0:1]
-        share_ref[:, :HALF] += before * cos
-        share_ref[:, HALF:] += before * sin
+        share_ref[:rows, :HALF] += before * cos
+        share_ref[:rows, HALF:] += before * sin
+        pack(share_ref[...], out_ref)
 
     @pl.when(jnp.logical_not(on_polar_band(z)))
     def _():
         if basis_here is not None:
             basis_here()
-        share_ref[...] = jnp.zeros_like(share_ref)
-
-    last = z.lon - 1
-    spare = share_ref[:, SPARE:HALF]
-    edges = ((g, last - 1), (g, last), (we, last), (wn, last), (g, 0), (g, 1), (we, 0), (wn, 0))
-    for n, (x, column) in enumerate(edges):
-        spare = put_lane(spare, KMAX - SPARE + n, x[:, column : column + 1])
-    share_ref[:, SPARE:HALF] = spare
+        last = z.lon - 1
+        columns = jnp.zeros((rows, 128), jnp.float32)
+        edges = ((g, last - 1), (g, last), (we, last), (wn, last), (g, 0), (g, 1), (we, 0), (wn, 0))
+        for n, (x, column) in enumerate(edges):
+            columns = put_lane(columns, n, x[:, column : column + 1])
+        out_ref[...] = jnp.zeros_like(out_ref)
+        out_ref[:rows] = columns
 
 
 def east_first(
     z, we_hbm, wn_hbm, g_hbm, row_hbm, phase_hbm, basis_hbm,
-    share_ref, even_ref, odd_ref, we_ref, wn_ref, g_ref, row_ref, phase_ref, basis_ref, lhs_ref, sems,
+    share_ref, even_ref, odd_ref, we_ref, wn_ref, g_ref, row_ref, phase_ref, basis_ref, lhs_ref, sums_ref, sems,
 ):
     fields = ((g_hbm, g_ref), (we_hbm, we_ref), (wn_hbm, wn_ref))
     cut, rim = z.first // z.lev, z.lat - 2
@@ -340,7 +379,7 @@
 
     east_shares_of(
         z, slice(0, z.first), we_ref, wn_ref, g_ref, row_ref, phase_ref, basis_ref, share_ref, lhs_ref,
-        basis_here,
+        sums_ref, basis_here,
     )
     odd = lax.rem(lax.axis_index("lat"), 2) == 1
     last, flat = z.lat - 1, (z.lev, z.lon)
@@ -357,7 +396,7 @@
 def north_forward(
     z, we_ref, wn_ref, g_ref, even_ref, odd_ref, row_ref, phase_ref, basis_ref, kept_ref, slot_ref, *rest
 ):
-    ahead_ref, rest_ref, north_ref, chosen_ref, g_rows, lhs_ref, share_ref = rest
+    ahead_ref, rest_ref, north_ref, chosen_ref, sorted_ref, g_rows, lhs_ref, share_ref = rest
     edge, lev = 2 * z.lev, z.lev
     odd = lax.rem(lax.axis_index("lat"), 2) == 1
     below = jnp.where(odd, odd_ref[...], even_ref[...])
@@ -385,21 +424,20 @@
         share_ref[:, SPARE:HALF] = put_lane(share_ref[:, SPARE:HALF], KMAX - SPARE, kept)
         chosen = slot_order(z, number, row_ref, slot_ref)
         ordered = reorder(chosen, share_ref[...])
-        ahead_ref[...] = ordered[: z.ahead]
-        rest_ref[...] = ordered[z.ahead : z.rows]
+        pack(ordered[: z.ahead], ahead_ref)
+        pack(ordered[z.ahead : z.rows], rest_ref)
+        sorted_ref[...] = ordered[: z.rows, SPARE:HALF]
         chosen_ref[...] = chosen
 
     @pl.when(jnp.logical_not(on_polar_band(z)))
     def _():
-        beyond = slice(z.own - z.ahead, z.rows - z.ahead)
         ahead_ref[...] = jnp.zeros_like(ahead_ref)
-        rest_ref[...] = jnp.zeros_like(rest_ref)
         chosen_ref[...] = jnp.zeros_like(chosen_ref)
+        share_ref[...] = jnp.zeros_like(share_ref)
         rows = widen(z, north_ref[z.own :])
-        forward_sums(z, rows, basis_ref, phase_ref, lhs_ref, rest_ref, beyond)
-        rest_ref[beyond, SPARE:HALF] = put_lane(
-            rest_ref[beyond, SPARE:HALF], KMAX - SPARE, kept[z.own :]
-        )
+        forward_sums(z, rows, basis_ref, phase_ref, lhs_ref, share_ref, slice(z.own, z.rows))
+        pack(share_ref[z.ahead :], rest_ref)
+        sorted_ref[...] = jnp.broadcast_to(kept, sorted_ref.shape)
 
 
 def arrival(arrived_ref, out_ref):
@@ -418,8 +456,9 @@
     @pl.when(on_polar_band(z))
     def _():
         number = column_of(row_ref, NUMBER)[: z.own].astype(jnp.int32)
-        sums_ref[: z.first] = sum(ref[...] for ref in firsts)
-        sums_ref[z.first :] = sum(ref[...] for ref in seconds)
+        second = round_up(z.own - z.first, 8)
+        sums_ref[: z.first] = unpack(sum(ref[...] for ref in firsts), z.first)
+        sums_ref[z.first :] = unpack(sum(ref[...] for ref in seconds), second)[: z.own - z.first]
         waves = coefficients(z, sums_ref[...], look_up(number, kept_ref))
         part = sector_part(z, waves, lax.axis_index("lon"))
         ordered = reorder(chosen_ref[: z.own], part)
@@ -434,9 +473,8 @@
     def _():
         send_ref[...] = jnp.zeros_like(send_ref)
         keep_ref[...] = jnp.zeros_like(keep_ref)
-        first = KMAX - SPARE
         left, right = (
-            jnp.concatenate([firsts[n][:, SPARE:HALF], seconds[n][:, SPARE:HALF]], axis=0)
+            jnp.concatenate([firsts[n][: z.first], seconds[n][: z.own - z.first]], axis=0)
             for n in (1, -1)
         )
         at_right = z.lon - (z.ext - 128)
@@ -445,9 +483,9 @@
             x = widen(z, flat_rows(z, ref))
             tail = x[:, z.ext - 128 :]
             for n, lane in enumerate(right_of):
-                tail = put_lane(tail, at_right + n, right[:, first + lane : first + lane + 1])
+                tail = put_lane(tail, at_right + n, right[:, lane : lane + 1])
             for n, lane in enumerate(left_of):
-                tail = put_lane(tail, 127 - n, left[:, first + lane : first + lane + 1])
+                tail = put_lane(tail, 127 - n, left[:, lane : lane + 1])
             return jnp.concatenate([x[:, : z.ext - 128], tail], axis=1)
 
         g = rimmed(g_ref, (1, 0), (4, 5))
@@ -460,43 +498,44 @@
     part_ref[...] = flat_rows(z, thick_ref) - change
 
 
-def send_spectra(z, east_ref, *rest):
-    shares, send_ref = rest[:-1], rest[-1]
-    kept = shares[0][:, KMAX : KMAX + 1]
-    coef = coefficients(z, sum(ref[...] for ref in shares), kept)
-    part = sector_part(z, coef, lax.axis_index("lon"))
+def ahead_waves(z, shares, sorted_ref):
+    sums = unpack(sum(ref[...] for ref in shares), z.ahead)
+    return coefficients(z, sums, sorted_ref[: z.ahead, MORE : MORE + 1])
+
+
+def send_spectra(z, east_ref, sorted_ref, *rest):
+    shares, send_ref, waves_ref = rest[:-2], rest[-2], rest[-1]
+    waves = ahead_waves(z, shares, sorted_ref)
+    waves_ref[...] = waves
+    part = sector_part(z, waves, lax.axis_index("lon"))
     send_ref[0] = east_ref[...]
     send_ref[1] = part[: z.helped].reshape(east_ref.shape)
 
 
-def ahead_inverse(z, phase_ref, *rest):
-    shares, (basis_ref, high_ref, low_ref, lhs_ref, rows_ref) = rest[: z.n_lon], rest[z.n_lon :]
-
+def ahead_inverse(z, phase_ref, waves_ref, basis_ref, high_ref, low_ref, lhs_ref, rows_ref):
     @pl.when(on_polar_band(z))
     def _():
-        kept = shares[0][:, KMAX : KMAX + 1]
-        waves = coefficients(z, sum(ref[...] for ref in shares), kept)
-        inverse_rows(z, waves, basis_ref, phase_ref, lhs_ref, rows_ref)
+        inverse_rows(z, waves_ref[...], basis_ref, phase_ref, lhs_ref, rows_ref)
         high_ref[...], low_ref[...] = split(rows_ref[...])
 
 
 def north_inverse(
-    z, active, depth_ref, north_ref, part_ref, row_ref, phase_ref, chosen_ref, high_ahead, low_ahead,
-    *rest,
+    z, active, depth_ref, north_ref, part_ref, row_ref, phase_ref, chosen_ref, sorted_ref, waves_ahead,
+    high_ahead, low_ahead, *rest,
 ):
-    ahead, shares, rest = rest[: z.n_lon], rest[z.n_lon : 2 * z.n_lon], rest[2 * z.n_lon :]
+    shares, rest = rest[: z.n_lon], rest[z.n_lon :]
     basis_ref, final_ref, thick_ref, column_ref, keep_ref, lhs_ref, rows_ref, high_ref, low_ref = rest
 
     @pl.when(active & on_polar_band(z))
     def _():
         more = z.ahead - 8
-        kept = [ahead[0][more:, KMAX : KMAX + 1], shares[0][:, KMAX : KMAX + 1]]
-        sums = [sum(ref[more:] for ref in ahead), sum(ref[...] for ref in shares)]
-        waves = coefficients(z, jnp.concatenate(sums, axis=0), jnp.concatenate(kept, axis=0))
-        part = sector_part(z, waves, lax.axis_index("lon"))
+        sums = unpack(sum(ref[...] for ref in shares), z.rows - z.ahead)
+        waves = coefficients(z, sums, sorted_ref[z.ahead :, MORE : MORE + 1])
+        both = jnp.concatenate([waves_ahead[more:], waves], axis=0)
+        part = sector_part(z, both, lax.axis_index("lon"))
         first = z.helped - more
         keep_ref[...] = part[first : first + z.helped].reshape(keep_ref.shape)
-        inverse_rows(z, waves[8:], basis_ref, phase_ref, lhs_ref, rows_ref, slice(z.rows - z.ahead))
+        inverse_rows(z, waves, basis_ref, phase_ref, lhs_ref, rows_ref, slice(z.rows - z.ahead))
         count = high_ref.shape[0] - z.ahead
         rest_high, rest_low = split(pad_rows(rows_ref[: z.rows - z.ahead], count))
         high_ref[: z.ahead], low_ref[: z.ahead] = high_ahead[...], low_ahead[...]
@@ -514,7 +553,8 @@
         keep_ref[...] = jnp.zeros_like(keep_ref)
         beyond = slice(z.own, z.rows)
         at = slice(z.own - z.ahead, z.rows - z.ahead)
-        waves = coefficients(z, sum(ref[at] for ref in shares), shares[0][at, KMAX : KMAX + 1])
+        sums = unpack(sum(ref[...] for ref in shares), z.rows - z.ahead)
+        waves = coefficients(z, sums[at], sorted_ref[beyond, MORE : MORE + 1])
         inverse_rows(z, waves, basis_ref, phase_ref, lhs_ref, rows_ref, beyond)
         polar = column_of(row_ref, POLAR)[beyond] > 0.0
         rows_ref[beyond, : z.lon] = jnp.where(polar, rows_ref[beyond, : z.lon], north_ref[beyond])
@@ -643,18 +683,23 @@
     share_first, to_even, to_odd, wind_east, wind_north, geopot, per_row, phase, forward = call(
         functools.partial(east_first, z),
         6,
-        [(z.first, WIDE), rims, rims]
+        [(packed_rows(z.first), 128), rims, rims]
         + [pltpu.VMEM(s, jnp.float32) for s in (field, field, field, row_shape, phase_shape)]
         + [pltpu.VMEM(forward.shape, forward.dtype)],
-        [columns_lhs, pltpu.SemaphoreType.DMA((12,))],
+        [
+            columns_lhs,
+            pltpu.VMEM((z.first, WIDE), jnp.float32),
+            pltpu.SemaphoreType.DMA((12,)),
+        ],
         1,
         {n: pltpu.HBM for n in range(6)},
     )(*pinned)
+    second = round_up(z.own - z.first, 8)
     (share_second,) = call(
         functools.partial(east_shares_of, z, slice(z.first, z.own)),
         6,
-        [(z.own - z.first, WIDE)],
-        [columns_lhs],
+        [(packed_rows(second), 128)],
+        [columns_lhs, pltpu.VMEM((second, WIDE), jnp.float32)],
         0.18,
     )(wind_east, wind_north, geopot, per_row, phase, forward)
     east_firsts, east_seconds = (
@@ -666,10 +711,16 @@
         met.append(lax.ppermute(rim, "lat", pairs + [(b, a) for a, b in pairs]))
 
     places = round_up(z.rows, 128)
-    north_ahead, north_rest, north_new, chosen = call(
+    north_ahead, north_rest, north_new, chosen, kept_sorted = call(
         functools.partial(north_forward, z),
         10,
-        [(z.ahead, WIDE), (z.rows - z.ahead, WIDE), (z.rows, z.lon), (z.rows, places)],
+        [
+            (packed_rows(z.ahead), 128),
+            (packed_rows(z.rows - z.ahead), 128),
+            (z.rows, z.lon),
+            (z.rows, places),
+            (z.rows, 128),
+        ],
         [
             pltpu.VMEM((z.rows, z.lon), jnp.float32),
             columns_lhs,
@@ -707,9 +758,9 @@
         first_here, *east_firsts, *east_seconds, inverse,
     )
 
-    (to_helper,) = call(
-        functools.partial(send_spectra, z), 1 + z.n_lon, [(2, *spec)], [], 0.1
-    )(east_send, *north_aheads)
+    to_helper, waves_ahead = call(
+        functools.partial(send_spectra, z), 2 + z.n_lon, [(2, *spec), (z.ahead, WIDE)], [], 0.1
+    )(east_send, kept_sorted, *north_aheads)
     arrived = lax.ppermute(
         to_helper, "lat", [(i, (i + z.half_axis) % z.n_lat) for i in polar_bands]
     )
@@ -717,15 +768,15 @@
     ahead_rows = jax.ShapeDtypeStruct((z.ahead, z.ext), jnp.bfloat16)
     ahead_high, ahead_low = call(
         functools.partial(ahead_inverse, z),
-        2 + z.n_lon,
+        3,
         [ahead_rows] * 2,
         [waves_lhs, pltpu.VMEM((z.ahead, z.ext), jnp.float32)],
         0.5,
-    )(phase, *north_aheads, inverse)
+    )(phase, waves_ahead, inverse)
 
     operands = (
-        mean_depth, north_new, thick_part, per_row, phase, chosen, ahead_high, ahead_low,
-        *north_aheads, *north_rests, inverse,
+        mean_depth, north_new, thick_part, per_row, phase, chosen, kept_sorted, waves_ahead,
+        ahead_high, ahead_low, *north_rests, inverse,
     )
     in_vmem = pltpu.VMEM(field, jnp.float32)
     scratch = [waves_lhs, pltpu.VMEM((z.rows, z.ext), jnp.float32)]

time: 40.2 us -> 39.4 us (0.980)
  starting transfers between devices: 13 us -> 11.8 us
    ppermute x1, starting transfers between devices: 2.06 us -> 1.48 us  [local(): lax.ppermute(to_helper, 'lat', [(i, (i + z.half_axis) % z.n_lat) for i in...]
    ppermute x2, starting transfers between devices: 2.05 us -> 1.47 us  [local(): met.append(lax.ppermute(rim, 'lat', pairs + [(b, a) for a, b in pairs]))]
  transfers between devices with their start and end apart: 8 -> 8, of which waited for: 3 -> 4; matrix products, arithmetic and copies ran while one was open for 0% -> 0% of each run, Pallas kernels for 38% -> 38%
where the time goes in v5:
time: 39.4 us; the launch traced here: 39.1 us
  Pallas kernels  20.8 us (53%)
  starting transfers between devices  11.8 us (30%)
  waiting for transfers between devices  5.49 us (14%)
  between operations  0.91 us (2%)
    ppermute x3, starting transfers between devices, shifted(): lax.ppermute(block, axis, [(i, (i + distance) % count) for i in range(cou...  4.56 us
    pallas_call x1, Pallas kernels, local(): call(functools.partial(east_first, z), 6, [(packed_rows(z.first), 128), r...  4.06 us
    pallas_call x1, Pallas kernels, local(): call(functools.partial(east_inverse, z), 11 + 2 * z.n_lon, [field, (z.own...  4.03 us
    pallas_call x1, Pallas kernels, local(): call(functools.partial(north_shallowest, z), 3 + len(operands), [in_vmem,...  3.91 us
    pallas_call x1, Pallas kernels, local(): call(functools.partial(north_forward, z), 10, [(packed_rows(z.ahead), 128...  3.62 us
    ppermute x1, starting transfers between devices, local(): north_aheads.append(lax.ppermute(north_ahead, ('lat', 'lon'), route))  3.03 us
    ppermute x3, waiting for transfers between devices, shifted(): lax.ppermute(block, axis, [(i, (i + distance) % count) for i in range(cou...  2.93 us
    ppermute x1, waiting for transfers between devices, local(): north_aheads.append(lax.ppermute(north_ahead, ('lat', 'lon'), route))  2.16 us
  transfers between devices with their start and end apart: 8, of which 4 were waited for; matrix products, arithmetic and copies ran while one was open for 0% of the time, Pallas kernels for 38%

profile of v5, /device:TPU:0, one launch (start us, length us, event | category | flops | bytes accessed | tf_op | source)
XLA Modules:
  0.0 39.1 jit_solution(321153899031400540)
XLA Ops:
  0.6 4.1 %shard_map.155 = (f32[456,128]{1,0:T(8,128)S(1)}, f32[8,1440]{1,0:T(8,128)S(1)}, f32[8,1440]{1,0:T(8,128)S(1)}, f32[90,2,1440]{2,1,0:T(2,128)S(1)}, f32[90,2,144...) custom-call(f32[90,2,1440]{2,1,0:T(2,128)} %bitcast.15, ...), custom_call_target="tpu_custom_call" | custom-call | flops 1150000000 | tf_op jit(solution)/shard_map/pallas_call | solution.py:683
  4.7 3.0 %collective-permute-start.2 = (f32[456,128]{1,0:T(8,128)S(1)}, f32[456,128]{1,0:T(8,128)S(1)}, u32[]{:S(2)}, u32[]{:S(2)}) collective-permute-start(f32[456,128]{1,0:T(8,128)S(1)} %get-tuple-element.46.rest_0_), channel_id=1, source_target_pairs={{0,2},{2,0},{1,3},{3,1},{4,6},{6,4},{5,7},{7,5},{8,10},{10,8},{9,1... | collective-permute-start | bytes 700424 | tf_op jit(solution)/shard_map/ppermute | solution.py:650
  7.7 0.8 %collective-permute-start = (f32[8,1440]{1,0:T(8,128)S(1)}, f32[8,1440]{1,0:T(8,128)S(1)}, u32[]{:S(2)}, u32[]{:S(2)}) collective-permute-start(f32[8,1440]{1,0:T(8,128)S(1)} %get-tuple-element.42), channel_id=1, source_target_pairs={{0,4},{8,12},{4,0},{12,8},{1,5},{9,13},{5,1},{13,9},{2,6},{10,14},... | collective-permute-start | bytes 138248 | tf_op jit(solution)/shard_map/ppermute | solution.py:711
  8.5 0.0 copy-start.3
  8.5 0.0 copy-start.4
  8.5 1.6 %shard_map.158.rest_2_ = f32[592,128]{1,0:T(8,128)S(1)} custom-call(f32[90,2,1440]{2,1,0:T(2,128)S(1)} %get-tuple-element.37.we_ref, f32[90,2,1440]{2,1,0:T(2,128)S(1)} %get-tuple-element.38.wn_ref, f32[90,2,1440]{2,1,0:T(2,128)S(1)} %get-tuple-element.39.g_ref, f32[184,8]{1,0:T(8,128)S(1)} %get-tuple-element.40.row_ref.refs_3_.rest_3_, ...), custom_call_target="tpu_custom_call" | custom-call | flops 207000000 | tf_op jit(solution)/shard_map/pallas_call | solution.py:698
  10.2 0.6 %collective-permute-start.3 = (f32[592,128]{1,0:T(8,128)S(1)}, f32[592,128]{1,0:T(8,128)S(1)}, u32[]{:S(2)}, u32[]{:S(2)}) collective-permute-start(f32[592,128]{1,0:T(8,128)S(1)} %shard_map.158.rest_2_), channel_id=1, source_target_pairs={{0,2},{2,0},{1,3},{3,1},{4,6},{6,4},{5,7},{7,5},{8,10},{10,8},{9,1... | collective-permute-start | bytes 909320 | tf_op jit(solution)/shard_map/ppermute | solution.py:650
  10.7 0.7 %collective-permute-start.1 = (f32[8,1440]{1,0:T(8,128)S(1)}, f32[8,1440]{1,0:T(8,128)S(1)}, u32[]{:S(2)}, u32[]{:S(2)}) collective-permute-start(f32[8,1440]{1,0:T(8,128)S(1)} %get-tuple-element.43), channel_id=1, source_target_pairs={{4,8},{8,4},{5,9},{9,5},{6,10},{10,6},{7,11},{11,7},{20,24},{24,20... | collective-permute-start | bytes 138248 | tf_op jit(solution)/shard_map/ppermute | solution.py:711
  11.4 0.4 collective-permute-done.even_ref
  11.8 0.0 collective-permute-done.1.odd_ref
  11.8 0.0 copy-done.3
  11.8 0.0 copy-done.4
  11.8 0.0 copy-start.1
  11.8 3.6 %shard_map.156 = (f32[544,128]{1,0:T(8,128)S(1)}, f32[504,128]{1,0:T(8,128)S(1)}, f32[184,1440]{1,0:T(8,128)S(1)}, f32[184,256]{1,0:T(8,128)S(1)}, f32[184,128]{1,0:T(8,128)S(1)}) custom-call(f32[90,2,1440]{2,1,0:T(2,128)S(1)} %get-tuple-element.37.we_ref, f32[90,2,1440]{2,1,0:T(2,128)S(1)} %get-tuple-element.38.wn_ref, ...), custom_call_target="tpu_custom_call" | custom-call | flops 920000000 | tf_op jit(solution)/shard_map/pallas_call | solution.py:714
  15.4 3.0 %collective-permute-start.4 = (f32[544,128]{1,0:T(8,128)S(1)}, f32[544,128]{1,0:T(8,128)S(1)}, u32[]{:S(2)}, u32[]{:S(2)}) collective-permute-start(f32[544,128]{1,0:T(8,128)S(1)} %get-tuple-element.52.rest_0_), channel_id=1, source_target_pairs={{0,2},{2,0},{12,14},{14,12},{1,3},{3,1},{13,15},{15,13},{16,18},{1... | collective-permute-start | bytes 835592 | tf_op jit(solution)/shard_map/ppermute | solution.py:742
  18.5 0.0 copy-start
  18.5 0.0 copy-start.5
  18.5 1.0 %collective-permute-start.5 = (f32[504,128]{1,0:T(8,128)S(1)}, f32[504,128]{1,0:T(8,128)S(1)}, u32[]{:S(2)}, u32[]{:S(2)}) collective-permute-start(f32[504,128]{1,0:T(8,128)S(1)} %get-tuple-element.56.refs_10_.rest_10_), channel_id=1, source_target_pairs={{0,2},{2,0},{1,3},{3,1},{4,6},{6,4},{5,7},{7,5},{8,10},{10,8},{9,1... | collective-permute-start | bytes 774152 | tf_op jit(solution)/shard_map/ppermute | solution.py:650
  19.5 0.0 collective-permute-done.2.arrived_ref.rest_1_
  19.5 1.2 %collective-permute-done.3.rest_3_ = f32[592,128]{1,0:T(8,128)S(1)} collective-permute-done((f32[592,128]{1,0:T(8,128)S(1)}, f32[592,128]{1,0:T(8,128)S(1)}, u32[]{:S(2)}, u32[]{:S(2)}) %collective-permute-start.3) | collective-permute-done | bytes 303136 | tf_op jit(solution)/shard_map/ppermute | solution.py:650
  20.7 0.0 copy-done.1
  20.7 0.0 copy-done
  20.7 0.0 copy-done.5
  20.7 4.0 %shard_map.159 = (f32[90,2,1440]{2,1,0:T(2,128)}, f32[180,1440]{1,0:T(8,128)S(1)}, f32[45,2,360]{2,1,0:T(2,128)S(1)}, f32[45,2,360]{2,1,0:T(2,128)S(1)}) custom-call(f32[2]{0:T(128)S(1)} %copy-done.5, f32[90,2,1440]{2,1,0:T(2,128)S(1)} %get-tuple-element.37.we_ref, f32[90,2,1440]{2,1,0:T(2,128)S(1)} %get-tuple-element.38.wn_ref, ...), custom_call_target="tpu_custom_call" | custom-call | flops 1150000000 | tf_op jit(solution)/shard_map/pallas_call | solution.py:745
  24.8 2.2 %collective-permute-done.4.rest_1_ = f32[544,128]{1,0:T(8,128)S(1)} collective-permute-done((f32[544,128]{1,0:T(8,128)S(1)}, f32[544,128]{1,0:T(8,128)S(1)}, u32[]{:S(2)}, u32[]{:S(2)}) %collective-permute-start.4) | collective-permute-done | bytes 278560 | tf_op jit(solution)/shard_map/ppermute | solution.py:742
  26.9 0.2 shard_map.160
  27.1 1.5 %collective-permute-start.6 = (f32[2,45,2,360]{3,2,1,0:T(2,128)S(1)}, f32[2,45,2,360]{3,2,1,0:T(2,128)S(1)}, u32[]{:S(2)}, u32[]{:S(2)}) collective-permute-start(f32[2,45,2,360]{3,2,1,0:T(2,128)S(1)} %get-tuple-element.61), channel_id=1, source_target_pairs={{0,8},{12,4},{1,9},{13,5},{2,10},{14,6},{3,11},{15,7},{16,24},{28,... | collective-permute-start | bytes 777608 | tf_op jit(solution)/shard_map/ppermute | solution.py:764
  28.6 1.1 %shard_map.161 = (bf16[96,1536]{1,0:T(8,128)(2,1)S(1)}, bf16[96,1536]{1,0:T(8,128)(2,1)S(1)}) custom-call(f32[16,384]{1,0:T(8,128)S(1)} %get-tuple-element.41.phase_ref.refs_4_.rest_4_, f32[96,768]{1,0:T(8,128)S(1)} %get-tuple-element.53.waves_ref.refs_7_.rest_7_, bf16[2304,768]{1,0:T(8,128)(2,1)S(1)} %copy-done), custom_call_target="tpu_custom_call" | custom-call | flops 575000000 | tf_op jit(solution)/shard_map/pallas_call | solution.py:769
  29.7 1.7 %collective-permute-done.5.refs_11_.rest_11_ = f32[504,128]{1,0:T(8,128)S(1)} collective-permute-done((f32[504,128]{1,0:T(8,128)S(1)}, f32[504,128]{1,0:T(8,128)S(1)}, u32[]{:S(2)}, u32[]{:S(2)}) %collective-permute-start.5) | collective-permute-done | bytes 258080 | tf_op jit(solution)/shard_map/ppermute | solution.py:650
  31.4 0.6 %shard_map.162 = (f32[90,2,1440]{2,1,0:T(2,128)S(1)}, f32[90,2,1440]{2,1,0:T(2,128)S(1)}, f32[90,1440]{1,0:T(8,128)S(1)}, f32[45,2,360]{2,1,0:T(2,128)S(1)}) custom-call(f32[2]{0:T(128)S(1)} %copy-done.5, f32[184,1440]{1,0:T(8,128)S(1)} %get-tuple-element.48.refs_1_.rest_1_, f32[180,1440]{1,0:T(8,128)S(1)} %get-tuple-element.49.refs_2_.rest_2_, ...), custom_call_target="tpu_custom_call" | custom-call | flops 2300000000 | tf_op jit(solution)/shard_map/pallas_call | solution.py:784
  32.0 1.3 %collective-permute-start.7 = (f32[90,1440]{1,0:T(8,128)S(1)}, f32[90,1440]{1,0:T(8,128)S(1)}, u32[]{:S(2)}, u32[]{:S(2)}) collective-permute-start(f32[90,1440]{1,0:T(8,128)S(1)} %get-tuple-element.64), channel_id=1, source_target_pairs={{1,0},{3,2},{5,4},{7,6},{9,8},{11,10},{13,12},{15,14},{17,16},{19,... | collective-permute-start | bytes 1555208 | tf_op jit(solution)/shard_map/ppermute | solution.py:793
  33.3 0.0 collective-permute-done.6.arrived_ref
  33.3 0.0 copy-start.2
  33.3 3.9 %shard_map.163 = (f32[90,2,1440]{2,1,0:T(2,128)S(1)}, f32[90,2,1440]{2,1,0:T(2,128)S(1)}, f32[2,45,2,360]{3,2,1,0:T(2,128)}) custom-call(f32[45,2,360]{2,1,0:T(2,128)S(1)} %get-tuple-element.59.east_keep, f32[45,2,360]{2,1,0:T(2,128)S(1)} %get-tuple-element.60.north_keep, f32[2,45,2,360]{3,2,1,0:T(2,128)S(1)} %collective-permute-done.6.arrived_ref, ...), custom_call_target="tpu_custom_call" | custom-call | flops 3680000000 | tf_op jit(solution)/shard_map/pallas_call | solution.py:796
  37.2 0.0 collective-permute-done.7.rest_4_
  37.2 0.0 copy-done.2
  37.2 1.7 %shard_map.164 = (f32[90,2,1440]{2,1,0:T(2,128)}, f32[90,2,1440]{2,1,0:T(2,128)}, f32[90,2,1440]{2,1,0:T(2,128)}) custom-call(f32[90,1440]{1,0:T(8,128)S(1)} %copy-done.2, f32[90,2,1440]{2,1,0:T(2,128)S(1)} %get-tuple-element.57.rest_0_, f32[90,2,1440]{2,1,0:T(2,128)S(1)} %get-tuple-element.58.rest_1_, f32[90,2,1440]{2,1,0:T(2,128)S(1)} %get-tuple-element.62.rest_2_, ...), custom_call_target="tpu_custom_call" | custom-call | flops 1150000000 | tf_op jit(solution)/shard_map/pallas_call | solution.py:804
  (1 shorter events, 0.0 us)
Async XLA Ops:
  4.7 14.8 %collective-permute-start.2 = (f32[456,128]{1,0:T(8,128)S(1)}, f32[456,128]{1,0:T(8,128)S(1)}, u32[]{:S(2)}, u32[]{:S(2)}) collective-permute-start(f32[456,128]{1,0:T(8,128)S(1)} %get-tuple-element.46.rest_0_), channel_id=1, source_target_pairs={{0,2},{2,0},{1,3},{3,1},{4,6},{6,4},{5,7},{7,5},{8,10},{10,8},{9,1... | collective-permute-start | bytes 700424 | tf_op jit(solution)/shard_map/ppermute | solution.py:650
  7.7 4.1 %collective-permute-start = (f32[8,1440]{1,0:T(8,128)S(1)}, f32[8,1440]{1,0:T(8,128)S(1)}, u32[]{:S(2)}, u32[]{:S(2)}) collective-permute-start(f32[8,1440]{1,0:T(8,128)S(1)} %get-tuple-element.42), channel_id=1, source_target_pairs={{0,4},{8,12},{4,0},{12,8},{1,5},{9,13},{5,1},{13,9},{2,6},{10,14},... | collective-permute-start | bytes 138248 | tf_op jit(solution)/shard_map/ppermute | solution.py:711
  8.5 3.3 %copy-start.3 = (s32[180]{0:T(256)S(1)}, s32[180]{0:T(256)}, u32[]{:S(2)}) copy-start(s32[180]{0:T(256)} %param.18) | copy-start | bytes 2164
  8.5 3.3 %copy-start.4 = (s32[180]{0:T(256)S(1)}, s32[180]{0:T(256)}, u32[]{:S(2)}) copy-start(s32[180]{0:T(256)} %param.19) | copy-start | bytes 2164
  10.2 10.6 %collective-permute-start.3 = (f32[592,128]{1,0:T(8,128)S(1)}, f32[592,128]{1,0:T(8,128)S(1)}, u32[]{:S(2)}, u32[]{:S(2)}) collective-permute-start(f32[592,128]{1,0:T(8,128)S(1)} %shard_map.158.rest_2_), channel_id=1, source_target_pairs={{0,2},{2,0},{1,3},{3,1},{4,6},{6,4},{5,7},{7,5},{8,10},{10,8},{9,1... | collective-permute-start | bytes 909320 | tf_op jit(solution)/shard_map/ppermute | solution.py:650
  10.7 1.1 %collective-permute-start.1 = (f32[8,1440]{1,0:T(8,128)S(1)}, f32[8,1440]{1,0:T(8,128)S(1)}, u32[]{:S(2)}, u32[]{:S(2)}) collective-permute-start(f32[8,1440]{1,0:T(8,128)S(1)} %get-tuple-element.43), channel_id=1, source_target_pairs={{4,8},{8,4},{5,9},{9,5},{6,10},{10,6},{7,11},{11,7},{20,24},{24,20... | collective-permute-start | bytes 138248 | tf_op jit(solution)/shard_map/ppermute | solution.py:711
  11.8 8.9 %copy-start.1 = (f32[2,90,1440]{2,0,1:T(2,128)S(1)}, f32[2,90,1440]{2,0,1:T(2,128)}, u32[]{:S(2)}) copy-start(f32[2,90,1440]{2,0,1:T(2,128)} %param.14) | copy-start | bytes 3110404
  15.4 11.5 %collective-permute-start.4 = (f32[544,128]{1,0:T(8,128)S(1)}, f32[544,128]{1,0:T(8,128)S(1)}, u32[]{:S(2)}, u32[]{:S(2)}) collective-permute-start(f32[544,128]{1,0:T(8,128)S(1)} %get-tuple-element.52.rest_0_), channel_id=1, source_target_pairs={{0,2},{2,0},{12,14},{14,12},{1,3},{3,1},{13,15},{15,13},{16,18},{1... | collective-permute-start | bytes 835592 | tf_op jit(solution)/shard_map/ppermute | solution.py:742
  18.5 2.2 %copy-start = (bf16[2304,768]{1,0:T(8,128)(2,1)S(1)}, bf16[2304,768]{1,0:T(8,128)(2,1)}, u32[]{:S(2)}) copy-start(bf16[2304,768]{1,0:T(8,128)(2,1)} %constant.9.clone.rest_4_.basis_ref.refs_12_.rest_12_) | copy-start | bytes 10616836
  18.5 2.2 %copy-start.5 = (f32[2]{0:T(128)S(1)}, f32[2]{0:T(128)}, u32[]{:S(2)}) copy-start(f32[2]{0:T(128)} %rest_0_.1) | copy-start | bytes 28
  18.5 12.9 %collective-permute-start.5 = (f32[504,128]{1,0:T(8,128)S(1)}, f32[504,128]{1,0:T(8,128)S(1)}, u32[]{:S(2)}, u32[]{:S(2)}) collective-permute-start(f32[504,128]{1,0:T(8,128)S(1)} %get-tuple-element.56.refs_10_.rest_10_), channel_id=1, source_target_pairs={{0,2},{2,0},{1,3},{3,1},{4,6},{6,4},{5,7},{7,5},{8,10},{10,8},{9,1... | collective-permute-start | bytes 774152 | tf_op jit(solution)/shard_map/ppermute | solution.py:650
  27.1 6.1 %collective-permute-start.6 = (f32[2,45,2,360]{3,2,1,0:T(2,128)S(1)}, f32[2,45,2,360]{3,2,1,0:T(2,128)S(1)}, u32[]{:S(2)}, u32[]{:S(2)}) collective-permute-start(f32[2,45,2,360]{3,2,1,0:T(2,128)S(1)} %get-tuple-element.61), channel_id=1, source_target_pairs={{0,8},{12,4},{1,9},{13,5},{2,10},{14,6},{3,11},{15,7},{16,24},{28,... | collective-permute-start | bytes 777608 | tf_op jit(solution)/shard_map/ppermute | solution.py:764
  32.0 5.2 %collective-permute-start.7 = (f32[90,1440]{1,0:T(8,128)S(1)}, f32[90,1440]{1,0:T(8,128)S(1)}, u32[]{:S(2)}, u32[]{:S(2)}) collective-permute-start(f32[90,1440]{1,0:T(8,128)S(1)} %get-tuple-element.64), channel_id=1, source_target_pairs={{1,0},{3,2},{5,4},{7,6},{9,8},{11,10},{13,12},{15,14},{17,16},{19,... | collective-permute-start | bytes 1555208 | tf_op jit(solution)/shard_map/ppermute | solution.py:793
  33.3 3.9 %copy-start.2 = (f32[90,1440]{1,0:T(8,128)S(1)}, f32[90,1440]{1,0:T(8,128)}, u32[]{:S(2)}) copy-start(f32[90,1440]{1,0:T(8,128)} %surface_ref.1) | copy-start | bytes 1555204

commit v6 on v5

--- a/solution.py
+++ b/solution.py
@@ -370,12 +370,12 @@
         copy.start()
     for copy in first + tables:
         copy.wait()
+    for copy in between:
+        copy.start()
 
     def basis_here():
         for copy in basis + edge:
             copy.wait()
-        for copy in between:
-            copy.start()
 
     east_shares_of(
         z, slice(0, z.first), we_ref, wn_ref, g_ref, row_ref, phase_ref, basis_ref, share_ref, lhs_ref,
@@ -540,7 +540,7 @@
         rest_high, rest_low = split(pad_rows(rows_ref[: z.rows - z.ahead], count))
         high_ref[: z.ahead], low_ref[: z.ahead] = high_ahead[...], low_ahead[...]
         high_ref[z.ahead :], low_ref[z.ahead :] = rest_high, rest_low
-        chosen = chosen_ref[...].astype(jnp.bfloat16)
+        chosen = chosen_ref[:, : z.mm_rows].astype(jnp.bfloat16)
         rows_ref[...] = jnp.dot(
             chosen, high_ref[...], preferred_element_type=jnp.float32
         ) + jnp.dot(chosen, low_ref[...], preferred_element_type=jnp.float32)
@@ -780,7 +780,7 @@
     )
     in_vmem = pltpu.VMEM(field, jnp.float32)
     scratch = [waves_lhs, pltpu.VMEM((z.rows, z.ext), jnp.float32)]
-    scratch += [pltpu.VMEM((places, z.ext), jnp.bfloat16)] * 2
+    scratch += [pltpu.VMEM((z.mm_rows, z.ext), jnp.bfloat16)] * 2
     final_deeper, thick_deeper, column, north_keep = call(
         functools.partial(north_deeper, z),
         len(operands),

time: 39.4 us -> 38.4 us (0.975)
  waiting for transfers between devices: 5.49 us -> 4.36 us
  Pallas kernels: 20.8 us -> 19.8 us
  local copies, waits for them, and re-layouts: 0.03 us -> 0.67 us
  starting transfers between devices: 11.8 us -> 12.3 us
    pallas_call x1, Pallas kernels: 4.06 us -> 3.06 us  [local(): call(functools.partial(east_first, z), 6, [(packed_rows(z.first), 128), r...]
    ppermute x2, starting transfers between devices: 1.47 us -> 2.14 us  [local(): met.append(lax.ppermute(rim, 'lat', pairs + [(b, a) for a, b in pairs]))]
    ppermute x3, waiting for transfers between devices: 2.93 us -> 2.29 us  [shifted(): lax.ppermute(block, axis, [(i, (i + distance) % count) for i in range(cou...]
    unnamed x12, local copies, waits for them, and re-layouts: 0.03 us -> 0.67 us
  transfers between devices with their start and end apart: 8 -> 8, of which waited for: 4 -> 3; matrix products, arithmetic and copies ran while one was open for 0% -> 0% of each run, Pallas kernels for 38% -> 39%
where the time goes in v6:
time: 38.4 us; the launch traced here: 38.1 us
  Pallas kernels  19.8 us (52%)
  starting transfers between devices  12.3 us (32%)
  waiting for transfers between devices  4.36 us (11%)
  between operations  0.94 us (2%)
  local copies, waits for them, and re-layouts  0.67 us (2%)
    ppermute x3, starting transfers between devices, shifted(): lax.ppermute(block, axis, [(i, (i + distance) % count) for i in range(cou...  4.18 us
    pallas_call x1, Pallas kernels, local(): call(functools.partial(east_inverse, z), 11 + 2 * z.n_lon, [field, (z.own...  4.02 us
    pallas_call x1, Pallas kernels, local(): call(functools.partial(north_shallowest, z), 3 + len(operands), [in_vmem,...  3.92 us
    pallas_call x1, Pallas kernels, local(): call(functools.partial(north_forward, z), 10, [(packed_rows(z.ahead), 128...  3.62 us
    ppermute x1, starting transfers between devices, local(): north_aheads.append(lax.ppermute(north_ahead, ('lat', 'lon'), route))  3.39 us
    pallas_call x1, Pallas kernels, local(): call(functools.partial(east_first, z), 6, [(packed_rows(z.first), 128), r...  3.06 us
    ppermute x3, waiting for transfers between devices, shifted(): lax.ppermute(block, axis, [(i, (i + distance) % count) for i in range(cou...  2.29 us
    ppermute x2, starting transfers between devices, local(): met.append(lax.ppermute(rim, 'lat', pairs + [(b, a) for a, b in pairs]))  2.14 us
  transfers between devices with their start and end apart: 8, of which 3 were waited for; matrix products, arithmetic and copies ran while one was open for 0% of the time, Pallas kernels for 39%

profile of v6, /device:TPU:0, one launch (start us, length us, event | category | flops | bytes accessed | tf_op | source)
XLA Modules:
  0.0 38.1 jit_solution(17190981542123781826)
XLA Ops:
  0.6 3.1 %shard_map.155 = (f32[456,128]{1,0:T(8,128)S(1)}, f32[8,1440]{1,0:T(8,128)S(1)}, f32[8,1440]{1,0:T(8,128)S(1)}, f32[90,2,1440]{2,1,0:T(2,128)S(1)}, f32[90,2,144...) custom-call(f32[90,2,1440]{2,1,0:T(2,128)} %bitcast.15, ...), custom_call_target="tpu_custom_call" | custom-call | flops 1150000000 | tf_op jit(solution)/shard_map/pallas_call | solution.py:683
  3.7 3.0 %collective-permute-start.2 = (f32[456,128]{1,0:T(8,128)S(1)}, f32[456,128]{1,0:T(8,128)S(1)}, u32[]{:S(2)}, u32[]{:S(2)}) collective-permute-start(f32[456,128]{1,0:T(8,128)S(1)} %get-tuple-element.46.rest_0_), channel_id=1, source_target_pairs={{0,2},{2,0},{1,3},{3,1},{4,6},{6,4},{5,7},{7,5},{8,10},{10,8},{9,1... | collective-permute-start | bytes 700424 | tf_op jit(solution)/shard_map/ppermute | solution.py:650
  6.7 1.5 %collective-permute-start = (f32[8,1440]{1,0:T(8,128)S(1)}, f32[8,1440]{1,0:T(8,128)S(1)}, u32[]{:S(2)}, u32[]{:S(2)}) collective-permute-start(f32[8,1440]{1,0:T(8,128)S(1)} %get-tuple-element.42), channel_id=1, source_target_pairs={{0,4},{8,12},{4,0},{12,8},{1,5},{9,13},{5,1},{13,9},{2,6},{10,14},... | collective-permute-start | bytes 138248 | tf_op jit(solution)/shard_map/ppermute | solution.py:711
  8.2 0.0 copy-start.3
  8.2 0.0 copy-start.4
  8.2 1.6 %shard_map.158.rest_2_ = f32[592,128]{1,0:T(8,128)S(1)} custom-call(f32[90,2,1440]{2,1,0:T(2,128)S(1)} %get-tuple-element.37.we_ref, f32[90,2,1440]{2,1,0:T(2,128)S(1)} %get-tuple-element.38.wn_ref, f32[90,2,1440]{2,1,0:T(2,128)S(1)} %get-tuple-element.39.g_ref, f32[184,8]{1,0:T(8,128)S(1)} %get-tuple-element.40.row_ref.refs_3_.rest_3_, ...), custom_call_target="tpu_custom_call" | custom-call | flops 207000000 | tf_op jit(solution)/shard_map/pallas_call | solution.py:698
  9.8 0.6 %collective-permute-start.3 = (f32[592,128]{1,0:T(8,128)S(1)}, f32[592,128]{1,0:T(8,128)S(1)}, u32[]{:S(2)}, u32[]{:S(2)}) collective-permute-start(f32[592,128]{1,0:T(8,128)S(1)} %shard_map.158.rest_2_), channel_id=1, source_target_pairs={{0,2},{2,0},{1,3},{3,1},{4,6},{6,4},{5,7},{7,5},{8,10},{10,8},{9,1... | collective-permute-start | bytes 909320 | tf_op jit(solution)/shard_map/ppermute | solution.py:650
  10.4 0.7 %collective-permute-start.1 = (f32[8,1440]{1,0:T(8,128)S(1)}, f32[8,1440]{1,0:T(8,128)S(1)}, u32[]{:S(2)}, u32[]{:S(2)}) collective-permute-start(f32[8,1440]{1,0:T(8,128)S(1)} %get-tuple-element.43), channel_id=1, source_target_pairs={{4,8},{8,4},{5,9},{9,5},{6,10},{10,6},{7,11},{11,7},{20,24},{24,20... | collective-permute-start | bytes 138248 | tf_op jit(solution)/shard_map/ppermute | solution.py:711
  11.1 0.0 collective-permute-done.even_ref
  11.1 0.0 collective-permute-done.1.odd_ref
  11.1 0.0 copy-done.3
  11.1 0.0 copy-done.4
  11.1 0.0 copy-start.1
  11.1 3.6 %shard_map.156 = (f32[544,128]{1,0:T(8,128)S(1)}, f32[504,128]{1,0:T(8,128)S(1)}, f32[184,1440]{1,0:T(8,128)S(1)}, f32[184,256]{1,0:T(8,128)S(1)}, f32[184,128]{1,0:T(8,128)S(1)}) custom-call(f32[90,2,1440]{2,1,0:T(2,128)S(1)} %get-tuple-element.37.we_ref, f32[90,2,1440]{2,1,0:T(2,128)S(1)} %get-tuple-element.38.wn_ref, ...), custom_call_target="tpu_custom_call" | custom-call | flops 920000000 | tf_op jit(solution)/shard_map/pallas_call | solution.py:714
  14.7 3.4 %collective-permute-start.4 = (f32[544,128]{1,0:T(8,128)S(1)}, f32[544,128]{1,0:T(8,128)S(1)}, u32[]{:S(2)}, u32[]{:S(2)}) collective-permute-start(f32[544,128]{1,0:T(8,128)S(1)} %get-tuple-element.52.rest_0_), channel_id=1, source_target_pairs={{0,2},{2,0},{12,14},{14,12},{1,3},{3,1},{13,15},{15,13},{16,18},{1... | collective-permute-start | bytes 835592 | tf_op jit(solution)/shard_map/ppermute | solution.py:742
  18.1 0.0 copy-start
  18.2 0.0 copy-start.5
  18.2 0.6 %collective-permute-start.5 = (f32[504,128]{1,0:T(8,128)S(1)}, f32[504,128]{1,0:T(8,128)S(1)}, u32[]{:S(2)}, u32[]{:S(2)}) collective-permute-start(f32[504,128]{1,0:T(8,128)S(1)} %get-tuple-element.56.refs_10_.rest_10_), channel_id=1, source_target_pairs={{0,2},{2,0},{1,3},{3,1},{4,6},{6,4},{5,7},{7,5},{8,10},{10,8},{9,1... | collective-permute-start | bytes 774152 | tf_op jit(solution)/shard_map/ppermute | solution.py:650
  18.8 0.0 collective-permute-done.2.arrived_ref.rest_1_
  18.8 0.7 %collective-permute-done.3.rest_3_ = f32[592,128]{1,0:T(8,128)S(1)} collective-permute-done((f32[592,128]{1,0:T(8,128)S(1)}, f32[592,128]{1,0:T(8,128)S(1)}, u32[]{:S(2)}, u32[]{:S(2)}) %collective-permute-start.3) | collective-permute-done | bytes 303136 | tf_op jit(solution)/shard_map/ppermute | solution.py:650
  19.5 0.0 copy-done.1
  19.5 0.6 %copy-done = bf16[2304,768]{1,0:T(8,128)(2,1)S(1)} copy-done((bf16[2304,768]{1,0:T(8,128)(2,1)S(1)}, bf16[2304,768]{1,0:T(8,128)(2,1)}, u32[]{:S(2)}) %copy-start) | copy-done | bytes 3538968
  20.1 0.0 copy-done.5
  20.1 4.0 %shard_map.159 = (f32[90,2,1440]{2,1,0:T(2,128)}, f32[180,1440]{1,0:T(8,128)S(1)}, f32[45,2,360]{2,1,0:T(2,128)S(1)}, f32[45,2,360]{2,1,0:T(2,128)S(1)}) custom-call(f32[2]{0:T(128)S(1)} %copy-done.5, f32[90,2,1440]{2,1,0:T(2,128)S(1)} %get-tuple-element.37.we_ref, f32[90,2,1440]{2,1,0:T(2,128)S(1)} %get-tuple-element.38.wn_ref, ...), custom_call_target="tpu_custom_call" | custom-call | flops 1150000000 | tf_op jit(solution)/shard_map/pallas_call | solution.py:745
  24.2 2.1 %collective-permute-done.4.rest_1_ = f32[544,128]{1,0:T(8,128)S(1)} collective-permute-done((f32[544,128]{1,0:T(8,128)S(1)}, f32[544,128]{1,0:T(8,128)S(1)}, u32[]{:S(2)}, u32[]{:S(2)}) %collective-permute-start.4) | collective-permute-done | bytes 278560 | tf_op jit(solution)/shard_map/ppermute | solution.py:742
  26.2 0.2 shard_map.160
  26.4 1.3 %collective-permute-start.6 = (f32[2,45,2,360]{3,2,1,0:T(2,128)S(1)}, f32[2,45,2,360]{3,2,1,0:T(2,128)S(1)}, u32[]{:S(2)}, u32[]{:S(2)}) collective-permute-start(f32[2,45,2,360]{3,2,1,0:T(2,128)S(1)} %get-tuple-element.61), channel_id=1, source_target_pairs={{0,8},{12,4},{1,9},{13,5},{2,10},{14,6},{3,11},{15,7},{16,24},{28,... | collective-permute-start | bytes 777608 | tf_op jit(solution)/shard_map/ppermute | solution.py:764
  27.7 1.1 %shard_map.161 = (bf16[96,1536]{1,0:T(8,128)(2,1)S(1)}, bf16[96,1536]{1,0:T(8,128)(2,1)S(1)}) custom-call(f32[16,384]{1,0:T(8,128)S(1)} %get-tuple-element.41.phase_ref.refs_4_.rest_4_, f32[96,768]{1,0:T(8,128)S(1)} %get-tuple-element.53.waves_ref.refs_7_.rest_7_, bf16[2304,768]{1,0:T(8,128)(2,1)S(1)} %copy-done), custom_call_target="tpu_custom_call" | custom-call | flops 575000000 | tf_op jit(solution)/shard_map/pallas_call | solution.py:769
  28.8 1.6 %collective-permute-done.5.refs_11_.rest_11_ = f32[504,128]{1,0:T(8,128)S(1)} collective-permute-done((f32[504,128]{1,0:T(8,128)S(1)}, f32[504,128]{1,0:T(8,128)S(1)}, u32[]{:S(2)}, u32[]{:S(2)}) %collective-permute-start.5) | collective-permute-done | bytes 258080 | tf_op jit(solution)/shard_map/ppermute | solution.py:650
  30.4 0.6 %shard_map.162 = (f32[90,2,1440]{2,1,0:T(2,128)S(1)}, f32[90,2,1440]{2,1,0:T(2,128)S(1)}, f32[90,1440]{1,0:T(8,128)S(1)}, f32[45,2,360]{2,1,0:T(2,128)S(1)}) custom-call(f32[2]{0:T(128)S(1)} %copy-done.5, f32[184,1440]{1,0:T(8,128)S(1)} %get-tuple-element.48.refs_1_.rest_1_, f32[180,1440]{1,0:T(8,128)S(1)} %get-tuple-element.49.refs_2_.rest_2_, ...), custom_call_target="tpu_custom_call" | custom-call | flops 2300000000 | tf_op jit(solution)/shard_map/pallas_call | solution.py:784
  31.0 1.3 %collective-permute-start.7 = (f32[90,1440]{1,0:T(8,128)S(1)}, f32[90,1440]{1,0:T(8,128)S(1)}, u32[]{:S(2)}, u32[]{:S(2)}) collective-permute-start(f32[90,1440]{1,0:T(8,128)S(1)} %get-tuple-element.64), channel_id=1, source_target_pairs={{1,0},{3,2},{5,4},{7,6},{9,8},{11,10},{13,12},{15,14},{17,16},{19,... | collective-permute-start | bytes 1555208 | tf_op jit(solution)/shard_map/ppermute | solution.py:793
  32.3 0.0 collective-permute-done.6.arrived_ref
  32.3 0.0 copy-start.2
  32.3 3.9 %shard_map.163 = (f32[90,2,1440]{2,1,0:T(2,128)S(1)}, f32[90,2,1440]{2,1,0:T(2,128)S(1)}, f32[2,45,2,360]{3,2,1,0:T(2,128)}) custom-call(f32[45,2,360]{2,1,0:T(2,128)S(1)} %get-tuple-element.59.east_keep, f32[45,2,360]{2,1,0:T(2,128)S(1)} %get-tuple-element.60.north_keep, f32[2,45,2,360]{3,2,1,0:T(2,128)S(1)} %collective-permute-done.6.arrived_ref, ...), custom_call_target="tpu_custom_call" | custom-call | flops 3680000000 | tf_op jit(solution)/shard_map/pallas_call | solution.py:796
  36.2 0.0 collective-permute-done.7.rest_4_
  36.2 0.0 copy-done.2
  36.2 1.7 %shard_map.164 = (f32[90,2,1440]{2,1,0:T(2,128)}, f32[90,2,1440]{2,1,0:T(2,128)}, f32[90,2,1440]{2,1,0:T(2,128)}) custom-call(f32[90,1440]{1,0:T(8,128)S(1)} %copy-done.2, f32[90,2,1440]{2,1,0:T(2,128)S(1)} %get-tuple-element.57.rest_0_, f32[90,2,1440]{2,1,0:T(2,128)S(1)} %get-tuple-element.58.rest_1_, f32[90,2,1440]{2,1,0:T(2,128)S(1)} %get-tuple-element.62.rest_2_, ...), custom_call_target="tpu_custom_call" | custom-call | flops 1150000000 | tf_op jit(solution)/shard_map/pallas_call | solution.py:804
  (1 shorter events, 0.0 us)
Async XLA Ops:
  3.7 15.1 %collective-permute-start.2 = (f32[456,128]{1,0:T(8,128)S(1)}, f32[456,128]{1,0:T(8,128)S(1)}, u32[]{:S(2)}, u32[]{:S(2)}) collective-permute-start(f32[456,128]{1,0:T(8,128)S(1)} %get-tuple-element.46.rest_0_), channel_id=1, source_target_pairs={{0,2},{2,0},{1,3},{3,1},{4,6},{6,4},{5,7},{7,5},{8,10},{10,8},{9,1... | collective-permute-start | bytes 700424 | tf_op jit(solution)/shard_map/ppermute | solution.py:650
  6.7 4.4 %collective-permute-start = (f32[8,1440]{1,0:T(8,128)S(1)}, f32[8,1440]{1,0:T(8,128)S(1)}, u32[]{:S(2)}, u32[]{:S(2)}) collective-permute-start(f32[8,1440]{1,0:T(8,128)S(1)} %get-tuple-element.42), channel_id=1, source_target_pairs={{0,4},{8,12},{4,0},{12,8},{1,5},{9,13},{5,1},{13,9},{2,6},{10,14},... | collective-permute-start | bytes 138248 | tf_op jit(solution)/shard_map/ppermute | solution.py:711
  8.2 2.9 %copy-start.3 = (s32[180]{0:T(256)S(1)}, s32[180]{0:T(256)}, u32[]{:S(2)}) copy-start(s32[180]{0:T(256)} %param.18) | copy-start | bytes 2164
  8.2 2.9 %copy-start.4 = (s32[180]{0:T(256)S(1)}, s32[180]{0:T(256)}, u32[]{:S(2)}) copy-start(s32[180]{0:T(256)} %param.19) | copy-start | bytes 2164
  9.8 9.7 %collective-permute-start.3 = (f32[592,128]{1,0:T(8,128)S(1)}, f32[592,128]{1,0:T(8,128)S(1)}, u32[]{:S(2)}, u32[]{:S(2)}) collective-permute-start(f32[592,128]{1,0:T(8,128)S(1)} %shard_map.158.rest_2_), channel_id=1, source_target_pairs={{0,2},{2,0},{1,3},{3,1},{4,6},{6,4},{5,7},{7,5},{8,10},{10,8},{9,1... | collective-permute-start | bytes 909320 | tf_op jit(solution)/shard_map/ppermute | solution.py:650
  10.4 0.7 %collective-permute-start.1 = (f32[8,1440]{1,0:T(8,128)S(1)}, f32[8,1440]{1,0:T(8,128)S(1)}, u32[]{:S(2)}, u32[]{:S(2)}) collective-permute-start(f32[8,1440]{1,0:T(8,128)S(1)} %get-tuple-element.43), channel_id=1, source_target_pairs={{4,8},{8,4},{5,9},{9,5},{6,10},{10,6},{7,11},{11,7},{20,24},{24,20... | collective-permute-start | bytes 138248 | tf_op jit(solution)/shard_map/ppermute | solution.py:711
  11.1 8.4 %copy-start.1 = (f32[2,90,1440]{2,0,1:T(2,128)S(1)}, f32[2,90,1440]{2,0,1:T(2,128)}, u32[]{:S(2)}) copy-start(f32[2,90,1440]{2,0,1:T(2,128)} %param.14) | copy-start | bytes 3110404
  14.7 11.5 %collective-permute-start.4 = (f32[544,128]{1,0:T(8,128)S(1)}, f32[544,128]{1,0:T(8,128)S(1)}, u32[]{:S(2)}, u32[]{:S(2)}) collective-permute-start(f32[544,128]{1,0:T(8,128)S(1)} %get-tuple-element.52.rest_0_), channel_id=1, source_target_pairs={{0,2},{2,0},{12,14},{14,12},{1,3},{3,1},{13,15},{15,13},{16,18},{1... | collective-permute-start | bytes 835592 | tf_op jit(solution)/shard_map/ppermute | solution.py:742
  18.1 2.0 %copy-start = (bf16[2304,768]{1,0:T(8,128)(2,1)S(1)}, bf16[2304,768]{1,0:T(8,128)(2,1)}, u32[]{:S(2)}) copy-start(bf16[2304,768]{1,0:T(8,128)(2,1)} %constant.9.clone.rest_4_.basis_ref.refs_12_.rest_12_) | copy-start | bytes 10616836
  18.2 2.0 %copy-start.5 = (f32[2]{0:T(128)S(1)}, f32[2]{0:T(128)}, u32[]{:S(2)}) copy-start(f32[2]{0:T(128)} %rest_0_.1) | copy-start | bytes 28
  18.2 12.2 %collective-permute-start.5 = (f32[504,128]{1,0:T(8,128)S(1)}, f32[504,128]{1,0:T(8,128)S(1)}, u32[]{:S(2)}, u32[]{:S(2)}) collective-permute-start(f32[504,128]{1,0:T(8,128)S(1)} %get-tuple-element.56.refs_10_.rest_10_), channel_id=1, source_target_pairs={{0,2},{2,0},{1,3},{3,1},{4,6},{6,4},{5,7},{7,5},{8,10},{10,8},{9,1... | collective-permute-start | bytes 774152 | tf_op jit(solution)/shard_map/ppermute | solution.py:650
  26.4 5.8 %collective-permute-start.6 = (f32[2,45,2,360]{3,2,1,0:T(2,128)S(1)}, f32[2,45,2,360]{3,2,1,0:T(2,128)S(1)}, u32[]{:S(2)}, u32[]{:S(2)}) collective-permute-start(f32[2,45,2,360]{3,2,1,0:T(2,128)S(1)} %get-tuple-element.61), channel_id=1, source_target_pairs={{0,8},{12,4},{1,9},{13,5},{2,10},{14,6},{3,11},{15,7},{16,24},{28,... | collective-permute-start | bytes 777608 | tf_op jit(solution)/shard_map/ppermute | solution.py:764
  31.0 5.2 %collective-permute-start.7 = (f32[90,1440]{1,0:T(8,128)S(1)}, f32[90,1440]{1,0:T(8,128)S(1)}, u32[]{:S(2)}, u32[]{:S(2)}) collective-permute-start(f32[90,1440]{1,0:T(8,128)S(1)} %get-tuple-element.64), channel_id=1, source_target_pairs={{1,0},{3,2},{5,4},{7,6},{9,8},{11,10},{13,12},{15,14},{17,16},{19,... | collective-permute-start | bytes 1555208 | tf_op jit(solution)/shard_map/ppermute | solution.py:793
  32.3 3.9 %copy-start.2 = (f32[90,1440]{1,0:T(8,128)S(1)}, f32[90,1440]{1,0:T(8,128)}, u32[]{:S(2)}) copy-start(f32[90,1440]{1,0:T(8,128)} %surface_ref.1) | copy-start | bytes 1555204

commit v7 on v6

--- a/solution.py
+++ b/solution.py
@@ -595,12 +595,14 @@
 
 def finish(z, surface_ref, *rest):
     deeper_fields, own_fields, deeper, outs = rest[:2], rest[2:4], rest[4 : 3 + z.n_lev], rest[3 + z.n_lev :]
-    final_out, thick_out, geo_out, geo_ref, sems = outs
+    spectra, (final_out, thick_out, geo_out, spectra_out, geo_ref, sems) = outs[0], outs[1:]
 
     def store(fields):
         copies = [
             pltpu.make_async_copy(*pair, sems.at[n])
-            for n, pair in enumerate(zip(fields, (final_out, thick_out), strict=True))
+            for n, pair in enumerate(
+                ((fields[0], final_out), (fields[1], thick_out), (spectra, spectra_out))
+            )
         ]
         for copy in copies:
             copy.start()
@@ -610,7 +612,7 @@
             for lev in reversed(range(z.lev)):
                 column = column + fields[1][at, lev, :]
                 geo_ref[at, lev, :] = surface_ref[at] + GRAVITY * column
-            copies.append(pltpu.make_async_copy(geo_ref.at[at], geo_out.at[at], sems.at[2 + n]))
+            copies.append(pltpu.make_async_copy(geo_ref.at[at], geo_out.at[at], sems.at[3 + n]))
             copies[-1].start()
         for copy in copies:
             copy.wait()
@@ -793,22 +795,22 @@
         lax.ppermute(column, "lev", [(i, i - distance) for i in range(distance, z.n_lev)])
         for distance in range(1, z.n_lev)
     ]
-    final_own, thick_own, spectra = call(
+    final_own, thick_own, joined = call(
         functools.partial(north_shallowest, z),
         3 + len(operands),
-        [in_vmem, in_vmem, (2, *spec)],
+        [in_vmem, in_vmem, pltpu.VMEM((2, *spec), jnp.float32)],
         [pltpu.VMEM((z.lat, z.lon), jnp.float32), pltpu.VMEM(spec, jnp.float32)] + scratch,
         3.2,
         {3: pltpu.SMEM},
     )(east_keep, north_keep, arrived, *operands)
-    north_final, thick_new, geo_new = call(
+    north_final, thick_new, geo_new, spectra = call(
         functools.partial(finish, z),
-        5 + len(deeper),
-        [pltpu.HBM(field, jnp.float32)] * 3,
-        [pltpu.VMEM(field, jnp.float32), pltpu.SemaphoreType.DMA((2 + z.cuts,))],
+        6 + len(deeper),
+        [pltpu.HBM(field, jnp.float32)] * 3 + [pltpu.HBM((2, *spec), jnp.float32)],
+        [pltpu.VMEM(field, jnp.float32), pltpu.SemaphoreType.DMA((3 + z.cuts,))],
         1,
-        in_hbm=3,
-    )(surface_geopot, final_deeper, thick_deeper, final_own, thick_own, *deeper)
+        in_hbm=4,
+    )(surface_geopot, final_deeper, thick_deeper, final_own, thick_own, *deeper, joined)
     return tuple(level_inside(x) for x in (east_final, north_final, thick_new, geo_new, spectra))
 
 

time: 38.4 us -> 37.9 us (0.987)
  Pallas kernels: 19.8 us -> 19.3 us
    pallas_call x1, Pallas kernels: 3.92 us -> 3.22 us  [local(): call(functools.partial(north_shallowest, z), 3 + len(operands), [in_vmem,...]
  transfers between devices with their start and end apart: 8 -> 8, of which waited for: 3 -> 3; matrix products, arithmetic and copies ran while one was open for 0% -> 0% of each run, Pallas kernels for 39% -> 38%
where the time goes in v7:
time: 37.9 us; the launch traced here: 37.5 us
  Pallas kernels  19.3 us (51%)
  starting transfers between devices  12.3 us (32%)
  waiting for transfers between devices  4.34 us (11%)
  between operations  0.95 us (3%)
  local copies, waits for them, and re-layouts  0.68 us (2%)
    ppermute x3, starting transfers between devices, shifted(): lax.ppermute(block, axis, [(i, (i + distance) % count) for i in range(cou...  4.18 us
    pallas_call x1, Pallas kernels, local(): call(functools.partial(east_inverse, z), 11 + 2 * z.n_lon, [field, (z.own...  4.02 us
    pallas_call x1, Pallas kernels, local(): call(functools.partial(north_forward, z), 10, [(packed_rows(z.ahead), 128...  3.62 us
    ppermute x1, starting transfers between devices, local(): north_aheads.append(lax.ppermute(north_ahead, ('lat', 'lon'), route))  3.39 us
    pallas_call x1, Pallas kernels, local(): call(functools.partial(north_shallowest, z), 3 + len(operands), [in_vmem,...  3.22 us
    pallas_call x1, Pallas kernels, local(): call(functools.partial(east_first, z), 6, [(packed_rows(z.first), 128), r...  3.06 us
    ppermute x3, waiting for transfers between devices, shifted(): lax.ppermute(block, axis, [(i, (i + distance) % count) for i in range(cou...  2.28 us
    ppermute x2, starting transfers between devices, local(): met.append(lax.ppermute(rim, 'lat', pairs + [(b, a) for a, b in pairs]))  2.14 us
  transfers between devices with their start and end apart: 8, of which 3 were waited for; matrix products, arithmetic and copies ran while one was open for 0% of the time, Pallas kernels for 38%

profile of v7, /device:TPU:0, one launch (start us, length us, event | category | flops | bytes accessed | tf_op | source)
XLA Modules:
  0.0 37.5 jit_solution(9512904320384378186)
XLA Ops:
  0.6 3.1 %shard_map.155 = (f32[456,128]{1,0:T(8,128)S(1)}, f32[8,1440]{1,0:T(8,128)S(1)}, f32[8,1440]{1,0:T(8,128)S(1)}, f32[90,2,1440]{2,1,0:T(2,128)S(1)}, f32[90,2,144...) custom-call(f32[90,2,1440]{2,1,0:T(2,128)} %bitcast.15, ...), custom_call_target="tpu_custom_call" | custom-call | flops 1150000000 | tf_op jit(solution)/shard_map/pallas_call | solution.py:685
  3.7 3.0 %collective-permute-start.2 = (f32[456,128]{1,0:T(8,128)S(1)}, f32[456,128]{1,0:T(8,128)S(1)}, u32[]{:S(2)}, u32[]{:S(2)}) collective-permute-start(f32[456,128]{1,0:T(8,128)S(1)} %get-tuple-element.47.rest_0_), channel_id=1, source_target_pairs={{0,2},{2,0},{1,3},{3,1},{4,6},{6,4},{5,7},{7,5},{8,10},{10,8},{9,1... | collective-permute-start | bytes 700424 | tf_op jit(solution)/shard_map/ppermute | solution.py:652
  6.7 1.5 %collective-permute-start = (f32[8,1440]{1,0:T(8,128)S(1)}, f32[8,1440]{1,0:T(8,128)S(1)}, u32[]{:S(2)}, u32[]{:S(2)}) collective-permute-start(f32[8,1440]{1,0:T(8,128)S(1)} %get-tuple-element.43), channel_id=1, source_target_pairs={{0,4},{8,12},{4,0},{12,8},{1,5},{9,13},{5,1},{13,9},{2,6},{10,14},... | collective-permute-start | bytes 138248 | tf_op jit(solution)/shard_map/ppermute | solution.py:713
  8.2 0.0 copy-start.3
  8.2 0.0 copy-start.4
  8.2 1.6 %shard_map.158.rest_2_ = f32[592,128]{1,0:T(8,128)S(1)} custom-call(f32[90,2,1440]{2,1,0:T(2,128)S(1)} %get-tuple-element.38.we_ref, f32[90,2,1440]{2,1,0:T(2,128)S(1)} %get-tuple-element.39.wn_ref, f32[90,2,1440]{2,1,0:T(2,128)S(1)} %get-tuple-element.40.g_ref, f32[184,8]{1,0:T(8,128)S(1)} %get-tuple-element.41.row_ref.refs_3_.rest_3_, ...), custom_call_target="tpu_custom_call" | custom-call | flops 207000000 | tf_op jit(solution)/shard_map/pallas_call | solution.py:700
  9.8 0.6 %collective-permute-start.3 = (f32[592,128]{1,0:T(8,128)S(1)}, f32[592,128]{1,0:T(8,128)S(1)}, u32[]{:S(2)}, u32[]{:S(2)}) collective-permute-start(f32[592,128]{1,0:T(8,128)S(1)} %shard_map.158.rest_2_), channel_id=1, source_target_pairs={{0,2},{2,0},{1,3},{3,1},{4,6},{6,4},{5,7},{7,5},{8,10},{10,8},{9,1... | collective-permute-start | bytes 909320 | tf_op jit(solution)/shard_map/ppermute | solution.py:652
  10.4 0.7 %collective-permute-start.1 = (f32[8,1440]{1,0:T(8,128)S(1)}, f32[8,1440]{1,0:T(8,128)S(1)}, u32[]{:S(2)}, u32[]{:S(2)}) collective-permute-start(f32[8,1440]{1,0:T(8,128)S(1)} %get-tuple-element.44), channel_id=1, source_target_pairs={{4,8},{8,4},{5,9},{9,5},{6,10},{10,6},{7,11},{11,7},{20,24},{24,20... | collective-permute-start | bytes 138248 | tf_op jit(solution)/shard_map/ppermute | solution.py:713
  11.1 0.0 collective-permute-done.even_ref
  11.1 0.0 collective-permute-done.1.odd_ref
  11.1 0.0 copy-done.3
  11.1 0.0 copy-done.4
  11.1 0.0 copy-start.1
  11.1 3.6 %shard_map.156 = (f32[544,128]{1,0:T(8,128)S(1)}, f32[504,128]{1,0:T(8,128)S(1)}, f32[184,1440]{1,0:T(8,128)S(1)}, f32[184,256]{1,0:T(8,128)S(1)}, f32[184,128]{1,0:T(8,128)S(1)}) custom-call(f32[90,2,1440]{2,1,0:T(2,128)S(1)} %get-tuple-element.38.we_ref, f32[90,2,1440]{2,1,0:T(2,128)S(1)} %get-tuple-element.39.wn_ref, ...), custom_call_target="tpu_custom_call" | custom-call | flops 920000000 | tf_op jit(solution)/shard_map/pallas_call | solution.py:716
  14.7 3.4 %collective-permute-start.4 = (f32[544,128]{1,0:T(8,128)S(1)}, f32[544,128]{1,0:T(8,128)S(1)}, u32[]{:S(2)}, u32[]{:S(2)}) collective-permute-start(f32[544,128]{1,0:T(8,128)S(1)} %get-tuple-element.53.rest_0_), channel_id=1, source_target_pairs={{0,2},{2,0},{12,14},{14,12},{1,3},{3,1},{13,15},{15,13},{16,18},{1... | collective-permute-start | bytes 835592 | tf_op jit(solution)/shard_map/ppermute | solution.py:744
  18.1 0.0 copy-start
  18.2 0.0 copy-start.5
  18.2 0.6 %collective-permute-start.5 = (f32[504,128]{1,0:T(8,128)S(1)}, f32[504,128]{1,0:T(8,128)S(1)}, u32[]{:S(2)}, u32[]{:S(2)}) collective-permute-start(f32[504,128]{1,0:T(8,128)S(1)} %get-tuple-element.57.refs_10_.rest_10_), channel_id=1, source_target_pairs={{0,2},{2,0},{1,3},{3,1},{4,6},{6,4},{5,7},{7,5},{8,10},{10,8},{9,1... | collective-permute-start | bytes 774152 | tf_op jit(solution)/shard_map/ppermute | solution.py:652
  18.8 0.0 collective-permute-done.2.arrived_ref.rest_1_
  18.8 0.7 %collective-permute-done.3.rest_3_ = f32[592,128]{1,0:T(8,128)S(1)} collective-permute-done((f32[592,128]{1,0:T(8,128)S(1)}, f32[592,128]{1,0:T(8,128)S(1)}, u32[]{:S(2)}, u32[]{:S(2)}) %collective-permute-start.3) | collective-permute-done | bytes 303136 | tf_op jit(solution)/shard_map/ppermute | solution.py:652
  19.5 0.0 copy-done.1
  19.5 0.7 %copy-done = bf16[2304,768]{1,0:T(8,128)(2,1)S(1)} copy-done((bf16[2304,768]{1,0:T(8,128)(2,1)S(1)}, bf16[2304,768]{1,0:T(8,128)(2,1)}, u32[]{:S(2)}) %copy-start) | copy-done | bytes 3538968
  20.1 0.0 copy-done.5
  20.1 4.0 %shard_map.159 = (f32[90,2,1440]{2,1,0:T(2,128)}, f32[180,1440]{1,0:T(8,128)S(1)}, f32[45,2,360]{2,1,0:T(2,128)S(1)}, f32[45,2,360]{2,1,0:T(2,128)S(1)}) custom-call(f32[2]{0:T(128)S(1)} %copy-done.5, f32[90,2,1440]{2,1,0:T(2,128)S(1)} %get-tuple-element.38.we_ref, f32[90,2,1440]{2,1,0:T(2,128)S(1)} %get-tuple-element.39.wn_ref, ...), custom_call_target="tpu_custom_call" | custom-call | flops 1150000000 | tf_op jit(solution)/shard_map/pallas_call | solution.py:747
  24.2 2.0 %collective-permute-done.4.rest_1_ = f32[544,128]{1,0:T(8,128)S(1)} collective-permute-done((f32[544,128]{1,0:T(8,128)S(1)}, f32[544,128]{1,0:T(8,128)S(1)}, u32[]{:S(2)}, u32[]{:S(2)}) %collective-permute-start.4) | collective-permute-done | bytes 278560 | tf_op jit(solution)/shard_map/ppermute | solution.py:744
  26.2 0.2 shard_map.160
  26.4 1.3 %collective-permute-start.6 = (f32[2,45,2,360]{3,2,1,0:T(2,128)S(1)}, f32[2,45,2,360]{3,2,1,0:T(2,128)S(1)}, u32[]{:S(2)}, u32[]{:S(2)}) collective-permute-start(f32[2,45,2,360]{3,2,1,0:T(2,128)S(1)} %get-tuple-element.62), channel_id=1, source_target_pairs={{0,8},{12,4},{1,9},{13,5},{2,10},{14,6},{3,11},{15,7},{16,24},{28,... | collective-permute-start | bytes 777608 | tf_op jit(solution)/shard_map/ppermute | solution.py:766
  27.7 1.1 %shard_map.161 = (bf16[96,1536]{1,0:T(8,128)(2,1)S(1)}, bf16[96,1536]{1,0:T(8,128)(2,1)S(1)}) custom-call(f32[16,384]{1,0:T(8,128)S(1)} %get-tuple-element.42.phase_ref.refs_4_.rest_4_, f32[96,768]{1,0:T(8,128)S(1)} %get-tuple-element.54.waves_ref.refs_7_.rest_7_, bf16[2304,768]{1,0:T(8,128)(2,1)S(1)} %copy-done), custom_call_target="tpu_custom_call" | custom-call | flops 575000000 | tf_op jit(solution)/shard_map/pallas_call | solution.py:771
  28.8 1.6 %collective-permute-done.5.refs_11_.rest_11_ = f32[504,128]{1,0:T(8,128)S(1)} collective-permute-done((f32[504,128]{1,0:T(8,128)S(1)}, f32[504,128]{1,0:T(8,128)S(1)}, u32[]{:S(2)}, u32[]{:S(2)}) %collective-permute-start.5) | collective-permute-done | bytes 258080 | tf_op jit(solution)/shard_map/ppermute | solution.py:652
  30.4 0.6 %shard_map.162 = (f32[90,2,1440]{2,1,0:T(2,128)S(1)}, f32[90,2,1440]{2,1,0:T(2,128)S(1)}, f32[90,1440]{1,0:T(8,128)S(1)}, f32[45,2,360]{2,1,0:T(2,128)S(1)}) custom-call(f32[2]{0:T(128)S(1)} %copy-done.5, f32[184,1440]{1,0:T(8,128)S(1)} %get-tuple-element.49.refs_1_.rest_1_, f32[180,1440]{1,0:T(8,128)S(1)} %get-tuple-element.50.refs_2_.rest_2_, ...), custom_call_target="tpu_custom_call" | custom-call | flops 2300000000 | tf_op jit(solution)/shard_map/pallas_call | solution.py:786
  31.0 1.3 %collective-permute-start.7 = (f32[90,1440]{1,0:T(8,128)S(1)}, f32[90,1440]{1,0:T(8,128)S(1)}, u32[]{:S(2)}, u32[]{:S(2)}) collective-permute-start(f32[90,1440]{1,0:T(8,128)S(1)} %get-tuple-element.65), channel_id=1, source_target_pairs={{1,0},{3,2},{5,4},{7,6},{9,8},{11,10},{13,12},{15,14},{17,16},{19,... | collective-permute-start | bytes 1555208 | tf_op jit(solution)/shard_map/ppermute | solution.py:795
  32.3 0.0 collective-permute-done.6.arrived_ref
  32.3 0.0 copy-start.2
  32.3 3.2 %shard_map.163 = (f32[90,2,1440]{2,1,0:T(2,128)S(1)}, f32[90,2,1440]{2,1,0:T(2,128)S(1)}, f32[2,45,2,360]{3,2,1,0:T(2,128)S(1)}) custom-call(f32[45,2,360]{2,1,0:T(2,128)S(1)} %get-tuple-element.60.east_keep, f32[45,2,360]{2,1,0:T(2,128)S(1)} %get-tuple-element.61.north_keep, f32[2,45,2,360]{3,2,1,0:T(2,128)S(1)} %collective-permute-done.6.arrived_ref, ...), custom_call_target="tpu_custom_call" | custom-call | flops 3680000000 | tf_op jit(solution)/shard_map/pallas_call | solution.py:798
  35.5 0.0 collective-permute-done.7.rest_4_
  35.5 0.0 copy-done.2
  35.5 1.9 %shard_map.164 = (f32[90,2,1440]{2,1,0:T(2,128)}, f32[90,2,1440]{2,1,0:T(2,128)}, f32[90,2,1440]{2,1,0:T(2,128)}, f32[2,45,2,360]{3,2,1,0:T(2,128)}) custom-call(f32[90,1440]{1,0:T(8,128)S(1)} %copy-done.2, f32[90,2,1440]{2,1,0:T(2,128)S(1)} %get-tuple-element.58.rest_0_, f32[90,2,1440]{2,1,0:T(2,128)S(1)} %get-tuple-element.59.rest_1_, ...), custom_call_target="tpu_custom_call" | custom-call | flops 1150000000 | tf_op jit(solution)/shard_map/pallas_call | solution.py:806
  (1 shorter events, 0.0 us)
Async XLA Ops:
  3.7 15.1 %collective-permute-start.2 = (f32[456,128]{1,0:T(8,128)S(1)}, f32[456,128]{1,0:T(8,128)S(1)}, u32[]{:S(2)}, u32[]{:S(2)}) collective-permute-start(f32[456,128]{1,0:T(8,128)S(1)} %get-tuple-element.47.rest_0_), channel_id=1, source_target_pairs={{0,2},{2,0},{1,3},{3,1},{4,6},{6,4},{5,7},{7,5},{8,10},{10,8},{9,1... | collective-permute-start | bytes 700424 | tf_op jit(solution)/shard_map/ppermute | solution.py:652
  6.7 4.4 %collective-permute-start = (f32[8,1440]{1,0:T(8,128)S(1)}, f32[8,1440]{1,0:T(8,128)S(1)}, u32[]{:S(2)}, u32[]{:S(2)}) collective-permute-start(f32[8,1440]{1,0:T(8,128)S(1)} %get-tuple-element.43), channel_id=1, source_target_pairs={{0,4},{8,12},{4,0},{12,8},{1,5},{9,13},{5,1},{13,9},{2,6},{10,14},... | collective-permute-start | bytes 138248 | tf_op jit(solution)/shard_map/ppermute | solution.py:713
  8.2 2.9 %copy-start.3 = (s32[180]{0:T(256)S(1)}, s32[180]{0:T(256)}, u32[]{:S(2)}) copy-start(s32[180]{0:T(256)} %param.18) | copy-start | bytes 2164
  8.2 2.9 %copy-start.4 = (s32[180]{0:T(256)S(1)}, s32[180]{0:T(256)}, u32[]{:S(2)}) copy-start(s32[180]{0:T(256)} %param.19) | copy-start | bytes 2164
  9.8 9.7 %collective-permute-start.3 = (f32[592,128]{1,0:T(8,128)S(1)}, f32[592,128]{1,0:T(8,128)S(1)}, u32[]{:S(2)}, u32[]{:S(2)}) collective-permute-start(f32[592,128]{1,0:T(8,128)S(1)} %shard_map.158.rest_2_), channel_id=1, source_target_pairs={{0,2},{2,0},{1,3},{3,1},{4,6},{6,4},{5,7},{7,5},{8,10},{10,8},{9,1... | collective-permute-start | bytes 909320 | tf_op jit(solution)/shard_map/ppermute | solution.py:652
  10.4 0.7 %collective-permute-start.1 = (f32[8,1440]{1,0:T(8,128)S(1)}, f32[8,1440]{1,0:T(8,128)S(1)}, u32[]{:S(2)}, u32[]{:S(2)}) collective-permute-start(f32[8,1440]{1,0:T(8,128)S(1)} %get-tuple-element.44), channel_id=1, source_target_pairs={{4,8},{8,4},{5,9},{9,5},{6,10},{10,6},{7,11},{11,7},{20,24},{24,20... | collective-permute-start | bytes 138248 | tf_op jit(solution)/shard_map/ppermute | solution.py:713
  11.1 8.4 %copy-start.1 = (f32[2,90,1440]{2,0,1:T(2,128)S(1)}, f32[2,90,1440]{2,0,1:T(2,128)}, u32[]{:S(2)}) copy-start(f32[2,90,1440]{2,0,1:T(2,128)} %param.14) | copy-start | bytes 3110404
  14.7 11.5 %collective-permute-start.4 = (f32[544,128]{1,0:T(8,128)S(1)}, f32[544,128]{1,0:T(8,128)S(1)}, u32[]{:S(2)}, u32[]{:S(2)}) collective-permute-start(f32[544,128]{1,0:T(8,128)S(1)} %get-tuple-element.53.rest_0_), channel_id=1, source_target_pairs={{0,2},{2,0},{12,14},{14,12},{1,3},{3,1},{13,15},{15,13},{16,18},{1... | collective-permute-start | bytes 835592 | tf_op jit(solution)/shard_map/ppermute | solution.py:744
  18.1 2.0 %copy-start = (bf16[2304,768]{1,0:T(8,128)(2,1)S(1)}, bf16[2304,768]{1,0:T(8,128)(2,1)}, u32[]{:S(2)}) copy-start(bf16[2304,768]{1,0:T(8,128)(2,1)} %constant.9.clone.rest_4_.basis_ref.refs_12_.rest_12_) | copy-start | bytes 10616836
  18.2 2.0 %copy-start.5 = (f32[2]{0:T(128)S(1)}, f32[2]{0:T(128)}, u32[]{:S(2)}) copy-start(f32[2]{0:T(128)} %rest_0_.1) | copy-start | bytes 28
  18.2 12.2 %collective-permute-start.5 = (f32[504,128]{1,0:T(8,128)S(1)}, f32[504,128]{1,0:T(8,128)S(1)}, u32[]{:S(2)}, u32[]{:S(2)}) collective-permute-start(f32[504,128]{1,0:T(8,128)S(1)} %get-tuple-element.57.refs_10_.rest_10_), channel_id=1, source_target_pairs={{0,2},{2,0},{1,3},{3,1},{4,6},{6,4},{5,7},{7,5},{8,10},{10,8},{9,1... | collective-permute-start | bytes 774152 | tf_op jit(solution)/shard_map/ppermute | solution.py:652
  26.4 5.8 %collective-permute-start.6 = (f32[2,45,2,360]{3,2,1,0:T(2,128)S(1)}, f32[2,45,2,360]{3,2,1,0:T(2,128)S(1)}, u32[]{:S(2)}, u32[]{:S(2)}) collective-permute-start(f32[2,45,2,360]{3,2,1,0:T(2,128)S(1)} %get-tuple-element.62), channel_id=1, source_target_pairs={{0,8},{12,4},{1,9},{13,5},{2,10},{14,6},{3,11},{15,7},{16,24},{28,... | collective-permute-start | bytes 777608 | tf_op jit(solution)/shard_map/ppermute | solution.py:766
  31.0 4.5 %collective-permute-start.7 = (f32[90,1440]{1,0:T(8,128)S(1)}, f32[90,1440]{1,0:T(8,128)S(1)}, u32[]{:S(2)}, u32[]{:S(2)}) collective-permute-start(f32[90,1440]{1,0:T(8,128)S(1)} %get-tuple-element.65), channel_id=1, source_target_pairs={{1,0},{3,2},{5,4},{7,6},{9,8},{11,10},{13,12},{15,14},{17,16},{19,... | collective-permute-start | bytes 1555208 | tf_op jit(solution)/shard_map/ppermute | solution.py:795
  32.3 3.2 %copy-start.2 = (f32[90,1440]{1,0:T(8,128)S(1)}, f32[90,1440]{1,0:T(8,128)}, u32[]{:S(2)}) copy-start(f32[90,1440]{1,0:T(8,128)} %surface_ref.1) | copy-start | bytes 1555204

commit v8 on v7

--- a/solution.py
+++ b/solution.py
@@ -17,7 +17,7 @@
 MOVED = 128 - MORE
 LEFT = MORE - MOVED
 BLOCK = 256
-INVERSE_BLOCK = 768
+INVERSE_BLOCK = 512
 
 STEP_FACTOR = 0.15
 CORIOLIS = 0.2

time: 37.9 us -> 37.7 us (level)
  Pallas kernels: 19.3 us -> 18.8 us
    pallas_call x1, Pallas kernels: 3.22 us -> 2.79 us  [local(): call(functools.partial(north_shallowest, z), 3 + len(operands), [in_vmem,...]
  transfers between devices with their start and end apart: 8 -> 8, of which waited for: 3 -> 3; matrix products, arithmetic and copies ran while one was open for 0% -> 0% of each run, Pallas kernels for 38% -> 37%
where the time goes in v8:
time: 37.7 us; the launch traced here: 37.1 us
  Pallas kernels  18.8 us (50%)
  starting transfers between devices  12.3 us (33%)
  waiting for transfers between devices  4.4 us (12%)
  between operations  0.95 us (3%)
  local copies, waits for them, and re-layouts  0.64 us (2%)
    ppermute x3, starting transfers between devices, shifted(): lax.ppermute(block, axis, [(i, (i + distance) % count) for i in range(cou...  4.19 us
    pallas_call x1, Pallas kernels, local(): call(functools.partial(east_inverse, z), 11 + 2 * z.n_lon, [field, (z.own...  4 us
    pallas_call x1, Pallas kernels, local(): call(functools.partial(north_forward, z), 10, [(packed_rows(z.ahead), 128...  3.65 us
    ppermute x1, starting transfers between devices, local(): north_aheads.append(lax.ppermute(north_ahead, ('lat', 'lon'), route))  3.39 us
    pallas_call x1, Pallas kernels, local(): call(functools.partial(east_first, z), 6, [(packed_rows(z.first), 128), r...  3.05 us
    pallas_call x1, Pallas kernels, local(): call(functools.partial(north_shallowest, z), 3 + len(operands), [in_vmem,...  2.79 us
    ppermute x3, waiting for transfers between devices, shifted(): lax.ppermute(block, axis, [(i, (i + distance) % count) for i in range(cou...  2.26 us
    ppermute x2, starting transfers between devices, local(): met.append(lax.ppermute(rim, 'lat', pairs + [(b, a) for a, b in pairs]))  2.14 us
  transfers between devices with their start and end apart: 8, of which 3 were waited for; matrix products, arithmetic and copies ran while one was open for 0% of the time, Pallas kernels for 37%

profile of v8, /device:TPU:0, one launch (start us, length us, event | category | flops | bytes accessed | tf_op | source)
XLA Modules:
  0.0 37.1 jit_solution(175129048607173878)
XLA Ops:
  0.6 3.1 %shard_map.155 = (f32[456,128]{1,0:T(8,128)S(1)}, f32[8,1440]{1,0:T(8,128)S(1)}, f32[8,1440]{1,0:T(8,128)S(1)}, f32[90,2,1440]{2,1,0:T(2,128)S(1)}, f32[90,2,144...) custom-call(f32[90,2,1440]{2,1,0:T(2,128)} %bitcast.15, ...), custom_call_target="tpu_custom_call" | custom-call | flops 1150000000 | tf_op jit(solution)/shard_map/pallas_call | solution.py:685
  3.7 3.0 %collective-permute-start.2 = (f32[456,128]{1,0:T(8,128)S(1)}, f32[456,128]{1,0:T(8,128)S(1)}, u32[]{:S(2)}, u32[]{:S(2)}) collective-permute-start(f32[456,128]{1,0:T(8,128)S(1)} %get-tuple-element.47.rest_0_), channel_id=1, source_target_pairs={{0,2},{2,0},{1,3},{3,1},{4,6},{6,4},{5,7},{7,5},{8,10},{10,8},{9,1... | collective-permute-start | bytes 700424 | tf_op jit(solution)/shard_map/ppermute | solution.py:652
  6.7 1.5 %collective-permute-start = (f32[8,1440]{1,0:T(8,128)S(1)}, f32[8,1440]{1,0:T(8,128)S(1)}, u32[]{:S(2)}, u32[]{:S(2)}) collective-permute-start(f32[8,1440]{1,0:T(8,128)S(1)} %get-tuple-element.43), channel_id=1, source_target_pairs={{0,4},{8,12},{4,0},{12,8},{1,5},{9,13},{5,1},{13,9},{2,6},{10,14},... | collective-permute-start | bytes 138248 | tf_op jit(solution)/shard_map/ppermute | solution.py:713
  8.2 0.0 copy-start.3
  8.2 0.0 copy-start.4
  8.2 1.6 %shard_map.158.rest_2_ = f32[592,128]{1,0:T(8,128)S(1)} custom-call(f32[90,2,1440]{2,1,0:T(2,128)S(1)} %get-tuple-element.38.we_ref, f32[90,2,1440]{2,1,0:T(2,128)S(1)} %get-tuple-element.39.wn_ref, f32[90,2,1440]{2,1,0:T(2,128)S(1)} %get-tuple-element.40.g_ref, f32[184,8]{1,0:T(8,128)S(1)} %get-tuple-element.41.row_ref.refs_3_.rest_3_, ...), custom_call_target="tpu_custom_call" | custom-call | flops 207000000 | tf_op jit(solution)/shard_map/pallas_call | solution.py:700
  9.8 0.6 %collective-permute-start.3 = (f32[592,128]{1,0:T(8,128)S(1)}, f32[592,128]{1,0:T(8,128)S(1)}, u32[]{:S(2)}, u32[]{:S(2)}) collective-permute-start(f32[592,128]{1,0:T(8,128)S(1)} %shard_map.158.rest_2_), channel_id=1, source_target_pairs={{0,2},{2,0},{1,3},{3,1},{4,6},{6,4},{5,7},{7,5},{8,10},{10,8},{9,1... | collective-permute-start | bytes 909320 | tf_op jit(solution)/shard_map/ppermute | solution.py:652
  10.4 0.7 %collective-permute-start.1 = (f32[8,1440]{1,0:T(8,128)S(1)}, f32[8,1440]{1,0:T(8,128)S(1)}, u32[]{:S(2)}, u32[]{:S(2)}) collective-permute-start(f32[8,1440]{1,0:T(8,128)S(1)} %get-tuple-element.44), channel_id=1, source_target_pairs={{4,8},{8,4},{5,9},{9,5},{6,10},{10,6},{7,11},{11,7},{20,24},{24,20... | collective-permute-start | bytes 138248 | tf_op jit(solution)/shard_map/ppermute | solution.py:713
  11.1 0.0 collective-permute-done.even_ref
  11.1 0.0 collective-permute-done.1.odd_ref
  11.1 0.0 copy-done.3
  11.1 0.0 copy-done.4
  11.1 3.6 %shard_map.156 = (f32[544,128]{1,0:T(8,128)S(1)}, f32[504,128]{1,0:T(8,128)S(1)}, f32[184,1440]{1,0:T(8,128)S(1)}, f32[184,256]{1,0:T(8,128)S(1)}, f32[184,128]{1,0:T(8,128)S(1)}) custom-call(f32[90,2,1440]{2,1,0:T(2,128)S(1)} %get-tuple-element.38.we_ref, f32[90,2,1440]{2,1,0:T(2,128)S(1)} %get-tuple-element.39.wn_ref, ...), custom_call_target="tpu_custom_call" | custom-call | flops 920000000 | tf_op jit(solution)/shard_map/pallas_call | solution.py:716
  14.7 3.4 %collective-permute-start.4 = (f32[544,128]{1,0:T(8,128)S(1)}, f32[544,128]{1,0:T(8,128)S(1)}, u32[]{:S(2)}, u32[]{:S(2)}) collective-permute-start(f32[544,128]{1,0:T(8,128)S(1)} %get-tuple-element.53.rest_0_), channel_id=1, source_target_pairs={{0,2},{2,0},{12,14},{14,12},{1,3},{3,1},{13,15},{15,13},{16,18},{1... | collective-permute-start | bytes 835592 | tf_op jit(solution)/shard_map/ppermute | solution.py:744
  18.1 0.0 copy-start
  18.2 0.0 copy-start.1
  18.2 0.0 copy-start.5
  18.2 0.6 %collective-permute-start.5 = (f32[504,128]{1,0:T(8,128)S(1)}, f32[504,128]{1,0:T(8,128)S(1)}, u32[]{:S(2)}, u32[]{:S(2)}) collective-permute-start(f32[504,128]{1,0:T(8,128)S(1)} %get-tuple-element.57.refs_10_.rest_10_), channel_id=1, source_target_pairs={{0,2},{2,0},{1,3},{3,1},{4,6},{6,4},{5,7},{7,5},{8,10},{10,8},{9,1... | collective-permute-start | bytes 774152 | tf_op jit(solution)/shard_map/ppermute | solution.py:652
  18.8 0.0 collective-permute-done.2.arrived_ref.rest_1_
  18.8 0.7 %collective-permute-done.3.rest_3_ = f32[592,128]{1,0:T(8,128)S(1)} collective-permute-done((f32[592,128]{1,0:T(8,128)S(1)}, f32[592,128]{1,0:T(8,128)S(1)}, u32[]{:S(2)}, u32[]{:S(2)}) %collective-permute-start.3) | collective-permute-done | bytes 303136 | tf_op jit(solution)/shard_map/ppermute | solution.py:652
  19.5 0.3 copy-done
  19.8 0.3 copy-done.1
  20.1 0.0 copy-done.5
  20.1 4.0 %shard_map.159 = (f32[90,2,1440]{2,1,0:T(2,128)}, f32[180,1440]{1,0:T(8,128)S(1)}, f32[45,2,360]{2,1,0:T(2,128)S(1)}, f32[45,2,360]{2,1,0:T(2,128)S(1)}) custom-call(f32[2]{0:T(128)S(1)} %copy-done.5, f32[90,2,1440]{2,1,0:T(2,128)S(1)} %get-tuple-element.38.we_ref, f32[90,2,1440]{2,1,0:T(2,128)S(1)} %get-tuple-element.39.wn_ref, ...), custom_call_target="tpu_custom_call" | custom-call | flops 1150000000 | tf_op jit(solution)/shard_map/pallas_call | solution.py:747
  24.1 2.1 %collective-permute-done.4.rest_1_ = f32[544,128]{1,0:T(8,128)S(1)} collective-permute-done((f32[544,128]{1,0:T(8,128)S(1)}, f32[544,128]{1,0:T(8,128)S(1)}, u32[]{:S(2)}, u32[]{:S(2)}) %collective-permute-start.4) | collective-permute-done | bytes 278560 | tf_op jit(solution)/shard_map/ppermute | solution.py:744
  26.2 0.2 shard_map.160
  26.4 1.3 %collective-permute-start.6 = (f32[2,45,2,360]{3,2,1,0:T(2,128)S(1)}, f32[2,45,2,360]{3,2,1,0:T(2,128)S(1)}, u32[]{:S(2)}, u32[]{:S(2)}) collective-permute-start(f32[2,45,2,360]{3,2,1,0:T(2,128)S(1)} %get-tuple-element.62), channel_id=1, source_target_pairs={{0,8},{12,4},{1,9},{13,5},{2,10},{14,6},{3,11},{15,7},{16,24},{28,... | collective-permute-start | bytes 777608 | tf_op jit(solution)/shard_map/ppermute | solution.py:766
  27.8 1.1 %shard_map.161 = (bf16[96,1536]{1,0:T(8,128)(2,1)S(1)}, bf16[96,1536]{1,0:T(8,128)(2,1)S(1)}) custom-call(f32[16,384]{1,0:T(8,128)S(1)} %get-tuple-element.42.phase_ref.refs_4_.rest_4_, f32[96,768]{1,0:T(8,128)S(1)} %get-tuple-element.54.waves_ref.refs_7_.rest_7_, bf16[2304,512]{1,0:T(8,128)(2,1)S(1)} %copy-done), custom_call_target="tpu_custom_call" | custom-call | flops 575000000 | tf_op jit(solution)/shard_map/pallas_call | solution.py:771
  28.8 1.6 %collective-permute-done.5.refs_11_.rest_11_ = f32[504,128]{1,0:T(8,128)S(1)} collective-permute-done((f32[504,128]{1,0:T(8,128)S(1)}, f32[504,128]{1,0:T(8,128)S(1)}, u32[]{:S(2)}, u32[]{:S(2)}) %collective-permute-start.5) | collective-permute-done | bytes 258080 | tf_op jit(solution)/shard_map/ppermute | solution.py:652
  30.4 0.6 %shard_map.162 = (f32[90,2,1440]{2,1,0:T(2,128)S(1)}, f32[90,2,1440]{2,1,0:T(2,128)S(1)}, f32[90,1440]{1,0:T(8,128)S(1)}, f32[45,2,360]{2,1,0:T(2,128)S(1)}) custom-call(f32[2]{0:T(128)S(1)} %copy-done.5, f32[184,1440]{1,0:T(8,128)S(1)} %get-tuple-element.49.refs_1_.rest_1_, f32[180,1440]{1,0:T(8,128)S(1)} %get-tuple-element.50.refs_2_.rest_2_, ...), custom_call_target="tpu_custom_call" | custom-call | flops 2300000000 | tf_op jit(solution)/shard_map/pallas_call | solution.py:786
  31.0 1.3 %collective-permute-start.7 = (f32[90,1440]{1,0:T(8,128)S(1)}, f32[90,1440]{1,0:T(8,128)S(1)}, u32[]{:S(2)}, u32[]{:S(2)}) collective-permute-start(f32[90,1440]{1,0:T(8,128)S(1)} %get-tuple-element.65), channel_id=1, source_target_pairs={{1,0},{3,2},{5,4},{7,6},{9,8},{11,10},{13,12},{15,14},{17,16},{19,... | collective-permute-start | bytes 1555208 | tf_op jit(solution)/shard_map/ppermute | solution.py:795
  32.3 0.0 collective-permute-done.6.arrived_ref
  32.3 0.0 copy-start.2
  32.3 2.8 %shard_map.163 = (f32[90,2,1440]{2,1,0:T(2,128)S(1)}, f32[90,2,1440]{2,1,0:T(2,128)S(1)}, f32[2,45,2,360]{3,2,1,0:T(2,128)S(1)}) custom-call(f32[45,2,360]{2,1,0:T(2,128)S(1)} %get-tuple-element.60.east_keep, f32[45,2,360]{2,1,0:T(2,128)S(1)} %get-tuple-element.61.north_keep, f32[2,45,2,360]{3,2,1,0:T(2,128)S(1)} %collective-permute-done.6.arrived_ref, ...), custom_call_target="tpu_custom_call" | custom-call | flops 3680000000 | tf_op jit(solution)/shard_map/pallas_call | solution.py:798
  35.1 0.0 collective-permute-done.7.rest_4_
  35.1 0.0 copy-done.2
  35.1 1.9 %shard_map.164 = (f32[90,2,1440]{2,1,0:T(2,128)}, f32[90,2,1440]{2,1,0:T(2,128)}, f32[90,2,1440]{2,1,0:T(2,128)}, f32[2,45,2,360]{3,2,1,0:T(2,128)}) custom-call(f32[90,1440]{1,0:T(8,128)S(1)} %copy-done.2, f32[90,2,1440]{2,1,0:T(2,128)S(1)} %get-tuple-element.58.rest_0_, f32[90,2,1440]{2,1,0:T(2,128)S(1)} %get-tuple-element.59.rest_1_, ...), custom_call_target="tpu_custom_call" | custom-call | flops 1150000000 | tf_op jit(solution)/shard_map/pallas_call | solution.py:806
  (1 shorter events, 0.0 us)
Async XLA Ops:
  3.7 15.1 %collective-permute-start.2 = (f32[456,128]{1,0:T(8,128)S(1)}, f32[456,128]{1,0:T(8,128)S(1)}, u32[]{:S(2)}, u32[]{:S(2)}) collective-permute-start(f32[456,128]{1,0:T(8,128)S(1)} %get-tuple-element.47.rest_0_), channel_id=1, source_target_pairs={{0,2},{2,0},{1,3},{3,1},{4,6},{6,4},{5,7},{7,5},{8,10},{10,8},{9,1... | collective-permute-start | bytes 700424 | tf_op jit(solution)/shard_map/ppermute | solution.py:652
  6.7 4.4 %collective-permute-start = (f32[8,1440]{1,0:T(8,128)S(1)}, f32[8,1440]{1,0:T(8,128)S(1)}, u32[]{:S(2)}, u32[]{:S(2)}) collective-permute-start(f32[8,1440]{1,0:T(8,128)S(1)} %get-tuple-element.43), channel_id=1, source_target_pairs={{0,4},{8,12},{4,0},{12,8},{1,5},{9,13},{5,1},{13,9},{2,6},{10,14},... | collective-permute-start | bytes 138248 | tf_op jit(solution)/shard_map/ppermute | solution.py:713
  8.2 2.9 %copy-start.3 = (s32[180]{0:T(256)S(1)}, s32[180]{0:T(256)}, u32[]{:S(2)}) copy-start(s32[180]{0:T(256)} %param.18) | copy-start | bytes 2164
  8.2 2.9 %copy-start.4 = (s32[180]{0:T(256)S(1)}, s32[180]{0:T(256)}, u32[]{:S(2)}) copy-start(s32[180]{0:T(256)} %param.19) | copy-start | bytes 2164
  9.8 9.7 %collective-permute-start.3 = (f32[592,128]{1,0:T(8,128)S(1)}, f32[592,128]{1,0:T(8,128)S(1)}, u32[]{:S(2)}, u32[]{:S(2)}) collective-permute-start(f32[592,128]{1,0:T(8,128)S(1)} %shard_map.158.rest_2_), channel_id=1, source_target_pairs={{0,2},{2,0},{1,3},{3,1},{4,6},{6,4},{5,7},{7,5},{8,10},{10,8},{9,1... | collective-permute-start | bytes 909320 | tf_op jit(solution)/shard_map/ppermute | solution.py:652
  10.4 0.7 %collective-permute-start.1 = (f32[8,1440]{1,0:T(8,128)S(1)}, f32[8,1440]{1,0:T(8,128)S(1)}, u32[]{:S(2)}, u32[]{:S(2)}) collective-permute-start(f32[8,1440]{1,0:T(8,128)S(1)} %get-tuple-element.44), channel_id=1, source_target_pairs={{4,8},{8,4},{5,9},{9,5},{6,10},{10,6},{7,11},{11,7},{20,24},{24,20... | collective-permute-start | bytes 138248 | tf_op jit(solution)/shard_map/ppermute | solution.py:713
  14.7 11.5 %collective-permute-start.4 = (f32[544,128]{1,0:T(8,128)S(1)}, f32[544,128]{1,0:T(8,128)S(1)}, u32[]{:S(2)}, u32[]{:S(2)}) collective-permute-start(f32[544,128]{1,0:T(8,128)S(1)} %get-tuple-element.53.rest_0_), channel_id=1, source_target_pairs={{0,2},{2,0},{12,14},{14,12},{1,3},{3,1},{13,15},{15,13},{16,18},{1... | collective-permute-start | bytes 835592 | tf_op jit(solution)/shard_map/ppermute | solution.py:744
  18.1 1.7 %copy-start = (bf16[2304,512]{1,0:T(8,128)(2,1)S(1)}, bf16[2304,512]{1,0:T(8,128)(2,1)}, u32[]{:S(2)}) copy-start(bf16[2304,512]{1,0:T(8,128)(2,1)} %constant.9.clone.rest_4_.basis_ref.refs_12_.rest_12_) | copy-start | bytes 7077892
  18.2 1.9 %copy-start.1 = (f32[2,90,1440]{2,0,1:T(2,128)S(1)}, f32[2,90,1440]{2,0,1:T(2,128)}, u32[]{:S(2)}) copy-start(f32[2,90,1440]{2,0,1:T(2,128)} %param.14) | copy-start | bytes 3110404
  18.2 1.9 %copy-start.5 = (f32[2]{0:T(128)S(1)}, f32[2]{0:T(128)}, u32[]{:S(2)}) copy-start(f32[2]{0:T(128)} %rest_0_.1) | copy-start | bytes 28
  18.2 12.2 %collective-permute-start.5 = (f32[504,128]{1,0:T(8,128)S(1)}, f32[504,128]{1,0:T(8,128)S(1)}, u32[]{:S(2)}, u32[]{:S(2)}) collective-permute-start(f32[504,128]{1,0:T(8,128)S(1)} %get-tuple-element.57.refs_10_.rest_10_), channel_id=1, source_target_pairs={{0,2},{2,0},{1,3},{3,1},{4,6},{6,4},{5,7},{7,5},{8,10},{10,8},{9,1... | collective-permute-start | bytes 774152 | tf_op jit(solution)/shard_map/ppermute | solution.py:652
  26.4 5.8 %collective-permute-start.6 = (f32[2,45,2,360]{3,2,1,0:T(2,128)S(1)}, f32[2,45,2,360]{3,2,1,0:T(2,128)S(1)}, u32[]{:S(2)}, u32[]{:S(2)}) collective-permute-start(f32[2,45,2,360]{3,2,1,0:T(2,128)S(1)} %get-tuple-element.62), channel_id=1, source_target_pairs={{0,8},{12,4},{1,9},{13,5},{2,10},{14,6},{3,11},{15,7},{16,24},{28,... | collective-permute-start | bytes 777608 | tf_op jit(solution)/shard_map/ppermute | solution.py:766
  31.0 4.1 %collective-permute-start.7 = (f32[90,1440]{1,0:T(8,128)S(1)}, f32[90,1440]{1,0:T(8,128)S(1)}, u32[]{:S(2)}, u32[]{:S(2)}) collective-permute-start(f32[90,1440]{1,0:T(8,128)S(1)} %get-tuple-element.65), channel_id=1, source_target_pairs={{1,0},{3,2},{5,4},{7,6},{9,8},{11,10},{13,12},{15,14},{17,16},{19,... | collective-permute-start | bytes 1555208 | tf_op jit(solution)/shard_map/ppermute | solution.py:795
  32.3 2.8 %copy-start.2 = (f32[90,1440]{1,0:T(8,128)S(1)}, f32[90,1440]{1,0:T(8,128)}, u32[]{:S(2)}) copy-start(f32[90,1440]{1,0:T(8,128)} %surface_ref.1) | copy-start | bytes 1555204

commit v9 on v8

--- a/solution.py
+++ b/solution.py
@@ -198,7 +198,7 @@
     out_ref[at, HALF:] = imag
 
 
-def inverse_rows(z, coef, basis_ref, phase_ref, lhs_ref, out_ref, at=slice(None)):
+def inverse_blocks(z, coef, basis_ref, phase_ref, lhs_ref):
     a, b = coef[:, :HALF], coef[:, HALF:]
     count, width = round_up(coef.shape[0], 16), z.inverse_block
     blocks = range(z.ext // width)
@@ -208,10 +208,22 @@
         store_split(lhs_ref, block * count, pad_rows(turned, count))
     lhs = lhs_ref[: len(blocks) * count]
     rows = jnp.dot(lhs, basis_ref[...], preferred_element_type=jnp.float32)
-    for block in blocks:
-        out_ref[at, block * width : (block + 1) * width] = rows[
-            block * count : block * count + coef.shape[0]
-        ]
+    return [rows[block * count : (block + 1) * count] for block in blocks]
+
+
+def inverse_rows(z, coef, basis_ref, phase_ref, lhs_ref, out_ref, at=slice(None)):
+    width = z.inverse_block
+    for n, rows in enumerate(inverse_blocks(z, coef, basis_ref, phase_ref, lhs_ref)):
+        out_ref[at, n * width : (n + 1) * width] = rows[: coef.shape[0]]
+
+
+def inverse_split(z, coef, basis_ref, phase_ref, lhs_ref, high_ref, low_ref, first, below=0):
+    width = z.inverse_block
+    for n, rows in enumerate(inverse_blocks(z, coef, basis_ref, phase_ref, lhs_ref)):
+        count, columns = rows.shape[0], slice(n * width, (n + 1) * width)
+        high, low = split(rows)
+        high_ref[first : first + count, columns] = high
+        low_ref[below + first : below + first + count, columns] = low
 
 
 def roll(x, shift, axis):
@@ -512,11 +524,10 @@
     send_ref[1] = part[: z.helped].reshape(east_ref.shape)
 
 
-def ahead_inverse(z, phase_ref, waves_ref, basis_ref, high_ref, low_ref, lhs_ref, rows_ref):
+def ahead_inverse(z, phase_ref, waves_ref, basis_ref, high_ref, low_ref, lhs_ref):
     @pl.when(on_polar_band(z))
     def _():
-        inverse_rows(z, waves_ref[...], basis_ref, phase_ref, lhs_ref, rows_ref)
-        high_ref[...], low_ref[...] = split(rows_ref[...])
+        inverse_split(z, waves_ref[...], basis_ref, phase_ref, lhs_ref, high_ref, low_ref, 0)
 
 
 def north_inverse(
@@ -524,7 +535,7 @@
     high_ahead, low_ahead, *rest,
 ):
     shares, rest = rest[: z.n_lon], rest[z.n_lon :]
-    basis_ref, final_ref, thick_ref, column_ref, keep_ref, lhs_ref, rows_ref, high_ref, low_ref = rest
+    basis_ref, final_ref, thick_ref, column_ref, keep_ref, lhs_ref, rows_ref, both_ref = rest
 
     @pl.when(active & on_polar_band(z))
     def _():
@@ -535,15 +546,17 @@
         part = sector_part(z, both, lax.axis_index("lon"))
         first = z.helped - more
         keep_ref[...] = part[first : first + z.helped].reshape(keep_ref.shape)
-        inverse_rows(z, waves, basis_ref, phase_ref, lhs_ref, rows_ref, slice(z.rows - z.ahead))
-        count = high_ref.shape[0] - z.ahead
-        rest_high, rest_low = split(pad_rows(rows_ref[: z.rows - z.ahead], count))
-        high_ref[: z.ahead], low_ref[: z.ahead] = high_ahead[...], low_ahead[...]
-        high_ref[z.ahead :], low_ref[z.ahead :] = rest_high, rest_low
+        both_ref[: z.ahead] = high_ahead[...]
+        both_ref[z.mm_rows : z.mm_rows + z.ahead] = low_ahead[...]
+        inverse_split(
+            z, waves, basis_ref, phase_ref, lhs_ref, both_ref, both_ref, z.ahead, z.mm_rows
+        )
         chosen = chosen_ref[:, : z.mm_rows].astype(jnp.bfloat16)
         rows_ref[...] = jnp.dot(
-            chosen, high_ref[...], preferred_element_type=jnp.float32
-        ) + jnp.dot(chosen, low_ref[...], preferred_element_type=jnp.float32)
+            jnp.concatenate([chosen, chosen], axis=1),
+            both_ref[...],
+            preferred_element_type=jnp.float32,
+        )
         beyond = slice(z.own, z.rows)
         polar = column_of(row_ref, POLAR)[beyond] > 0.0
         rows_ref[beyond, : z.lon] = jnp.where(polar, rows_ref[beyond, : z.lon], north_ref[beyond])
@@ -580,9 +593,9 @@
 
 
 def north_shallowest(z, east_keep, north_keep, arrived_ref, *rest):
-    *refs, spectra_ref, column_ref, keep_ref, lhs_ref, rows_ref, high_ref, low_ref = rest
+    *refs, spectra_ref, column_ref, keep_ref, lhs_ref, rows_ref, both_ref = rest
     active = jnp.logical_not(sends_column())
-    north_inverse(z, active, *refs, column_ref, keep_ref, lhs_ref, rows_ref, high_ref, low_ref)
+    north_inverse(z, active, *refs, column_ref, keep_ref, lhs_ref, rows_ref, both_ref)
 
     @pl.when(sends_column())
     def _():
@@ -772,7 +785,7 @@
         functools.partial(ahead_inverse, z),
         3,
         [ahead_rows] * 2,
-        [waves_lhs, pltpu.VMEM((z.ahead, z.ext), jnp.float32)],
+        [waves_lhs],
         0.5,
     )(phase, waves_ahead, inverse)
 
@@ -782,7 +795,7 @@
     )
     in_vmem = pltpu.VMEM(field, jnp.float32)
     scratch = [waves_lhs, pltpu.VMEM((z.rows, z.ext), jnp.float32)]
-    scratch += [pltpu.VMEM((z.mm_rows, z.ext), jnp.bfloat16)] * 2
+    scratch += [pltpu.VMEM((2 * z.mm_rows, z.ext), jnp.bfloat16)]
     final_deeper, thick_deeper, column, north_keep = call(
         functools.partial(north_deeper, z),
         len(operands),

time: 37.7 us -> 37.7 us (level)
  transfers between devices with their start and end apart: 8 -> 8, of which waited for: 3 -> 3; matrix products, arithmetic and copies ran while one was open for 0% -> 0% of each run, Pallas kernels for 37% -> 38%
where the time goes in v9:
time: 37.7 us; the launch traced here: 37.1 us
  Pallas kernels  18.8 us (50%)
  starting transfers between devices  12.3 us (33%)
  waiting for transfers between devices  4.4 us (12%)
  between operations  0.95 us (3%)
  local copies, waits for them, and re-layouts  0.64 us (2%)
    ppermute x3, starting transfers between devices, shifted(): lax.ppermute(block, axis, [(i, (i + distance) % count) for i in range(cou...  4.19 us
    pallas_call x1, Pallas kernels, local(): call(functools.partial(east_inverse, z), 11 + 2 * z.n_lon, [field, (z.own...  4 us
    pallas_call x1, Pallas kernels, local(): call(functools.partial(north_forward, z), 10, [(packed_rows(z.ahead), 128...  3.65 us
    ppermute x1, starting transfers between devices, local(): north_aheads.append(lax.ppermute(north_ahead, ('lat', 'lon'), route))  3.39 us
    pallas_call x1, Pallas kernels, local(): call(functools.partial(east_first, z), 6, [(packed_rows(z.first), 128), r...  3.05 us
    pallas_call x1, Pallas kernels, local(): call(functools.partial(north_shallowest, z), 3 + len(operands), [in_vmem,...  2.81 us
    ppermute x3, waiting for transfers between devices, shifted(): lax.ppermute(block, axis, [(i, (i + distance) % count) for i in range(cou...  2.26 us
    ppermute x2, starting transfers between devices, local(): met.append(lax.ppermute(rim, 'lat', pairs + [(b, a) for a, b in pairs]))  2.14 us
  transfers between devices with their start and end apart: 8, of which 3 were waited for; matrix products, arithmetic and copies ran while one was open for 0% of the time, Pallas kernels for 38%

profile of v9, /device:TPU:0, one launch (start us, length us, event | category | flops | bytes accessed | tf_op | source)
XLA Modules:
  0.0 37.1 jit_solution(884110653017613084)
XLA Ops:
  0.6 3.1 %shard_map.155 = (f32[456,128]{1,0:T(8,128)S(1)}, f32[8,1440]{1,0:T(8,128)S(1)}, f32[8,1440]{1,0:T(8,128)S(1)}, f32[90,2,1440]{2,1,0:T(2,128)S(1)}, f32[90,2,144...) custom-call(f32[90,2,1440]{2,1,0:T(2,128)} %bitcast.15, ...), custom_call_target="tpu_custom_call" | custom-call | flops 1150000000 | tf_op jit(solution)/shard_map/pallas_call | solution.py:698
  3.7 3.0 %collective-permute-start.2 = (f32[456,128]{1,0:T(8,128)S(1)}, f32[456,128]{1,0:T(8,128)S(1)}, u32[]{:S(2)}, u32[]{:S(2)}) collective-permute-start(f32[456,128]{1,0:T(8,128)S(1)} %get-tuple-element.47.rest_0_), channel_id=1, source_target_pairs={{0,2},{2,0},{1,3},{3,1},{4,6},{6,4},{5,7},{7,5},{8,10},{10,8},{9,1... | collective-permute-start | bytes 700424 | tf_op jit(solution)/shard_map/ppermute | solution.py:665
  6.7 1.5 %collective-permute-start = (f32[8,1440]{1,0:T(8,128)S(1)}, f32[8,1440]{1,0:T(8,128)S(1)}, u32[]{:S(2)}, u32[]{:S(2)}) collective-permute-start(f32[8,1440]{1,0:T(8,128)S(1)} %get-tuple-element.43), channel_id=1, source_target_pairs={{0,4},{8,12},{4,0},{12,8},{1,5},{9,13},{5,1},{13,9},{2,6},{10,14},... | collective-permute-start | bytes 138248 | tf_op jit(solution)/shard_map/ppermute | solution.py:726
  8.2 0.0 copy-start.3
  8.2 0.0 copy-start.4
  8.2 1.6 %shard_map.158.rest_2_ = f32[592,128]{1,0:T(8,128)S(1)} custom-call(f32[90,2,1440]{2,1,0:T(2,128)S(1)} %get-tuple-element.38.we_ref, f32[90,2,1440]{2,1,0:T(2,128)S(1)} %get-tuple-element.39.wn_ref, f32[90,2,1440]{2,1,0:T(2,128)S(1)} %get-tuple-element.40.g_ref, f32[184,8]{1,0:T(8,128)S(1)} %get-tuple-element.41.row_ref.refs_3_.rest_3_, ...), custom_call_target="tpu_custom_call" | custom-call | flops 207000000 | tf_op jit(solution)/shard_map/pallas_call | solution.py:713
  9.8 0.6 %collective-permute-start.3 = (f32[592,128]{1,0:T(8,128)S(1)}, f32[592,128]{1,0:T(8,128)S(1)}, u32[]{:S(2)}, u32[]{:S(2)}) collective-permute-start(f32[592,128]{1,0:T(8,128)S(1)} %shard_map.158.rest_2_), channel_id=1, source_target_pairs={{0,2},{2,0},{1,3},{3,1},{4,6},{6,4},{5,7},{7,5},{8,10},{10,8},{9,1... | collective-permute-start | bytes 909320 | tf_op jit(solution)/shard_map/ppermute | solution.py:665
  10.4 0.7 %collective-permute-start.1 = (f32[8,1440]{1,0:T(8,128)S(1)}, f32[8,1440]{1,0:T(8,128)S(1)}, u32[]{:S(2)}, u32[]{:S(2)}) collective-permute-start(f32[8,1440]{1,0:T(8,128)S(1)} %get-tuple-element.44), channel_id=1, source_target_pairs={{4,8},{8,4},{5,9},{9,5},{6,10},{10,6},{7,11},{11,7},{20,24},{24,20... | collective-permute-start | bytes 138248 | tf_op jit(solution)/shard_map/ppermute | solution.py:726
  11.1 0.0 collective-permute-done.even_ref
  11.1 0.0 collective-permute-done.1.odd_ref
  11.1 0.0 copy-done.3
  11.1 0.0 copy-done.4
  11.1 3.6 %shard_map.156 = (f32[544,128]{1,0:T(8,128)S(1)}, f32[504,128]{1,0:T(8,128)S(1)}, f32[184,1440]{1,0:T(8,128)S(1)}, f32[184,256]{1,0:T(8,128)S(1)}, f32[184,128]{1,0:T(8,128)S(1)}) custom-call(f32[90,2,1440]{2,1,0:T(2,128)S(1)} %get-tuple-element.38.we_ref, f32[90,2,1440]{2,1,0:T(2,128)S(1)} %get-tuple-element.39.wn_ref, ...), custom_call_target="tpu_custom_call" | custom-call | flops 920000000 | tf_op jit(solution)/shard_map/pallas_call | solution.py:729
  14.7 3.4 %collective-permute-start.4 = (f32[544,128]{1,0:T(8,128)S(1)}, f32[544,128]{1,0:T(8,128)S(1)}, u32[]{:S(2)}, u32[]{:S(2)}) collective-permute-start(f32[544,128]{1,0:T(8,128)S(1)} %get-tuple-element.53.rest_0_), channel_id=1, source_target_pairs={{0,2},{2,0},{12,14},{14,12},{1,3},{3,1},{13,15},{15,13},{16,18},{1... | collective-permute-start | bytes 835592 | tf_op jit(solution)/shard_map/ppermute | solution.py:757
  18.1 0.0 copy-start
  18.2 0.0 copy-start.1
  18.2 0.0 copy-start.5
  18.2 0.6 %collective-permute-start.5 = (f32[504,128]{1,0:T(8,128)S(1)}, f32[504,128]{1,0:T(8,128)S(1)}, u32[]{:S(2)}, u32[]{:S(2)}) collective-permute-start(f32[504,128]{1,0:T(8,128)S(1)} %get-tuple-element.57.refs_10_.rest_10_), channel_id=1, source_target_pairs={{0,2},{2,0},{1,3},{3,1},{4,6},{6,4},{5,7},{7,5},{8,10},{10,8},{9,1... | collective-permute-start | bytes 774152 | tf_op jit(solution)/shard_map/ppermute | solution.py:665
  18.8 0.0 collective-permute-done.2.arrived_ref.rest_1_
  18.8 0.7 %collective-permute-done.3.rest_3_ = f32[592,128]{1,0:T(8,128)S(1)} collective-permute-done((f32[592,128]{1,0:T(8,128)S(1)}, f32[592,128]{1,0:T(8,128)S(1)}, u32[]{:S(2)}, u32[]{:S(2)}) %collective-permute-start.3) | collective-permute-done | bytes 303136 | tf_op jit(solution)/shard_map/ppermute | solution.py:665
  19.5 0.3 copy-done
  19.8 0.3 copy-done.1
  20.1 0.0 copy-done.5
  20.1 4.0 %shard_map.159 = (f32[90,2,1440]{2,1,0:T(2,128)}, f32[180,1440]{1,0:T(8,128)S(1)}, f32[45,2,360]{2,1,0:T(2,128)S(1)}, f32[45,2,360]{2,1,0:T(2,128)S(1)}) custom-call(f32[2]{0:T(128)S(1)} %copy-done.5, f32[90,2,1440]{2,1,0:T(2,128)S(1)} %get-tuple-element.38.we_ref, f32[90,2,1440]{2,1,0:T(2,128)S(1)} %get-tuple-element.39.wn_ref, ...), custom_call_target="tpu_custom_call" | custom-call | flops 1150000000 | tf_op jit(solution)/shard_map/pallas_call | solution.py:760
  24.1 2.1 %collective-permute-done.4.rest_1_ = f32[544,128]{1,0:T(8,128)S(1)} collective-permute-done((f32[544,128]{1,0:T(8,128)S(1)}, f32[544,128]{1,0:T(8,128)S(1)}, u32[]{:S(2)}, u32[]{:S(2)}) %collective-permute-start.4) | collective-permute-done | bytes 278560 | tf_op jit(solution)/shard_map/ppermute | solution.py:757
  26.2 0.2 shard_map.160
  26.4 1.3 %collective-permute-start.6 = (f32[2,45,2,360]{3,2,1,0:T(2,128)S(1)}, f32[2,45,2,360]{3,2,1,0:T(2,128)S(1)}, u32[]{:S(2)}, u32[]{:S(2)}) collective-permute-start(f32[2,45,2,360]{3,2,1,0:T(2,128)S(1)} %get-tuple-element.62), channel_id=1, source_target_pairs={{0,8},{12,4},{1,9},{13,5},{2,10},{14,6},{3,11},{15,7},{16,24},{28,... | collective-permute-start | bytes 777608 | tf_op jit(solution)/shard_map/ppermute | solution.py:779
  27.8 1.1 %shard_map.161 = (bf16[96,1536]{1,0:T(8,128)(2,1)S(1)}, bf16[96,1536]{1,0:T(8,128)(2,1)S(1)}) custom-call(f32[16,384]{1,0:T(8,128)S(1)} %get-tuple-element.42.phase_ref.refs_4_.rest_4_, f32[96,768]{1,0:T(8,128)S(1)} %get-tuple-element.54.waves_ref.refs_7_.rest_7_, bf16[2304,512]{1,0:T(8,128)(2,1)S(1)} %copy-done), custom_call_target="tpu_custom_call" | custom-call | flops 575000000 | tf_op jit(solution)/shard_map/pallas_call | solution.py:784
  28.8 1.6 %collective-permute-done.5.refs_11_.rest_11_ = f32[504,128]{1,0:T(8,128)S(1)} collective-permute-done((f32[504,128]{1,0:T(8,128)S(1)}, f32[504,128]{1,0:T(8,128)S(1)}, u32[]{:S(2)}, u32[]{:S(2)}) %collective-permute-start.5) | collective-permute-done | bytes 258080 | tf_op jit(solution)/shard_map/ppermute | solution.py:665
  30.4 0.6 %shard_map.162 = (f32[90,2,1440]{2,1,0:T(2,128)S(1)}, f32[90,2,1440]{2,1,0:T(2,128)S(1)}, f32[90,1440]{1,0:T(8,128)S(1)}, f32[45,2,360]{2,1,0:T(2,128)S(1)}) custom-call(f32[2]{0:T(128)S(1)} %copy-done.5, f32[184,1440]{1,0:T(8,128)S(1)} %get-tuple-element.49.refs_1_.rest_1_, f32[180,1440]{1,0:T(8,128)S(1)} %get-tuple-element.50.refs_2_.rest_2_, ...), custom_call_target="tpu_custom_call" | custom-call | flops 2300000000 | tf_op jit(solution)/shard_map/pallas_call | solution.py:799
  31.0 1.3 %collective-permute-start.7 = (f32[90,1440]{1,0:T(8,128)S(1)}, f32[90,1440]{1,0:T(8,128)S(1)}, u32[]{:S(2)}, u32[]{:S(2)}) collective-permute-start(f32[90,1440]{1,0:T(8,128)S(1)} %get-tuple-element.65), channel_id=1, source_target_pairs={{1,0},{3,2},{5,4},{7,6},{9,8},{11,10},{13,12},{15,14},{17,16},{19,... | collective-permute-start | bytes 1555208 | tf_op jit(solution)/shard_map/ppermute | solution.py:808
  32.3 0.0 collective-permute-done.6.arrived_ref
  32.3 0.0 copy-start.2
  32.3 2.8 %shard_map.163 = (f32[90,2,1440]{2,1,0:T(2,128)S(1)}, f32[90,2,1440]{2,1,0:T(2,128)S(1)}, f32[2,45,2,360]{3,2,1,0:T(2,128)S(1)}) custom-call(f32[45,2,360]{2,1,0:T(2,128)S(1)} %get-tuple-element.60.east_keep, f32[45,2,360]{2,1,0:T(2,128)S(1)} %get-tuple-element.61.north_keep, f32[2,45,2,360]{3,2,1,0:T(2,128)S(1)} %collective-permute-done.6.arrived_ref, ...), custom_call_target="tpu_custom_call" | custom-call | flops 3680000000 | tf_op jit(solution)/shard_map/pallas_call | solution.py:811
  35.1 0.0 collective-permute-done.7.rest_4_
  35.1 0.0 copy-done.2
  35.1 1.9 %shard_map.164 = (f32[90,2,1440]{2,1,0:T(2,128)}, f32[90,2,1440]{2,1,0:T(2,128)}, f32[90,2,1440]{2,1,0:T(2,128)}, f32[2,45,2,360]{3,2,1,0:T(2,128)}) custom-call(f32[90,1440]{1,0:T(8,128)S(1)} %copy-done.2, f32[90,2,1440]{2,1,0:T(2,128)S(1)} %get-tuple-element.58.rest_0_, f32[90,2,1440]{2,1,0:T(2,128)S(1)} %get-tuple-element.59.rest_1_, ...), custom_call_target="tpu_custom_call" | custom-call | flops 1150000000 | tf_op jit(solution)/shard_map/pallas_call | solution.py:819
  (1 shorter events, 0.0 us)
Async XLA Ops:
  3.7 15.1 %collective-permute-start.2 = (f32[456,128]{1,0:T(8,128)S(1)}, f32[456,128]{1,0:T(8,128)S(1)}, u32[]{:S(2)}, u32[]{:S(2)}) collective-permute-start(f32[456,128]{1,0:T(8,128)S(1)} %get-tuple-element.47.rest_0_), channel_id=1, source_target_pairs={{0,2},{2,0},{1,3},{3,1},{4,6},{6,4},{5,7},{7,5},{8,10},{10,8},{9,1... | collective-permute-start | bytes 700424 | tf_op jit(solution)/shard_map/ppermute | solution.py:665
  6.7 4.4 %collective-permute-start = (f32[8,1440]{1,0:T(8,128)S(1)}, f32[8,1440]{1,0:T(8,128)S(1)}, u32[]{:S(2)}, u32[]{:S(2)}) collective-permute-start(f32[8,1440]{1,0:T(8,128)S(1)} %get-tuple-element.43), channel_id=1, source_target_pairs={{0,4},{8,12},{4,0},{12,8},{1,5},{9,13},{5,1},{13,9},{2,6},{10,14},... | collective-permute-start | bytes 138248 | tf_op jit(solution)/shard_map/ppermute | solution.py:726
  8.2 2.9 %copy-start.3 = (s32[180]{0:T(256)S(1)}, s32[180]{0:T(256)}, u32[]{:S(2)}) copy-start(s32[180]{0:T(256)} %param.18) | copy-start | bytes 2164
  8.2 2.9 %copy-start.4 = (s32[180]{0:T(256)S(1)}, s32[180]{0:T(256)}, u32[]{:S(2)}) copy-start(s32[180]{0:T(256)} %param.19) | copy-start | bytes 2164
  9.8 9.7 %collective-permute-start.3 = (f32[592,128]{1,0:T(8,128)S(1)}, f32[592,128]{1,0:T(8,128)S(1)}, u32[]{:S(2)}, u32[]{:S(2)}) collective-permute-start(f32[592,128]{1,0:T(8,128)S(1)} %shard_map.158.rest_2_), channel_id=1, source_target_pairs={{0,2},{2,0},{1,3},{3,1},{4,6},{6,4},{5,7},{7,5},{8,10},{10,8},{9,1... | collective-permute-start | bytes 909320 | tf_op jit(solution)/shard_map/ppermute | solution.py:665
  10.4 0.7 %collective-permute-start.1 = (f32[8,1440]{1,0:T(8,128)S(1)}, f32[8,1440]{1,0:T(8,128)S(1)}, u32[]{:S(2)}, u32[]{:S(2)}) collective-permute-start(f32[8,1440]{1,0:T(8,128)S(1)} %get-tuple-element.44), channel_id=1, source_target_pairs={{4,8},{8,4},{5,9},{9,5},{6,10},{10,6},{7,11},{11,7},{20,24},{24,20... | collective-permute-start | bytes 138248 | tf_op jit(solution)/shard_map/ppermute | solution.py:726
  14.7 11.5 %collective-permute-start.4 = (f32[544,128]{1,0:T(8,128)S(1)}, f32[544,128]{1,0:T(8,128)S(1)}, u32[]{:S(2)}, u32[]{:S(2)}) collective-permute-start(f32[544,128]{1,0:T(8,128)S(1)} %get-tuple-element.53.rest_0_), channel_id=1, source_target_pairs={{0,2},{2,0},{12,14},{14,12},{1,3},{3,1},{13,15},{15,13},{16,18},{1... | collective-permute-start | bytes 835592 | tf_op jit(solution)/shard_map/ppermute | solution.py:757
  18.1 1.7 %copy-start = (bf16[2304,512]{1,0:T(8,128)(2,1)S(1)}, bf16[2304,512]{1,0:T(8,128)(2,1)}, u32[]{:S(2)}) copy-start(bf16[2304,512]{1,0:T(8,128)(2,1)} %constant.9.clone.rest_4_.basis_ref.refs_12_.rest_12_) | copy-start | bytes 7077892
  18.2 1.9 %copy-start.1 = (f32[2,90,1440]{2,0,1:T(2,128)S(1)}, f32[2,90,1440]{2,0,1:T(2,128)}, u32[]{:S(2)}) copy-start(f32[2,90,1440]{2,0,1:T(2,128)} %param.14) | copy-start | bytes 3110404
  18.2 1.9 %copy-start.5 = (f32[2]{0:T(128)S(1)}, f32[2]{0:T(128)}, u32[]{:S(2)}) copy-start(f32[2]{0:T(128)} %rest_0_.1) | copy-start | bytes 28
  18.2 12.2 %collective-permute-start.5 = (f32[504,128]{1,0:T(8,128)S(1)}, f32[504,128]{1,0:T(8,128)S(1)}, u32[]{:S(2)}, u32[]{:S(2)}) collective-permute-start(f32[504,128]{1,0:T(8,128)S(1)} %get-tuple-element.57.refs_10_.rest_10_), channel_id=1, source_target_pairs={{0,2},{2,0},{1,3},{3,1},{4,6},{6,4},{5,7},{7,5},{8,10},{10,8},{9,1... | collective-permute-start | bytes 774152 | tf_op jit(solution)/shard_map/ppermute | solution.py:665
  26.4 5.8 %collective-permute-start.6 = (f32[2,45,2,360]{3,2,1,0:T(2,128)S(1)}, f32[2,45,2,360]{3,2,1,0:T(2,128)S(1)}, u32[]{:S(2)}, u32[]{:S(2)}) collective-permute-start(f32[2,45,2,360]{3,2,1,0:T(2,128)S(1)} %get-tuple-element.62), channel_id=1, source_target_pairs={{0,8},{12,4},{1,9},{13,5},{2,10},{14,6},{3,11},{15,7},{16,24},{28,... | collective-permute-start | bytes 777608 | tf_op jit(solution)/shard_map/ppermute | solution.py:779
  31.0 4.1 %collective-permute-start.7 = (f32[90,1440]{1,0:T(8,128)S(1)}, f32[90,1440]{1,0:T(8,128)S(1)}, u32[]{:S(2)}, u32[]{:S(2)}) collective-permute-start(f32[90,1440]{1,0:T(8,128)S(1)} %get-tuple-element.65), channel_id=1, source_target_pairs={{1,0},{3,2},{5,4},{7,6},{9,8},{11,10},{13,12},{15,14},{17,16},{19,... | collective-permute-start | bytes 1555208 | tf_op jit(solution)/shard_map/ppermute | solution.py:808
  32.3 2.8 %copy-start.2 = (f32[90,1440]{1,0:T(8,128)S(1)}, f32[90,1440]{1,0:T(8,128)}, u32[]{:S(2)}) copy-start(f32[90,1440]{1,0:T(8,128)} %surface_ref.1) | copy-start | bytes 1555204

commit v10 on v8

--- a/solution.py
+++ b/solution.py
@@ -52,7 +52,7 @@
         self.helped = self.help * self.lev
         self.ahead = round_up(self.helped, 16)
         self.cuts = 2
-        self.first = min(round_up(self.own * 4 // 9, 8 * self.lev), self.own)
+        self.first = min(round_up(self.own // 2, 8 * self.lev), self.own)
 
 
 def high_low(x):

time: 37.7 us -> 38 us (level)
  waiting for transfers between devices: 4.4 us -> 5.35 us
  local copies, waits for them, and re-layouts: 0.64 us -> 0.04 us
    ppermute x3, waiting for transfers between devices: 2.26 us -> 2.94 us  [shifted(): lax.ppermute(block, axis, [(i, (i + distance) % count) for i in range(cou...]
    unnamed x12, local copies, waits for them, and re-layouts: 0.64 us -> 0.04 us
  transfers between devices with their start and end apart: 8 -> 8, of which waited for: 3 -> 4; matrix products, arithmetic and copies ran while one was open for 0% -> 0% of each run, Pallas kernels for 37% -> 37%
where the time goes in v10:
time: 38 us; the launch traced here: 37.5 us
  Pallas kernels  19 us (50%)
  starting transfers between devices  12.1 us (32%)
  waiting for transfers between devices  5.35 us (14%)
  between operations  0.94 us (2%)
    ppermute x3, starting transfers between devices, shifted(): lax.ppermute(block, axis, [(i, (i + distance) % count) for i in range(cou...  4.4 us
    pallas_call x1, Pallas kernels, local(): call(functools.partial(east_inverse, z), 11 + 2 * z.n_lon, [field, (z.own...  4.02 us
    pallas_call x1, Pallas kernels, local(): call(functools.partial(north_forward, z), 10, [(packed_rows(z.ahead), 128...  3.63 us
    pallas_call x1, Pallas kernels, local(): call(functools.partial(east_first, z), 6, [(packed_rows(z.first), 128), r...  3.39 us
    ppermute x1, starting transfers between devices, local(): north_aheads.append(lax.ppermute(north_ahead, ('lat', 'lon'), route))  3.18 us
    ppermute x3, waiting for transfers between devices, shifted(): lax.ppermute(block, axis, [(i, (i + distance) % count) for i in range(cou...  2.94 us
    pallas_call x1, Pallas kernels, local(): call(functools.partial(north_shallowest, z), 3 + len(operands), [in_vmem,...  2.8 us
    ppermute x1, waiting for transfers between devices, local(): north_aheads.append(lax.ppermute(north_ahead, ('lat', 'lon'), route))  2.17 us
  transfers between devices with their start and end apart: 8, of which 4 were waited for; matrix products, arithmetic and copies ran while one was open for 0% of the time, Pallas kernels for 37%

profile of v10, /device:TPU:0, one launch (start us, length us, event | category | flops | bytes accessed | tf_op | source)
XLA Modules:
  0.0 37.5 jit_solution(2029604483484459827)
XLA Ops:
  0.6 3.4 %shard_map.155 = (f32[544,128]{1,0:T(8,128)S(1)}, f32[8,1440]{1,0:T(8,128)S(1)}, f32[8,1440]{1,0:T(8,128)S(1)}, f32[90,2,1440]{2,1,0:T(2,128)S(1)}, f32[90,2,144...) custom-call(f32[90,2,1440]{2,1,0:T(2,128)} %bitcast.15, ...), custom_call_target="tpu_custom_call" | custom-call | flops 1150000000 | tf_op jit(solution)/shard_map/pallas_call | solution.py:685
  4.0 3.0 %collective-permute-start.2 = (f32[544,128]{1,0:T(8,128)S(1)}, f32[544,128]{1,0:T(8,128)S(1)}, u32[]{:S(2)}, u32[]{:S(2)}) collective-permute-start(f32[544,128]{1,0:T(8,128)S(1)} %get-tuple-element.47.rest_0_), channel_id=1, source_target_pairs={{0,2},{2,0},{1,3},{3,1},{4,6},{6,4},{5,7},{7,5},{8,10},{10,8},{9,1... | collective-permute-start | bytes 835592 | tf_op jit(solution)/shard_map/ppermute | solution.py:652
  7.0 1.1 %collective-permute-start = (f32[8,1440]{1,0:T(8,128)S(1)}, f32[8,1440]{1,0:T(8,128)S(1)}, u32[]{:S(2)}, u32[]{:S(2)}) collective-permute-start(f32[8,1440]{1,0:T(8,128)S(1)} %get-tuple-element.43), channel_id=1, source_target_pairs={{0,4},{8,12},{4,0},{12,8},{1,5},{9,13},{5,1},{13,9},{2,6},{10,14},... | collective-permute-start | bytes 138248 | tf_op jit(solution)/shard_map/ppermute | solution.py:713
  8.2 0.7 %collective-permute-start.1 = (f32[8,1440]{1,0:T(8,128)S(1)}, f32[8,1440]{1,0:T(8,128)S(1)}, u32[]{:S(2)}, u32[]{:S(2)}) collective-permute-start(f32[8,1440]{1,0:T(8,128)S(1)} %get-tuple-element.44), channel_id=1, source_target_pairs={{4,8},{8,4},{5,9},{9,5},{6,10},{10,6},{7,11},{11,7},{20,24},{24,20... | collective-permute-start | bytes 138248 | tf_op jit(solution)/shard_map/ppermute | solution.py:713
  8.8 0.0 copy-start.3
  8.8 0.0 copy-start.4
  8.9 1.5 %shard_map.158.rest_2_ = f32[504,128]{1,0:T(8,128)S(1)} custom-call(f32[90,2,1440]{2,1,0:T(2,128)S(1)} %get-tuple-element.38.we_ref, f32[90,2,1440]{2,1,0:T(2,128)S(1)} %get-tuple-element.39.wn_ref, f32[90,2,1440]{2,1,0:T(2,128)S(1)} %get-tuple-element.40.g_ref, f32[184,8]{1,0:T(8,128)S(1)} %get-tuple-element.41.row_ref.refs_3_.rest_3_, ...), custom_call_target="tpu_custom_call" | custom-call | flops 207000000 | tf_op jit(solution)/shard_map/pallas_call | solution.py:700
  10.3 0.6 %collective-permute-start.3 = (f32[504,128]{1,0:T(8,128)S(1)}, f32[504,128]{1,0:T(8,128)S(1)}, u32[]{:S(2)}, u32[]{:S(2)}) collective-permute-start(f32[504,128]{1,0:T(8,128)S(1)} %shard_map.158.rest_2_), channel_id=1, source_target_pairs={{0,2},{2,0},{1,3},{3,1},{4,6},{6,4},{5,7},{7,5},{8,10},{10,8},{9,1... | collective-permute-start | bytes 774152 | tf_op jit(solution)/shard_map/ppermute | solution.py:652
  10.9 0.2 collective-permute-done.even_ref
  11.1 0.0 collective-permute-done.1.odd_ref
  11.1 0.0 copy-done.3
  11.1 0.0 copy-done.4
  11.1 3.6 %shard_map.156 = (f32[544,128]{1,0:T(8,128)S(1)}, f32[504,128]{1,0:T(8,128)S(1)}, f32[184,1440]{1,0:T(8,128)S(1)}, f32[184,256]{1,0:T(8,128)S(1)}, f32[184,128]{1,0:T(8,128)S(1)}) custom-call(f32[90,2,1440]{2,1,0:T(2,128)S(1)} %get-tuple-element.38.we_ref, f32[90,2,1440]{2,1,0:T(2,128)S(1)} %get-tuple-element.39.wn_ref, ...), custom_call_target="tpu_custom_call" | custom-call | flops 920000000 | tf_op jit(solution)/shard_map/pallas_call | solution.py:716
  14.8 3.2 %collective-permute-start.4 = (f32[544,128]{1,0:T(8,128)S(1)}, f32[544,128]{1,0:T(8,128)S(1)}, u32[]{:S(2)}, u32[]{:S(2)}) collective-permute-start(f32[544,128]{1,0:T(8,128)S(1)} %get-tuple-element.53.rest_0_), channel_id=1, source_target_pairs={{0,2},{2,0},{12,14},{14,12},{1,3},{3,1},{13,15},{15,13},{16,18},{1... | collective-permute-start | bytes 835592 | tf_op jit(solution)/shard_map/ppermute | solution.py:744
  17.9 0.0 copy-start
  18.0 0.0 copy-start.1
  18.0 0.0 copy-start.5
  18.0 0.8 %collective-permute-start.5 = (f32[504,128]{1,0:T(8,128)S(1)}, f32[504,128]{1,0:T(8,128)S(1)}, u32[]{:S(2)}, u32[]{:S(2)}) collective-permute-start(f32[504,128]{1,0:T(8,128)S(1)} %get-tuple-element.57.refs_10_.rest_10_), channel_id=1, source_target_pairs={{0,2},{2,0},{1,3},{3,1},{4,6},{6,4},{5,7},{7,5},{8,10},{10,8},{9,1... | collective-permute-start | bytes 774152 | tf_op jit(solution)/shard_map/ppermute | solution.py:652
  18.8 0.0 collective-permute-done.2.arrived_ref.rest_1_
  18.8 1.2 %collective-permute-done.3.rest_3_ = f32[504,128]{1,0:T(8,128)S(1)} collective-permute-done((f32[504,128]{1,0:T(8,128)S(1)}, f32[504,128]{1,0:T(8,128)S(1)}, u32[]{:S(2)}, u32[]{:S(2)}) %collective-permute-start.3) | collective-permute-done | bytes 258080 | tf_op jit(solution)/shard_map/ppermute | solution.py:652
  20.0 0.0 copy-done
  20.0 0.0 copy-done.1
  20.1 0.0 copy-done.5
  20.1 4.0 %shard_map.159 = (f32[90,2,1440]{2,1,0:T(2,128)}, f32[180,1440]{1,0:T(8,128)S(1)}, f32[45,2,360]{2,1,0:T(2,128)S(1)}, f32[45,2,360]{2,1,0:T(2,128)S(1)}) custom-call(f32[2]{0:T(128)S(1)} %copy-done.5, f32[90,2,1440]{2,1,0:T(2,128)S(1)} %get-tuple-element.38.we_ref, f32[90,2,1440]{2,1,0:T(2,128)S(1)} %get-tuple-element.39.wn_ref, ...), custom_call_target="tpu_custom_call" | custom-call | flops 1150000000 | tf_op jit(solution)/shard_map/pallas_call | solution.py:747
  24.1 2.2 %collective-permute-done.4.rest_1_ = f32[544,128]{1,0:T(8,128)S(1)} collective-permute-done((f32[544,128]{1,0:T(8,128)S(1)}, f32[544,128]{1,0:T(8,128)S(1)}, u32[]{:S(2)}, u32[]{:S(2)}) %collective-permute-start.4) | collective-permute-done | bytes 278560 | tf_op jit(solution)/shard_map/ppermute | solution.py:744
  26.3 0.2 shard_map.160
  26.5 1.5 %collective-permute-start.6 = (f32[2,45,2,360]{3,2,1,0:T(2,128)S(1)}, f32[2,45,2,360]{3,2,1,0:T(2,128)S(1)}, u32[]{:S(2)}, u32[]{:S(2)}) collective-permute-start(f32[2,45,2,360]{3,2,1,0:T(2,128)S(1)} %get-tuple-element.62), channel_id=1, source_target_pairs={{0,8},{12,4},{1,9},{13,5},{2,10},{14,6},{3,11},{15,7},{16,24},{28,... | collective-permute-start | bytes 777608 | tf_op jit(solution)/shard_map/ppermute | solution.py:766
  27.9 1.1 %shard_map.161 = (bf16[96,1536]{1,0:T(8,128)(2,1)S(1)}, bf16[96,1536]{1,0:T(8,128)(2,1)S(1)}) custom-call(f32[16,384]{1,0:T(8,128)S(1)} %get-tuple-element.42.phase_ref.refs_4_.rest_4_, f32[96,768]{1,0:T(8,128)S(1)} %get-tuple-element.54.waves_ref.refs_7_.rest_7_, bf16[2304,512]{1,0:T(8,128)(2,1)S(1)} %copy-done), custom_call_target="tpu_custom_call" | custom-call | flops 575000000 | tf_op jit(solution)/shard_map/pallas_call | solution.py:771
  29.0 1.7 %collective-permute-done.5.refs_11_.rest_11_ = f32[504,128]{1,0:T(8,128)S(1)} collective-permute-done((f32[504,128]{1,0:T(8,128)S(1)}, f32[504,128]{1,0:T(8,128)S(1)}, u32[]{:S(2)}, u32[]{:S(2)}) %collective-permute-start.5) | collective-permute-done | bytes 258080 | tf_op jit(solution)/shard_map/ppermute | solution.py:652
  30.7 0.6 %shard_map.162 = (f32[90,2,1440]{2,1,0:T(2,128)S(1)}, f32[90,2,1440]{2,1,0:T(2,128)S(1)}, f32[90,1440]{1,0:T(8,128)S(1)}, f32[45,2,360]{2,1,0:T(2,128)S(1)}) custom-call(f32[2]{0:T(128)S(1)} %copy-done.5, f32[184,1440]{1,0:T(8,128)S(1)} %get-tuple-element.49.refs_1_.rest_1_, f32[180,1440]{1,0:T(8,128)S(1)} %get-tuple-element.50.refs_2_.rest_2_, ...), custom_call_target="tpu_custom_call" | custom-call | flops 2300000000 | tf_op jit(solution)/shard_map/pallas_call | solution.py:786
  31.3 1.3 %collective-permute-start.7 = (f32[90,1440]{1,0:T(8,128)S(1)}, f32[90,1440]{1,0:T(8,128)S(1)}, u32[]{:S(2)}, u32[]{:S(2)}) collective-permute-start(f32[90,1440]{1,0:T(8,128)S(1)} %get-tuple-element.65), channel_id=1, source_target_pairs={{1,0},{3,2},{5,4},{7,6},{9,8},{11,10},{13,12},{15,14},{17,16},{19,... | collective-permute-start | bytes 1555208 | tf_op jit(solution)/shard_map/ppermute | solution.py:795
  32.6 0.0 collective-permute-done.6.arrived_ref
  32.6 0.0 copy-start.2
  32.6 2.8 %shard_map.163 = (f32[90,2,1440]{2,1,0:T(2,128)S(1)}, f32[90,2,1440]{2,1,0:T(2,128)S(1)}, f32[2,45,2,360]{3,2,1,0:T(2,128)S(1)}) custom-call(f32[45,2,360]{2,1,0:T(2,128)S(1)} %get-tuple-element.60.east_keep, f32[45,2,360]{2,1,0:T(2,128)S(1)} %get-tuple-element.61.north_keep, f32[2,45,2,360]{3,2,1,0:T(2,128)S(1)} %collective-permute-done.6.arrived_ref, ...), custom_call_target="tpu_custom_call" | custom-call | flops 3680000000 | tf_op jit(solution)/shard_map/pallas_call | solution.py:798
  35.4 0.0 collective-permute-done.7.rest_4_
  35.4 0.0 copy-done.2
  35.4 1.9 %shard_map.164 = (f32[90,2,1440]{2,1,0:T(2,128)}, f32[90,2,1440]{2,1,0:T(2,128)}, f32[90,2,1440]{2,1,0:T(2,128)}, f32[2,45,2,360]{3,2,1,0:T(2,128)}) custom-call(f32[90,1440]{1,0:T(8,128)S(1)} %copy-done.2, f32[90,2,1440]{2,1,0:T(2,128)S(1)} %get-tuple-element.58.rest_0_, f32[90,2,1440]{2,1,0:T(2,128)S(1)} %get-tuple-element.59.rest_1_, ...), custom_call_target="tpu_custom_call" | custom-call | flops 1150000000 | tf_op jit(solution)/shard_map/pallas_call | solution.py:806
  (1 shorter events, 0.0 us)
Async XLA Ops:
  4.0 14.8 %collective-permute-start.2 = (f32[544,128]{1,0:T(8,128)S(1)}, f32[544,128]{1,0:T(8,128)S(1)}, u32[]{:S(2)}, u32[]{:S(2)}) collective-permute-start(f32[544,128]{1,0:T(8,128)S(1)} %get-tuple-element.47.rest_0_), channel_id=1, source_target_pairs={{0,2},{2,0},{1,3},{3,1},{4,6},{6,4},{5,7},{7,5},{8,10},{10,8},{9,1... | collective-permute-start | bytes 835592 | tf_op jit(solution)/shard_map/ppermute | solution.py:652
  7.0 4.1 %collective-permute-start = (f32[8,1440]{1,0:T(8,128)S(1)}, f32[8,1440]{1,0:T(8,128)S(1)}, u32[]{:S(2)}, u32[]{:S(2)}) collective-permute-start(f32[8,1440]{1,0:T(8,128)S(1)} %get-tuple-element.43), channel_id=1, source_target_pairs={{0,4},{8,12},{4,0},{12,8},{1,5},{9,13},{5,1},{13,9},{2,6},{10,14},... | collective-permute-start | bytes 138248 | tf_op jit(solution)/shard_map/ppermute | solution.py:713
  8.2 2.9 %collective-permute-start.1 = (f32[8,1440]{1,0:T(8,128)S(1)}, f32[8,1440]{1,0:T(8,128)S(1)}, u32[]{:S(2)}, u32[]{:S(2)}) collective-permute-start(f32[8,1440]{1,0:T(8,128)S(1)} %get-tuple-element.44), channel_id=1, source_target_pairs={{4,8},{8,4},{5,9},{9,5},{6,10},{10,6},{7,11},{11,7},{20,24},{24,20... | collective-permute-start | bytes 138248 | tf_op jit(solution)/shard_map/ppermute | solution.py:713
  8.8 2.3 %copy-start.3 = (s32[180]{0:T(256)S(1)}, s32[180]{0:T(256)}, u32[]{:S(2)}) copy-start(s32[180]{0:T(256)} %param.18) | copy-start | bytes 2164
  8.8 2.3 %copy-start.4 = (s32[180]{0:T(256)S(1)}, s32[180]{0:T(256)}, u32[]{:S(2)}) copy-start(s32[180]{0:T(256)} %param.19) | copy-start | bytes 2164
  10.3 9.7 %collective-permute-start.3 = (f32[504,128]{1,0:T(8,128)S(1)}, f32[504,128]{1,0:T(8,128)S(1)}, u32[]{:S(2)}, u32[]{:S(2)}) collective-permute-start(f32[504,128]{1,0:T(8,128)S(1)} %shard_map.158.rest_2_), channel_id=1, source_target_pairs={{0,2},{2,0},{1,3},{3,1},{4,6},{6,4},{5,7},{7,5},{8,10},{10,8},{9,1... | collective-permute-start | bytes 774152 | tf_op jit(solution)/shard_map/ppermute | solution.py:652
  14.8 11.5 %collective-permute-start.4 = (f32[544,128]{1,0:T(8,128)S(1)}, f32[544,128]{1,0:T(8,128)S(1)}, u32[]{:S(2)}, u32[]{:S(2)}) collective-permute-start(f32[544,128]{1,0:T(8,128)S(1)} %get-tuple-element.53.rest_0_), channel_id=1, source_target_pairs={{0,2},{2,0},{12,14},{14,12},{1,3},{3,1},{13,15},{15,13},{16,18},{1... | collective-permute-start | bytes 835592 | tf_op jit(solution)/shard_map/ppermute | solution.py:744
  17.9 2.1 %copy-start = (bf16[2304,512]{1,0:T(8,128)(2,1)S(1)}, bf16[2304,512]{1,0:T(8,128)(2,1)}, u32[]{:S(2)}) copy-start(bf16[2304,512]{1,0:T(8,128)(2,1)} %constant.9.clone.rest_4_.basis_ref.refs_12_.rest_12_) | copy-start | bytes 7077892
  18.0 2.1 %copy-start.1 = (f32[2,90,1440]{2,0,1:T(2,128)S(1)}, f32[2,90,1440]{2,0,1:T(2,128)}, u32[]{:S(2)}) copy-start(f32[2,90,1440]{2,0,1:T(2,128)} %param.14) | copy-start | bytes 3110404
  18.0 2.1 %copy-start.5 = (f32[2]{0:T(128)S(1)}, f32[2]{0:T(128)}, u32[]{:S(2)}) copy-start(f32[2]{0:T(128)} %rest_0_.1) | copy-start | bytes 28
  18.0 12.7 %collective-permute-start.5 = (f32[504,128]{1,0:T(8,128)S(1)}, f32[504,128]{1,0:T(8,128)S(1)}, u32[]{:S(2)}, u32[]{:S(2)}) collective-permute-start(f32[504,128]{1,0:T(8,128)S(1)} %get-tuple-element.57.refs_10_.rest_10_), channel_id=1, source_target_pairs={{0,2},{2,0},{1,3},{3,1},{4,6},{6,4},{5,7},{7,5},{8,10},{10,8},{9,1... | collective-permute-start | bytes 774152 | tf_op jit(solution)/shard_map/ppermute | solution.py:652
  26.5 6.1 %collective-permute-start.6 = (f32[2,45,2,360]{3,2,1,0:T(2,128)S(1)}, f32[2,45,2,360]{3,2,1,0:T(2,128)S(1)}, u32[]{:S(2)}, u32[]{:S(2)}) collective-permute-start(f32[2,45,2,360]{3,2,1,0:T(2,128)S(1)} %get-tuple-element.62), channel_id=1, source_target_pairs={{0,8},{12,4},{1,9},{13,5},{2,10},{14,6},{3,11},{15,7},{16,24},{28,... | collective-permute-start | bytes 777608 | tf_op jit(solution)/shard_map/ppermute | solution.py:766
  31.3 4.1 %collective-permute-start.7 = (f32[90,1440]{1,0:T(8,128)S(1)}, f32[90,1440]{1,0:T(8,128)S(1)}, u32[]{:S(2)}, u32[]{:S(2)}) collective-permute-start(f32[90,1440]{1,0:T(8,128)S(1)} %get-tuple-element.65), channel_id=1, source_target_pairs={{1,0},{3,2},{5,4},{7,6},{9,8},{11,10},{13,12},{15,14},{17,16},{19,... | collective-permute-start | bytes 1555208 | tf_op jit(solution)/shard_map/ppermute | solution.py:795
  32.6 2.8 %copy-start.2 = (f32[90,1440]{1,0:T(8,128)S(1)}, f32[90,1440]{1,0:T(8,128)}, u32[]{:S(2)}) copy-start(f32[90,1440]{1,0:T(8,128)} %surface_ref.1) | copy-start | bytes 1555204
